TPU v7x, 128 devices: a whole 4x4x4 slice. The times are simulated.
128 devices in a mesh: dp: 32 (over x, z, core), row: 2 (over y_lo), col: 2 (over y_hi).
Axes of the slice: x: 4, y: 4 (y_hi: 2, y_lo: 2; y = y_hi * 2 + y_lo), z: 4, core: 2. Of those that a mesh axis runs over, the one named last changes fastest.
Arguments:
- tokens: bfloat16 [16384, 1536], P(('dp', 'row'), 'col'), may hold values from -6 to 6
- cotangent: bfloat16 [16384, 1536], P(('dp', 'row'), 'col'), may hold values from -6 to 6
- norm_gains: bfloat16 [2, 2, 1536], P(None, None, 'col'), may hold values from 0.5 to 1.5
- query_weight: bfloat16 [2, 1536, 1536], P(None, 'col', 'row'), may hold values from -0.15625 to 0.15625
- key_weight: bfloat16 [2, 1536, 256], P(None, 'col', 'row'), may hold values from -0.15625 to 0.15625
- value_weight: bfloat16 [2, 1536, 256], P(None, 'col', 'row'), may hold values from -0.15625 to 0.15625
- output_weight: bfloat16 [2, 1536, 1536], P(None, 'row', 'col'), may hold values from -1.75 to 1.75
- router_weight: bfloat16 [2, 1536, 8], P(None, 'col'), may hold values from -0.078125 to 0.078125
- gate_weight: bfloat16 [2, 8, 1536, 768], P(None, None, 'col', 'row'), may hold values from -0.15625 to 0.15625
- up_weight: bfloat16 [2, 8, 1536, 768], P(None, None, 'col', 'row'), may hold values from -0.15625 to 0.15625
- down_weight: bfloat16 [2, 8, 768, 1536], P(None, None, 'row', 'col'), may hold values from -0.875 to 0.875
- expert_ids: int32 [2, 16384, 4], P(None, 'dp'), may hold values from 0 to 7, all different within a row; in each aligned block of 512 rows (0 to 511, 512 to 1023, ..., all dimensions but the last counted through in order) at most 288 rows name the same one
- seq_lengths: int32 [128], replicated, may hold values from 1 to 509, as said below
- seq_owner: int32 [128], replicated, may hold values from 0 to 31, as said below
Outputs:
- block_output: bfloat16 [16384, 1536], P(('dp', 'row'), 'col')
- grad_tokens: bfloat16 [16384, 1536], P(('dp', 'row'), 'col')
- grad_gains: float32 [2, 2, 1536], P(None, None, 'col')
- grad_query: float32 [2, 1536, 1536], P(None, ('col', 'dp'), 'row')
- grad_key: float32 [2, 1536, 256], P(None, ('col', 'dp'), 'row')
- grad_value: float32 [2, 1536, 256], P(None, ('col', 'dp'), 'row')
- grad_output: float32 [2, 1536, 1536], P(None, ('row', 'dp'), 'col')
- grad_router: float32 [2, 1536, 8], P(None, 'col')
- grad_gate: float32 [2, 8, 1536, 768], P(None, None, ('col', 'dp'), 'row')
- grad_up: float32 [2, 8, 1536, 768], P(None, None, ('col', 'dp'), 'row')
- grad_down: float32 [2, 8, 768, 1536], P(None, None, ('row', 'dp'), 'col')
Inputs may be any that keep to these rules, and one draw needn't show every extreme that they name: `seq_owner`: each data index holds exactly 4 sequences. `seq_lengths`: the sequences of one data index take at most 512 rows together, and one of them is longer than 256. `expert_ids`: the 4 experts of a token differ; within one layer and the 512 rows of one data index no expert is named more than 288 times.
All inputs are finite; a program needn't handle non-finite values.
Results may differ from a plain program's by a relative error of at most 0.022.
Values may be sent and summed in bfloat16 or wider, within the bound.
No kernel may reach another device: no remote copies, remote signals or barrier semaphores. Data moves between devices by JAX's collectives and lax.ppermute only.
A program may use at most 256 MiB of HBM per device.

v0:
```python
import jax
import jax.numpy as jnp
from jax import lax
from jax.sharding import PartitionSpec as P

D = 1536
HEAD = 128
TOP = 4
EXPERTS = 8
LAYERS = 2
TOK_DP = 512
CAP = 288


EPSILON = 1e-06
ROPE_THETA = 1000000.0
MASKED_SCORE = -1e30
HIGHEST_PRECISION = lax.Precision.HIGHEST
ACROSS = (((1,), (1,)), ((), ()))
DOWNWARD = (((0,), (0,)), ((), ()))


def segments(seq_lengths, seq_owner, data_index, places_count):
    owned_len = jnp.where(seq_owner == data_index, seq_lengths, 0)
    seq_ends = jnp.cumsum(owned_len)
    places = jnp.arange(places_count, dtype=jnp.int32)
    finished = (seq_ends[None, :] <= places[:, None]).astype(jnp.int32)
    segment = jnp.sum(finished, axis=1)
    starts = jnp.sum(finished * owned_len[None, :], axis=1)
    valid_row = places < jnp.sum(owned_len)
    position = jnp.where(valid_row, places - starts, 0)
    return (segment, position, valid_row)


def rotate(values, position, direction):
    half_dim = values.shape[-1] // 2
    exponent = jnp.arange(half_dim, dtype=jnp.float32) * (-2.0 / values.shape[-1])
    frequency = jnp.power(ROPE_THETA, exponent)
    angle_grid = position.astype(jnp.float32)[:, None] * frequency[None, :]
    cosine = jnp.cos(angle_grid)
    sine_part = jnp.sin(angle_grid) * direction
    former = values[..., :half_dim]
    latter = values[..., half_dim:]
    return jnp.concatenate(
        [former * cosine - latter * sine_part, latter * cosine + former * sine_part], axis=-1
    )


def route_slots(expert_ids):
    flat_ids = expert_ids.reshape(-1)
    pair_count = flat_ids.shape[0]
    one_hot = (flat_ids[:, None] == jnp.arange(EXPERTS, dtype=jnp.int32)[None, :]).astype(jnp.int32)
    earlier = jnp.cumsum(one_hot, axis=0) - one_hot
    slot_index = jnp.sum(earlier * one_hot, axis=1)
    pair_slot = flat_ids * CAP + slot_index
    slot_pair = (
        jnp.full((EXPERTS * CAP,), pair_count, jnp.int32)
        .at[pair_slot]
        .set(jnp.arange(pair_count, dtype=jnp.int32))
    )
    return (pair_slot, slot_pair)


def feature_total(partial_value):
    return lax.psum(partial_value, "col")


def rows_whole(shard_piece):
    return lax.all_gather(shard_piece, "row", axis=0, tiled=True)


def rows_share(partial_value):
    return lax.psum_scatter(partial_value, "row", scatter_dimension=0, tiled=True)


def cols_share(partial_value):
    return lax.psum_scatter(partial_value, "col", scatter_dimension=0, tiled=True)


def cols_whole(shard_piece):
    return lax.all_gather(shard_piece, "col", axis=0, tiled=True)


def pair_total(former, latter):
    return lax.psum((former, latter), "col")


def normalize(stream, gain):
    inv_rms = lax.rsqrt(feature_total(jnp.sum(stream * stream, axis=1)) / D + EPSILON)
    normed = (stream * inv_rms[:, None] * gain.astype(jnp.float32)).astype(jnp.bfloat16)
    return (inv_rms, normed)


def norm_back(upstream, grad_normed, stream, inv_rms, gain):
    scaled = gain.astype(jnp.float32) * grad_normed
    dot_sums = feature_total(jnp.sum(scaled * stream, axis=1))
    grad_stream = (
        upstream
        + inv_rms[:, None] * scaled
        - stream * (inv_rms * inv_rms * inv_rms * dot_sums / D)[:, None]
    )
    grad_gain = jnp.sum(grad_normed * stream * inv_rms[:, None], axis=0)
    return (grad_stream, grad_gain)


def visible(segment, valid_row, query_start, query_rows, group_size):
    rows_all = segment.shape[0]
    query_segment = lax.dynamic_slice_in_dim(segment, query_start, query_rows)
    query_valid = lax.dynamic_slice_in_dim(valid_row, query_start, query_rows)
    query_place = query_start + jnp.arange(query_rows, dtype=jnp.int32)
    key_place = jnp.arange(rows_all, dtype=jnp.int32)
    seen_mask = (
        (query_segment[:, None] == segment[None, :])
        & (key_place[None, :] <= query_place[:, None])
        & query_valid[:, None]
    )
    return (
        jnp.tile(seen_mask, (group_size, 1))[None],
        jnp.tile(query_valid, group_size)[None, :, None],
    )


def attention_scores(query_rot, key_rot):
    return jnp.einsum(
        "gqd,gkd->gqk", query_rot, key_rot, preferred_element_type=jnp.float32
    ) * HEAD ** (-0.5)


def attention_forward(
    stream,
    gain,
    query_weight,
    key_weight,
    value_weight,
    output_weight,
    segment,
    position,
    valid_row,
    column,
):
    inv_rms, normed = normalize(stream, gain)
    inputs = rows_whole(normed)
    rows_all = inputs.shape[0]
    query_sum = cols_share(jnp.dot(inputs, query_weight, preferred_element_type=jnp.float32))
    key_sum, value_sum = pair_total(
        jnp.dot(inputs, key_weight, preferred_element_type=jnp.float32),
        jnp.dot(inputs, value_weight, preferred_element_type=jnp.float32),
    )
    query_rows = query_sum.shape[0]
    query_start = column * query_rows
    local_heads = query_sum.shape[1] // HEAD
    local_groups = key_sum.shape[1] // HEAD
    group_size = local_heads // local_groups
    query_pos = lax.dynamic_slice_in_dim(position, query_start, query_rows)
    query_rot = rotate(
        query_sum.reshape(query_rows, local_heads, HEAD).transpose(1, 0, 2), query_pos, 1.0
    )
    query_rot = query_rot.astype(jnp.bfloat16).reshape(local_groups, group_size * query_rows, HEAD)
    key_rot = rotate(
        key_sum.reshape(rows_all, local_groups, HEAD).transpose(1, 0, 2), position, 1.0
    ).astype(jnp.bfloat16)
    value_low = (
        value_sum.reshape(rows_all, local_groups, HEAD).transpose(1, 0, 2).astype(jnp.bfloat16)
    )
    seen_mask, row_valid = visible(segment, valid_row, query_start, query_rows, group_size)
    scores = attention_scores(query_rot, key_rot)
    row_max = jnp.max(jnp.where(seen_mask, scores, MASKED_SCORE), axis=-1, keepdims=True)
    row_max = jnp.where(row_valid, row_max, 0.0)
    exponent = jnp.where(seen_mask, jnp.exp(scores - row_max), 0.0)
    denominator = jnp.sum(exponent, axis=-1, keepdims=True) + jnp.where(row_valid, 0.0, 1.0)
    log_total = row_max + jnp.log(denominator)
    probabilities = (exponent / denominator).astype(jnp.bfloat16)
    attended = jnp.einsum(
        "gqk,gkd->gqd", probabilities, value_low, preferred_element_type=jnp.float32
    )
    attended = (
        attended.reshape(local_heads, query_rows, HEAD)
        .transpose(1, 0, 2)
        .reshape(query_rows, local_heads * HEAD)
        .astype(jnp.bfloat16)
    )
    gathered = cols_whole(attended)
    branch = rows_share(jnp.dot(gathered, output_weight, preferred_element_type=jnp.float32))
    return (
        (stream, inv_rms, inputs, query_rot, key_rot, value_low, log_total, gathered),
        stream + branch,
    )


def attention_backward(
    upstream,
    cache,
    gain,
    query_weight,
    key_weight,
    value_weight,
    output_weight,
    segment,
    position,
    valid_row,
    column,
):
    stream, inv_rms, inputs, query_rot, key_rot, value_low, log_total, gathered = cache
    rows_all = inputs.shape[0]
    local_groups = key_rot.shape[0]
    local_heads = gathered.shape[1] // HEAD
    group_size = local_heads // local_groups
    query_rows = query_rot.shape[1] // group_size
    query_start = column * query_rows
    query_pos = lax.dynamic_slice_in_dim(position, query_start, query_rows)
    out_grad = rows_whole(upstream.astype(jnp.bfloat16))
    grad_output_w = lax.dot_general(
        gathered, out_grad, DOWNWARD, preferred_element_type=jnp.float32
    )
    attended_grad = cols_share(
        lax.dot_general(out_grad, output_weight, ACROSS, preferred_element_type=jnp.float32)
    )
    attended_grad = (
        attended_grad.astype(jnp.bfloat16)
        .reshape(query_rows, local_heads, HEAD)
        .transpose(1, 0, 2)
        .reshape(local_groups, group_size * query_rows, HEAD)
    )
    seen_mask, row_valid = visible(segment, valid_row, query_start, query_rows, group_size)
    scores = attention_scores(query_rot, key_rot)
    probabilities = jnp.where(seen_mask, jnp.exp(scores - log_total), 0.0)
    prob_grad = jnp.einsum(
        "gqd,gkd->gqk", attended_grad, value_low, preferred_element_type=jnp.float32
    )
    value_grad = jnp.einsum(
        "gqk,gqd->gkd",
        probabilities.astype(jnp.bfloat16),
        attended_grad,
        preferred_element_type=jnp.float32,
    )
    row_delta = jnp.sum(prob_grad * probabilities, axis=-1, keepdims=True)
    score_grad = (probabilities * (prob_grad - row_delta)).astype(jnp.bfloat16)
    query_grad = jnp.einsum(
        "gqk,gkd->gqd", score_grad, key_rot, preferred_element_type=jnp.float32
    ) * HEAD ** (-0.5)
    key_grad = jnp.einsum(
        "gqk,gqd->gkd", score_grad, query_rot, preferred_element_type=jnp.float32
    ) * HEAD ** (-0.5)
    key_grad, value_grad = pair_total(key_grad, value_grad)
    key_grad = (
        rotate(key_grad, position, -1.0)
        .transpose(1, 0, 2)
        .reshape(rows_all, local_groups * HEAD)
        .astype(jnp.bfloat16)
    )
    value_grad = (
        value_grad.transpose(1, 0, 2).reshape(rows_all, local_groups * HEAD).astype(jnp.bfloat16)
    )
    query_grad = rotate(query_grad.reshape(local_heads, query_rows, HEAD), query_pos, -1.0)
    query_grad = cols_whole(
        query_grad.transpose(1, 0, 2).reshape(query_rows, local_heads * HEAD).astype(jnp.bfloat16)
    )
    input_grad = lax.dot_general(
        query_grad, query_weight, ACROSS, preferred_element_type=jnp.float32
    )
    input_grad = input_grad + lax.dot_general(
        key_grad, key_weight, ACROSS, preferred_element_type=jnp.float32
    )
    input_grad = input_grad + lax.dot_general(
        value_grad, value_weight, ACROSS, preferred_element_type=jnp.float32
    )
    normed_grad = rows_share(input_grad)
    grad_query_w = lax.dot_general(inputs, query_grad, DOWNWARD, preferred_element_type=jnp.float32)
    grad_key_w = lax.dot_general(inputs, key_grad, DOWNWARD, preferred_element_type=jnp.float32)
    grad_value_w = lax.dot_general(inputs, value_grad, DOWNWARD, preferred_element_type=jnp.float32)
    grad_stream, grad_gain = norm_back(upstream, normed_grad, stream, inv_rms, gain)
    return (grad_stream, (grad_query_w, grad_key_w, grad_value_w, grad_output_w), grad_gain)


def expert_forward(stream, gain, router_weight, gate_weight, up_weight, down_weight, layer_ids):
    inv_rms, normed = normalize(stream, gain)
    inputs = rows_whole(normed)
    rows_all = inputs.shape[0]
    pair_slot, slot_pair = route_slots(layer_ids)
    slot_token = slot_pair // TOP
    expert_rows = jnp.take(inputs, slot_token, axis=0, mode="fill", fill_value=0).reshape(
        EXPERTS, CAP, inputs.shape[1]
    )
    gate_value, up_value, logits = lax.psum(
        (
            jnp.einsum(
                "esd,edf->esf", expert_rows, gate_weight, preferred_element_type=jnp.float32
            ),
            jnp.einsum("esd,edf->esf", expert_rows, up_weight, preferred_element_type=jnp.float32),
            jnp.dot(inputs, router_weight, preferred_element_type=jnp.float32),
        ),
        "col",
    )
    one_hot = layer_ids[:, :, None] == jnp.arange(EXPERTS, dtype=jnp.int32)[None, None, :]
    chosen = jnp.sum(jnp.where(one_hot, logits[:, None, :], 0.0), axis=-1)
    gate_share = jax.nn.softmax(chosen, axis=-1)
    slot_weight = jnp.take(gate_share.reshape(-1), slot_pair, mode="fill", fill_value=0.0).reshape(
        EXPERTS, CAP, 1
    )
    hidden = (slot_weight * jax.nn.silu(gate_value) * up_value).astype(jnp.bfloat16)
    result = jnp.einsum(
        "esf,efd->esd", hidden, down_weight, preferred_element_type=jnp.float32
    ).reshape(EXPERTS * CAP, -1)
    combined = jnp.take(result, pair_slot, axis=0).reshape(rows_all, TOP, -1).sum(axis=1)
    branch = rows_share(combined)
    cache = (
        stream,
        inv_rms,
        inputs,
        expert_rows,
        gate_value,
        up_value,
        slot_weight,
        gate_share,
        one_hot,
        pair_slot,
        slot_token,
        hidden,
    )
    return (cache, stream + branch)


def expert_backward(upstream, cache, gain, router_weight, gate_weight, up_weight, down_weight):
    (
        stream,
        inv_rms,
        inputs,
        expert_rows,
        gate_value,
        up_value,
        slot_weight,
        gate_share,
        one_hot,
        pair_slot,
        slot_token,
        hidden,
    ) = cache
    rows_all = inputs.shape[0]
    out_grad = rows_whole(upstream.astype(jnp.bfloat16))
    slot_grad = jnp.take(out_grad, slot_token, axis=0, mode="fill", fill_value=0).reshape(
        EXPERTS, CAP, -1
    )
    grad_down_w = jnp.einsum("esf,esd->efd", hidden, slot_grad, preferred_element_type=jnp.float32)
    hidden_grad = feature_total(
        jnp.einsum("esd,efd->esf", slot_grad, down_weight, preferred_element_type=jnp.float32)
    )
    sigmoid_gate = jax.nn.sigmoid(gate_value)
    silu_gate = gate_value * sigmoid_gate
    weight_grad_slots = jnp.sum(hidden_grad * silu_gate * up_value, axis=-1).reshape(-1)
    activation_grad = hidden_grad * slot_weight
    gate_grad = (
        activation_grad * up_value * sigmoid_gate * (1.0 + gate_value * (1.0 - sigmoid_gate))
    ).astype(jnp.bfloat16)
    up_grad = (activation_grad * silu_gate).astype(jnp.bfloat16)
    grad_gate_w = jnp.einsum(
        "esd,esf->edf", expert_rows, gate_grad, preferred_element_type=jnp.float32
    )
    grad_up_w = jnp.einsum("esd,esf->edf", expert_rows, up_grad, preferred_element_type=jnp.float32)
    rows_grad = jnp.einsum(
        "esf,edf->esd", gate_grad, gate_weight, preferred_element_type=jnp.float32
    )
    rows_grad = rows_grad + jnp.einsum(
        "esf,edf->esd", up_grad, up_weight, preferred_element_type=jnp.float32
    )
    share_grad = jnp.take(weight_grad_slots, pair_slot, axis=0).reshape(rows_all, TOP)
    chosen_grad = gate_share * (
        share_grad - jnp.sum(gate_share * share_grad, axis=-1, keepdims=True)
    )
    logits_grad = jnp.sum(jnp.where(one_hot, chosen_grad[:, :, None], 0.0), axis=1)
    router_float = router_weight.astype(jnp.float32)
    input_grad = (
        jnp.take(rows_grad.reshape(EXPERTS * CAP, -1), pair_slot, axis=0)
        .reshape(rows_all, TOP, -1)
        .sum(axis=1)
    )
    input_grad = input_grad + lax.dot_general(
        logits_grad, router_float, ACROSS, precision=HIGHEST_PRECISION
    )
    grad_router_part = lax.dot_general(
        inputs.astype(jnp.float32), logits_grad, DOWNWARD, precision=HIGHEST_PRECISION
    )
    normed_grad = rows_share(input_grad)
    grad_stream, grad_gain = norm_back(upstream, normed_grad, stream, inv_rms, gain)
    return (grad_stream, (grad_gate_w, grad_up_w, grad_down_w), grad_gain, grad_router_part)


def shards(
    tokens,
    cotangent,
    norm_gains,
    query_weight,
    key_weight,
    value_weight,
    output_weight,
    router_weight,
    gate_weight,
    up_weight,
    down_weight,
    expert_ids,
    seq_lengths,
    seq_owner,
):
    data_index = lax.axis_index("dp")
    column = lax.axis_index("col")
    segment, position, valid_row = segments(seq_lengths, seq_owner, data_index, TOK_DP)
    stream = tokens.astype(jnp.float32)
    caches = []
    for layer_index in range(LAYERS):
        attention_cache, stream = attention_forward(
            stream,
            norm_gains[layer_index, 0],
            query_weight[layer_index],
            key_weight[layer_index],
            value_weight[layer_index],
            output_weight[layer_index],
            segment,
            position,
            valid_row,
            column,
        )
        expert_cache, stream = expert_forward(
            stream,
            norm_gains[layer_index, 1],
            router_weight[layer_index],
            gate_weight[layer_index],
            up_weight[layer_index],
            down_weight[layer_index],
            expert_ids[layer_index],
        )
        caches.append((attention_cache, expert_cache))
    block_output = stream.astype(jnp.bfloat16)
    upstream = cotangent.astype(jnp.float32)
    collected = [None] * LAYERS
    gain_grads = [None] * LAYERS
    router_grads = [None] * LAYERS
    for layer_index in reversed(range(LAYERS)):
        attention_cache, expert_cache = caches[layer_index]
        upstream, expert_grads, expert_gain, router_part = expert_backward(
            upstream,
            expert_cache,
            norm_gains[layer_index, 1],
            router_weight[layer_index],
            gate_weight[layer_index],
            up_weight[layer_index],
            down_weight[layer_index],
        )
        upstream, attention_grads, attention_gain = attention_backward(
            upstream,
            attention_cache,
            norm_gains[layer_index, 0],
            query_weight[layer_index],
            key_weight[layer_index],
            value_weight[layer_index],
            output_weight[layer_index],
            segment,
            position,
            valid_row,
            column,
        )
        collected[layer_index] = attention_grads + expert_grads
        gain_grads[layer_index] = jnp.stack([attention_gain, expert_gain])
        router_grads[layer_index] = router_part
    stacks = [
        jnp.stack([collected[layer_index][member] for layer_index in range(LAYERS)])
        for member in range(7)
    ]
    summed = (
        lax.psum_scatter(stacks[0][:, None], "dp", scatter_dimension=2, tiled=True),
        lax.psum_scatter(stacks[1][:, None], "dp", scatter_dimension=2, tiled=True),
        lax.psum_scatter(stacks[2][:, None], "dp", scatter_dimension=2, tiled=True),
        lax.psum_scatter(stacks[3][:, None], "dp", scatter_dimension=2, tiled=True),
        lax.psum_scatter(stacks[4], "dp", scatter_dimension=2, tiled=True),
        lax.psum_scatter(stacks[5], "dp", scatter_dimension=2, tiled=True),
        lax.psum_scatter(stacks[6], "dp", scatter_dimension=2, tiled=True),
    )
    finals = [
        summed[0][:, 0],
        summed[1][:, 0],
        summed[2][:, 0],
        summed[3][:, 0],
        summed[4],
        summed[5],
        summed[6],
    ]
    grad_gains, grad_router = lax.psum(
        (jnp.stack(gain_grads), jnp.stack(router_grads)), ("dp", "row")
    )
    grad_tokens = upstream.astype(jnp.bfloat16)
    return (
        block_output,
        grad_tokens,
        grad_gains,
        finals[0],
        finals[1],
        finals[2],
        finals[3],
        grad_router,
        finals[4],
        finals[5],
        finals[6],
    )


def solution(mesh):
    in_specs = (
        P(("dp", "row"), "col"),
        P(("dp", "row"), "col"),
        P(None, None, "col"),
        P(None, "col", "row"),
        P(None, "col", "row"),
        P(None, "col", "row"),
        P(None, "row", "col"),
        P(None, "col", None),
        P(None, None, "col", "row"),
        P(None, None, "col", "row"),
        P(None, None, "row", "col"),
        P(None, "dp", None),
        P(),
        P(),
    )
    out_specs = (
        P(("dp", "row"), "col"),
        P(("dp", "row"), "col"),
        P(None, None, "col"),
        P(None, ("col", "dp"), "row"),
        P(None, ("col", "dp"), "row"),
        P(None, ("col", "dp"), "row"),
        P(None, ("row", "dp"), "col"),
        P(None, "col", None),
        P(None, None, ("col", "dp"), "row"),
        P(None, None, ("col", "dp"), "row"),
        P(None, None, ("row", "dp"), "col"),
    )
    return jax.shard_map(shards, mesh=mesh, in_specs=in_specs, out_specs=out_specs, check_vma=False)
```

profile of v0, /device:TPU:6, one launch (start us, length us, event | category | flops | bytes accessed | tf_op | source)
XLA Modules:
  0.0 2297.7 jit_solution(16277060527518952334)
XLA Ops:
  37.4 16.9 all-reduce.28
  67.5 29.8 %reduce-scatter.20.cloned.1.call-done = f32[256,768]{1,0:T(8,128)} async-done(((f32[512,768]{1,0:T(8,128)}), f32[256,768]{1,0:T(8,128)}) %reduce-scatter.20.cloned.1.call-update) | async-done | bytes 786448 | tf_op jit(solution)/shard_map/reduce_scatter | solution.py:77
  104.0 13.0 all_gather.37
  131.6 15.6 reduce-scatter.22.cloned.1.call-done
  226.5 142.0 %all-reduce.27.cloned.1.call-done = (f32[8,288,384]{2,1,0:T(8,128)}, f32[8,288,384]{2,1,0:T(8,128)}) async-done(((f32[8,288,384]{2,1,0:T(8,128)}, f32[8,288,384]{2,1,0:T(8,128)}), (f32[8,288,384]{2,1,0:T(8,128)}, f32[8,288,384]{2,1,0:T(8,128)})) %all-reduce.27.cloned.1.call-update) | async-done | bytes 7077904 | tf_op jit(solution)/shard_map/psum | solution.py:284
  380.0 13.7 gather_fusion.2
  414.0 28.1 %reduce-scatter.24.cloned.1.call-done = f32[256,768]{1,0:T(8,128)} async-done(((f32[512,768]{1,0:T(8,128)}), f32[256,768]{1,0:T(8,128)}) %reduce-scatter.24.cloned.1.call-update) | async-done | bytes 786448 | tf_op jit(solution)/shard_map/reduce_scatter | solution.py:73
  465.2 17.6 all-reduce.29
  482.7 12.6 all-reduce.17.cloned.1.call-done
  497.5 29.7 %reduce-scatter.26.cloned.1.call-done = f32[256,768]{1,0:T(8,128)} async-done(((f32[512,768]{1,0:T(8,128)}), f32[256,768]{1,0:T(8,128)}) %reduce-scatter.26.cloned.1.call-update) | async-done | bytes 786448 | tf_op jit(solution)/shard_map/reduce_scatter | solution.py:77
  532.5 13.2 all_gather.40
  636.7 244.3 %all-reduce.25.cloned.1.call-done = (f32[8,288,384]{2,1,0:T(8,128)}, f32[8,288,384]{2,1,0:T(8,128)}, f32[8,288,384]{2,1,0:T(8,128)}) async-done(((f32[8,288,384]{2,1,0:T(8,128)}, f32[8,288,384]{2,1,0:T(8,128)}, f32[8,288,384]{2,1,0:T(8,128)}), (f32[8,288,384]{2,1,0:T(8,128)}, f32[8,288,384]{2,1,0:T(8,128)}, f32[8,288,384]{2,1,0:T(8,128)})) %all-reduce.25.cloned.1.call-update) | async-done | bytes 10616848 | tf_op jit(solution)/shard_map/psum | solution.py:284
  928.2 13.7 gather_fusion.7
  949.2 13.6 gather_fusion.5
  988.1 28.1 %reduce-scatter.32.cloned.1.call-done = f32[256,768]{1,0:T(8,128)} async-done(((f32[512,768]{1,0:T(8,128)}), f32[256,768]{1,0:T(8,128)}) %reduce-scatter.32.cloned.1.call-update) | async-done | bytes 786448 | tf_op jit(solution)/shard_map/reduce_scatter | solution.py:73
  1039.5 31.2 %reduce-scatter.34.cloned.1.call-done = f32[256,768]{1,0:T(8,128)} async-done(((f32[512,768]{1,0:T(8,128)}), f32[256,768]{1,0:T(8,128)}) %reduce-scatter.34.cloned.1.call-update) | async-done | bytes 786448 | tf_op jit(solution)/shard_map/reduce_scatter | solution.py:77
  1099.3 13.0 all_gather.44
  1113.8 18.0 all-reduce.19.cloned.1.call-done
  1173.4 23.4 %reduce-scatter.30.cloned.1.call-done = f32[256,768]{1,0:T(8,128)} async-done(((f32[512,768]{1,0:T(8,128)}), f32[256,768]{1,0:T(8,128)}) %reduce-scatter.30.cloned.1.call-update) | async-done | bytes 786448 | tf_op jit(solution)/shard_map/reduce_scatter | solution.py:73
  1229.7 103.5 %all-reduce.21.cloned.1.call-done = f32[8,288,384]{2,1,0:T(8,128)} async-done(((f32[8,288,384]{2,1,0:T(8,128)}), f32[8,288,384]{2,1,0:T(8,128)}) %all-reduce.21.cloned.1.call-update) | async-done | bytes 3538960 | tf_op jit(solution)/shard_map/psum | solution.py:65
  1349.7 13.7 gather_fusion.10
  1398.6 28.1 %reduce-scatter.38.cloned.1.call-done = f32[256,768]{1,0:T(8,128)} async-done(((f32[512,768]{1,0:T(8,128)}), f32[256,768]{1,0:T(8,128)}) %reduce-scatter.38.cloned.1.call-update) | async-done | bytes 786448 | tf_op jit(solution)/shard_map/reduce_scatter | solution.py:73
  1451.1 31.2 %reduce-scatter.40.cloned.1.call-done = f32[256,768]{1,0:T(8,128)} async-done(((f32[512,768]{1,0:T(8,128)}), f32[256,768]{1,0:T(8,128)}) %reduce-scatter.40.cloned.1.call-update) | async-done | bytes 786448 | tf_op jit(solution)/shard_map/reduce_scatter | solution.py:77
  1498.4 12.8 all-reduce.31
  1512.3 13.0 all_gather.47
  1526.8 17.9 all-reduce.23.cloned.1.call-done
  1561.3 22.7 copy.139
  1645.2 248.1 %all-reduce = (f32[2,2,768]{2,1,0:T(2,128)}, f32[2,768,8]{1,2,0:T(8,128)}) all-reduce(f32[2,2,768]{2,1,0:T(2,128)S(1)} %pad_maximum_fusion.12, f32[2,768,8]{1,2,0:T(8,128)S(1)} %pad_maximum_fusion.7), channel_id=1, replica_groups=mesh['dp'=32,'row'=2,'col'=2] {'dp','row'}, use_global_device_ids=true, to_apply=%region_82.87 | all-reduce | flops 15360 | bytes 122880 | tf_op jit(solution)/shard_map/psum | solution.py:485
  1897.4 54.8 %reduce-scatter.50.cloned.1.call-done = f32[2,1,24,768]{3,2,0,1:T(8,128)} async-done(((f32[2,1,768,768]{3,2,0,1:T(8,128)}), f32[2,1,24,768]{3,2,0,1:T(8,128)}) %reduce-scatter.50.cloned.1.call-update) | async-done | bytes 147472 | tf_op jit(solution)/shard_map/reduce_scatter | solution.py:471
  1952.2 87.2 %reduce-scatter.44.cloned.1.call-done = f32[2,1,24,768]{3,2,0,1:T(8,128)} async-done(((f32[2,1,768,768]{3,2,0,1:T(8,128)}), f32[2,1,24,768]{3,2,0,1:T(8,128)}) %reduce-scatter.44.cloned.1.call-update) | async-done | bytes 147472 | tf_op jit(solution)/shard_map/reduce_scatter | solution.py:468
  2039.4 126.1 %reduce-scatter.52.cloned.1.call-done = f32[2,8,24,384]{3,2,1,0:T(8,128)} async-done(((f32[2,8,768,384]{3,2,1,0:T(8,128)}), f32[2,8,24,384]{3,2,1,0:T(8,128)}) %reduce-scatter.52.cloned.1.call-update) | async-done | bytes 589840 | tf_op jit(solution)/shard_map/reduce_scatter | solution.py:472
  2165.4 125.3 %reduce-scatter.54.cloned.1.call-done = f32[2,8,24,384]{3,2,1,0:T(8,128)} async-done(((f32[2,8,768,384]{3,2,1,0:T(8,128)}), f32[2,8,24,384]{3,2,1,0:T(8,128)}) %reduce-scatter.54.cloned.1.call-update) | async-done | bytes 589840 | tf_op jit(solution)/shard_map/reduce_scatter | solution.py:473
  (672 shorter events, 678.8 us)
Async XLA Ops:
  7.2 58.1 %all-reduce.15.cloned.1.call-start = ((), (), s32[]{:S(2)}) async-start(), calls=%async_computation.20 | async-start | bytes 524288 | tf_op jit(solution)/shard_map/psum | solution.py:85
  30.2 67.1 %reduce-scatter.20.cloned.1.call-start = ((), (), s32[]{:S(2)}) async-start(), calls=%async_computation.19 | async-start | bytes 2359296 | tf_op jit(solution)/shard_map/reduce_scatter | solution.py:77
  32.3 114.9 %reduce-scatter.22.cloned.1.call-start = ((), (), s32[]{:S(2)}) async-start(), calls=%async_computation.21 | async-start | bytes 2359296 | tf_op jit(solution)/shard_map/reduce_scatter | solution.py:73
  35.5 459.8 %copy-start.142 = (f32[64]{0:T(128)}, f32[64]{0:T(128)S(1)}, u32[]{:S(2)}) copy-start(f32[64]{0:T(128)S(1)} %multiply_power_fusion) | copy-start | bytes 772
  36.2 459.1 %copy-start.116 = (f32[512]{0:T(512)}, f32[512]{0:T(512)S(1)}, u32[]{:S(2)}) copy-start(f32[512]{0:T(512)S(1)} %get-tuple-element.102) | copy-start | bytes 6148
  119.0 249.5 %all-reduce.27.cloned.1.call-start = ((), (), s32[]{:S(2)}) async-start(), calls=%async_computation.44 | async-start | bytes 14155776 | tf_op jit(solution)/shard_map/psum | solution.py:284
  148.5 293.6 %copy-start.19 = (f32[256,768]{1,0:T(8,128)}, f32[256,768]{1,0:T(8,128)S(1)}, u32[]{:S(2)}) copy-start(f32[256,768]{1,0:T(8,128)S(1)} %get-tuple-element.101) | copy-start | bytes 2359300
  188.4 253.7 %reduce-scatter.24.cloned.1.call-start = ((), (), s32[]{:S(2)}) async-start(), calls=%async_computation.22 | async-start | bytes 2359296 | tf_op jit(solution)/shard_map/reduce_scatter | solution.py:73
  413.9 81.4 %all-reduce.17.cloned.1.call-start = ((), (), s32[]{:S(2)}) async-start(), calls=%async_computation.24 | async-start | bytes 524288 | tf_op jit(solution)/shard_map/psum | solution.py:85
  461.5 65.8 %reduce-scatter.26.cloned.1.call-start = ((), (), s32[]{:S(2)}) async-start(), calls=%async_computation.23 | async-start | bytes 2359296 | tf_op jit(solution)/shard_map/reduce_scatter | solution.py:77
  464.7 111.9 %reduce-scatter.28.cloned.1.call-start = ((), (), s32[]{:S(2)}) async-start(), calls=%async_computation.25 | async-start | bytes 2359296 | tf_op jit(solution)/shard_map/reduce_scatter | solution.py:73
  547.7 333.3 %all-reduce.25.cloned.1.call-start = ((), (), s32[]{:S(2)}) async-start(), calls=%async_computation.43 | async-start | bytes 21233664 | tf_op jit(solution)/shard_map/psum | solution.py:284
  577.9 446.7 %copy-start.23 = (f32[256,768]{1,0:T(8,128)}, f32[256,768]{1,0:T(8,128)S(1)}, u32[]{:S(2)}) copy-start(f32[256,768]{1,0:T(8,128)S(1)} %get-tuple-element.95) | copy-start | bytes 2359300
  584.4 431.8 %copy-start.130 = (f32[256]{0:T(256)}, f32[256]{0:T(256)S(1)}, u32[]{:S(2)}) copy-start(f32[256]{0:T(256)S(1)} %add_rsqrt_fusion) | copy-start | bytes 3076
  625.6 390.5 %reduce-scatter.32.cloned.1.call-start = ((), (), s32[]{:S(2)}) async-start(), calls=%async_computation.27 | async-start | bytes 2359296 | tf_op jit(solution)/shard_map/reduce_scatter | solution.py:73
  988.0 82.7 %reduce-scatter.34.cloned.1.call-start = ((), (), s32[]{:S(2)}) async-start(), calls=%async_computation.28 | async-start | bytes 2359296 | tf_op jit(solution)/shard_map/reduce_scatter | solution.py:77
  1039.4 92.3 %all-reduce.19.cloned.1.call-start = ((), (), s32[]{:S(2)}) async-start(), calls=%async_computation.29 | async-start | bytes 524288 | tf_op jit(solution)/shard_map/psum | solution.py:85
  1098.3 66.7 %reduce-scatter.36.cloned.1.call-start = ((), (), s32[]{:S(2)}) async-start(), calls=%async_computation.30 | async-start | bytes 2359296 | tf_op jit(solution)/shard_map/reduce_scatter | solution.py:73
  1136.8 60.0 %reduce-scatter.30.cloned.1.call-start = ((), (), s32[]{:S(2)}) async-start(), calls=%async_computation.26 | async-start | bytes 2359296 | tf_op jit(solution)/shard_map/reduce_scatter | solution.py:73
  1152.7 180.5 %all-reduce.21.cloned.1.call-start = ((), (), s32[]{:S(2)}) async-start(), calls=%async_computation.31 | async-start | bytes 7077888 | tf_op jit(solution)/shard_map/psum | solution.py:65
  1229.7 197.0 %reduce-scatter.38.cloned.1.call-start = ((), (), s32[]{:S(2)}) async-start(), calls=%async_computation.32 | async-start | bytes 2359296 | tf_op jit(solution)/shard_map/reduce_scatter | solution.py:73
  1398.5 83.8 %reduce-scatter.40.cloned.1.call-start = ((), (), s32[]{:S(2)}) async-start(), calls=%async_computation.33 | async-start | bytes 2359296 | tf_op jit(solution)/shard_map/reduce_scatter | solution.py:77
  1451.1 93.6 %all-reduce.23.cloned.1.call-start = ((), (), s32[]{:S(2)}) async-start(), calls=%async_computation.34 | async-start | bytes 524288 | tf_op jit(solution)/shard_map/psum | solution.py:85
  1511.3 126.0 %reduce-scatter.42.cloned.1.call-start = ((), (), s32[]{:S(2)}) async-start(), calls=%async_computation.35 | async-start | bytes 2359296 | tf_op jit(solution)/shard_map/reduce_scatter | solution.py:73
  1551.6 343.9 %reduce-scatter.56.cloned.1.call-start = ((), (), s32[]{:S(2)}) async-start(), calls=%async_computation.42 | async-start | bytes 19464192 | tf_op jit(solution)/shard_map/reduce_scatter | solution.py:474
  1584.1 313.3 %reduce-scatter.48.cloned.1.call-start = ((), (), s32[]{:S(2)}) async-start(), calls=%async_computation.38 | async-start | bytes 811008 | tf_op jit(solution)/shard_map/reduce_scatter | solution.py:470
  1587.0 310.4 %reduce-scatter.46.cloned.1.call-start = ((), (), s32[]{:S(2)}) async-start(), calls=%async_computation.37 | async-start | bytes 811008 | tf_op jit(solution)/shard_map/reduce_scatter | solution.py:469
  1590.1 362.1 %reduce-scatter.50.cloned.1.call-start = ((), (), s32[]{:S(2)}) async-start(), calls=%async_computation.39 | async-start | bytes 4866048 | tf_op jit(solution)/shard_map/reduce_scatter | solution.py:471
  1595.5 443.9 %reduce-scatter.44.cloned.1.call-start = ((), (), s32[]{:S(2)}) async-start(), calls=%async_computation.36 | async-start | bytes 4866048 | tf_op jit(solution)/shard_map/reduce_scatter | solution.py:468
  1600.8 564.6 %reduce-scatter.52.cloned.1.call-start = ((), (), s32[]{:S(2)}) async-start(), calls=%async_computation.40 | async-start | bytes 19464192 | tf_op jit(solution)/shard_map/reduce_scatter | solution.py:472
  1618.8 672.0 %reduce-scatter.54.cloned.1.call-start = ((), (), s32[]{:S(2)}) async-start(), calls=%async_computation.41 | async-start | bytes 19464192 | tf_op jit(solution)/shard_map/reduce_scatter | solution.py:473
  1635.3 258.1 %copy-start.148 = (f32[256]{0:T(256)S(1)}, f32[256]{0:T(256)}, u32[]{:S(2)}) copy-start(f32[256]{0:T(256)} %copy-done.147) | copy-start | bytes 3076
  (163 other events, 3684.3 us)
Sparse Core Ops, SparseCore 0:
  30.4 34.9 all-reduce.14
  67.8 29.5 reduce-scatter.19
  119.1 27.9 reduce-scatter.21
  188.5 179.9 all-reduce.26
  414.0 27.9 reduce-scatter.23
  461.6 33.6 all-reduce.16
  497.7 29.5 reduce-scatter.25
  547.9 28.6 reduce-scatter.27
  625.8 255.2 all-reduce.24
  988.2 27.9 reduce-scatter.31
  1039.5 31.1 reduce-scatter.33
  1098.4 33.2 all-reduce.18
  1137.0 27.9 reduce-scatter.35
  1167.2 29.5 reduce-scatter.29
  1229.8 103.3 all-reduce.20
  1398.6 27.9 reduce-scatter.37
  1451.2 31.1 reduce-scatter.39
  1511.4 33.3 all-reduce.22
  1551.7 27.9 reduce-scatter.41
  1584.2 121.9 reduce-scatter.55
  1710.7 74.5 reduce-scatter.47
  1789.7 74.6 reduce-scatter.45
  1869.2 82.9 reduce-scatter.49
  1956.3 82.9 reduce-scatter.43
  2044.4 120.9 reduce-scatter.51
  2169.8 120.8 reduce-scatter.53
where the time goes:
time: 2310 us; the launch traced here: 2300 us
  waiting for transfers between devices  1210 us (52%)
  blocking collectives  519 us (22%)
  local copies, waits for them, and re-layouts  236 us (10%)
  other arithmetic  159 us (7%)
  matrix products  155 us (7%)
    psum x2, waiting for transfers between devices, expert_forward(): lax.psum((jnp.einsum('esd,edf->esf', expert_rows, gate_weight, preferred_...  386 us
    psum x1, blocking collectives, shards(): lax.psum((jnp.stack(gain_grads), jnp.stack(router_grads)), ('dp', 'row'))  248 us
    reduce_scatter x8, waiting for transfers between devices, rows_share(): lax.psum_scatter(partial_value, 'row', scatter_dimension=0, tiled=True)  144 us
    reduce_scatter x1, waiting for transfers between devices, shards(): lax.psum_scatter(stacks[4], 'dp', scatter_dimension=2, tiled=True)  126 us
    reduce_scatter x1, waiting for transfers between devices, shards(): lax.psum_scatter(stacks[5], 'dp', scatter_dimension=2, tiled=True)  125 us
    reduce_scatter x4, waiting for transfers between devices, cols_share(): lax.psum_scatter(partial_value, 'col', scatter_dimension=0, tiled=True)  122 us
    psum x1, waiting for transfers between devices, feature_total(): return lax.psum(partial_value, 'col')  103 us
    reduce_scatter x1, waiting for transfers between devices, shards(): lax.psum_scatter(stacks[0][:, None], 'dp', scatter_dimension=2, tiled=True)  87.2 us
  transfers between devices with their start and end apart: 26, of which 22 were waited for; matrix products, arithmetic and copies ran while one was open for 7% of the time, Pallas kernels for 0%

commit v1 on v0

v1 whole, which is shorter than its diff:
```python
import jax
import jax.numpy as jnp
from jax import lax
from jax.sharding import PartitionSpec as P

D = 1536
HALF = D // 2
HEAD = 128
Q_HEADS = 6
EXPERTS = 8
MINE = 4
FF = 384
LAYERS = 2
TOK_DP = 512
QUARTER = 128
EPSILON = 1e-06
ROPE_THETA = 1000000.0
MASKED_SCORE = -1e30
ACROSS = (((1,), (1,)), ((), ()))
DOWNWARD = (((0,), (0,)), ((), ()))
SWAP = [(0, 1), (1, 0)]
DIAGONAL = [(0, 3), (1, 2), (2, 1), (3, 0)]
N_DP = 32
BF16 = jnp.bfloat16
F32 = jnp.float32


def dot(a, b):
    return jnp.dot(a, b, preferred_element_type=F32)


def dot_across(a, b):
    return lax.dot_general(a, b, ACROSS, preferred_element_type=F32)


def dot_down(a, b):
    return lax.dot_general(a, b, DOWNWARD, preferred_element_type=F32)


def over_row(x):
    return lax.ppermute(x, "row", SWAP)


def over_col(x):
    return lax.ppermute(x, "col", SWAP)


def over_both(x):
    return lax.ppermute(x, ("row", "col"), DIAGONAL)


def over_dp(x, target):
    return lax.ppermute(x, "dp", [(i, target(i)) for i in range(N_DP)])


def by_col(column, own, other, axis):
    return jnp.where(
        column == 0,
        jnp.concatenate([own, other], axis=axis),
        jnp.concatenate([other, own], axis=axis),
    )


def half_of(x, index, axis):
    size = x.shape[axis] // 2
    return lax.dynamic_slice_in_dim(x, index * size, size, axis=axis)


def halves(x):
    return [x[:, :HALF], x[:, HALF:]]


def pack(parts):
    return jnp.concatenate([x.astype(BF16) for x in parts], axis=1)


def to_quarter(block, column):
    own = half_of(block, column, 0)
    other = over_col(half_of(block, 1 - column, 0))
    return by_col(column, own, other, 1)


def from_quarter(block, column):
    own = half_of(block, column, 1)
    other = over_col(half_of(block, 1 - column, 1))
    return by_col(column, own, other, 0)


def gather_four(x):
    return jnp.concatenate([x, over_row(x), over_col(x), over_both(x)], axis=0)


def scatter_four(x):
    own, row, col, both = [x[i * QUARTER : (i + 1) * QUARTER] for i in range(4)]
    return (
        own
        + over_row(row.astype(BF16)).astype(F32)
        + over_col(col.astype(BF16)).astype(F32)
        + over_both(both.astype(BF16)).astype(F32)
    )


def gather_two(x):
    return jnp.concatenate([x, over_row(x)], axis=0)


def scatter_two(x):
    return x[:QUARTER] + over_row(x[QUARTER:].astype(BF16)).astype(F32)


def segments(seq_lengths, seq_owner, data_index):
    owned_len = jnp.where(seq_owner == data_index, seq_lengths, 0)
    seq_ends = jnp.cumsum(owned_len)
    places = jnp.arange(TOK_DP, dtype=jnp.int32)
    finished = (seq_ends[None, :] <= places[:, None]).astype(jnp.int32)
    segment = jnp.sum(finished, axis=1)
    starts = jnp.sum(finished * owned_len[None, :], axis=1)
    valid_row = places < jnp.sum(owned_len)
    position = jnp.where(valid_row, places - starts, 0)
    return (segment, position, valid_row, places)


def rotate(values, cosine, sine):
    half_dim = values.shape[-1] // 2
    former = values[..., :half_dim]
    latter = values[..., half_dim:]
    return jnp.concatenate(
        [former * cosine - latter * sine, latter * cosine + former * sine], axis=-1
    )


def normalize(stream, gain):
    inv_rms = lax.rsqrt(jnp.mean(stream * stream, axis=1, keepdims=True) + EPSILON)
    return (inv_rms, (stream * inv_rms * gain).astype(BF16))


def norm_back(upstream, grad_normed, stream, inv_rms, gain):
    scaled = gain * grad_normed
    dots = jnp.sum(scaled * stream, axis=1, keepdims=True)
    grad_stream = upstream + inv_rms * scaled - stream * (inv_rms * inv_rms * inv_rms * dots / D)
    grad_gain = jnp.sum(grad_normed * stream * inv_rms, axis=0)
    return (grad_stream, grad_gain)


def attention_weights(own, column, core):
    sent = over_col(half_of(own, core, 0))
    swapped = over_dp(sent, lambda i: i ^ 1)
    return jnp.where(
        core == 0,
        jnp.concatenate([sent, swapped], axis=0),
        jnp.concatenate([swapped, sent], axis=0),
    )


def expert_weights(gate, up, down, column, data_index):
    rows = 48
    start = (data_index % 16) * rows

    def piece(weight, side):
        cut = lax.dynamic_slice(weight, (MINE * side, start, 0), (MINE, rows, FF))
        return cut.transpose(1, 0, 2).reshape(rows, MINE * FF)

    def down_piece(side):
        place = (MINE * side + data_index // 8, (data_index % 8) * rows, 0)
        return lax.dynamic_slice(down, place, (1, rows, HALF))[0]

    def pack(side):
        return jnp.concatenate([piece(gate, side), piece(up, side), down_piece(side)], axis=1)

    other = over_col(pack(1 - column))
    own = pack(column)
    mine = data_index // 16 == column
    gate_up = jnp.where(mine, own[:, : 2 * D], other[:, : 2 * D])
    downs = by_col(column, own[:, 2 * D :], other[:, 2 * D :], 1)
    whole = lax.all_gather(jnp.concatenate([gate_up, downs], axis=1), "dp", axis=0, tiled=True)
    return (whole[:, : 2 * D], whole[:, 2 * D :])


def attention_forward(stream, gain, qkv_weight, out_weight, geometry):
    cosine, sine, seen_mask, row_valid = geometry
    inv_rms, normed = normalize(stream, gain)
    inputs = gather_two(normed)
    qkv = dot(inputs, qkv_weight)
    rows = inputs.shape[0]
    width = Q_HEADS * HEAD
    key_rot = rotate(qkv[:, width : width + HEAD], cosine, sine).astype(BF16)
    value_low = qkv[:, width + HEAD :].astype(BF16)
    pair = jnp.concatenate([key_rot, value_low], axis=1)
    pair = jnp.concatenate([pair, over_col(pair)], axis=0)
    keys, values = pair[:, :HEAD], pair[:, HEAD:]
    query = qkv[:, :width].reshape(rows, Q_HEADS, HEAD).transpose(1, 0, 2)
    query_rot = rotate(query, cosine, sine).astype(BF16).reshape(Q_HEADS * rows, HEAD)
    scores = dot_across(query_rot, keys).reshape(Q_HEADS, rows, TOK_DP) * HEAD ** (-0.5)
    row_max = jnp.max(jnp.where(seen_mask, scores, MASKED_SCORE), axis=-1, keepdims=True)
    row_max = jnp.where(row_valid, row_max, 0.0)
    exponent = jnp.where(seen_mask, jnp.exp(scores - row_max), 0.0)
    denominator = jnp.sum(exponent, axis=-1, keepdims=True) + jnp.where(row_valid, 0.0, 1.0)
    log_total = row_max + jnp.log(denominator)
    probabilities = (exponent / denominator).astype(BF16).reshape(Q_HEADS * rows, TOK_DP)
    attended = dot(probabilities, values).reshape(Q_HEADS, rows, HEAD)
    attended = attended.transpose(1, 0, 2).reshape(rows, width).astype(BF16)
    branch = scatter_two(dot(attended, out_weight))
    cache = (stream, inv_rms, inputs, query_rot, keys, values, log_total, attended)
    return (cache, stream + branch)


def attention_backward(upstream, cache, gain, qkv_weight, out_weight, geometry):
    cosine, sine, seen_mask, row_valid = geometry
    stream, inv_rms, inputs, query_rot, keys, values, log_total, attended = cache
    rows = inputs.shape[0]
    width = Q_HEADS * HEAD
    out_grad = gather_two(upstream.astype(BF16))
    attended_grad = dot_across(out_grad, out_weight).astype(BF16)
    attended_grad = (
        attended_grad.reshape(rows, Q_HEADS, HEAD).transpose(1, 0, 2).reshape(Q_HEADS * rows, HEAD)
    )
    scores = dot_across(query_rot, keys).reshape(Q_HEADS, rows, TOK_DP) * HEAD ** (-0.5)
    probabilities = jnp.where(seen_mask, jnp.exp(scores - log_total), 0.0)
    prob_grad = dot_across(attended_grad, values).reshape(Q_HEADS, rows, TOK_DP)
    low_prob = probabilities.astype(BF16).reshape(Q_HEADS * rows, TOK_DP)
    value_grad = dot_down(low_prob, attended_grad)
    row_delta = jnp.sum(prob_grad * probabilities, axis=-1, keepdims=True)
    score_grad = (probabilities * (prob_grad - row_delta)).astype(BF16)
    score_grad = score_grad.reshape(Q_HEADS * rows, TOK_DP)
    key_grad = dot_down(score_grad, query_rot) * HEAD ** (-0.5)
    pair = jnp.concatenate([key_grad, value_grad], axis=1)
    pair = pair[:rows] + over_col(pair[rows:].astype(BF16)).astype(F32)
    query_grad = dot(score_grad, keys) * HEAD ** (-0.5)
    query_grad = rotate(query_grad.reshape(Q_HEADS, rows, HEAD), cosine, -sine)
    query_grad = query_grad.transpose(1, 0, 2).reshape(rows, width)
    key_grad = rotate(pair[:, :HEAD], cosine, -sine)
    qkv_grad = jnp.concatenate([query_grad, key_grad, pair[:, HEAD:]], axis=1).astype(BF16)
    normed_grad = scatter_two(dot_across(qkv_grad, qkv_weight))
    packed = pack(
        [dot_down(x, qkv_grad) for x in halves(inputs)]
        + [dot_down(attended, x) for x in halves(out_grad)]
    )
    grad_stream, grad_gain = norm_back(upstream, normed_grad, stream, inv_rms, gain)
    return (grad_stream, packed, grad_gain)


def spread(share):
    rows = share.shape[0]
    return jnp.concatenate(
        [jnp.broadcast_to(share[:, e : e + 1], (rows, FF)) for e in range(MINE)], axis=1
    )


def expert_forward(stream, gain, router, gate_up_weight, down_weight, chosen_mask, column):
    inv_rms, normed = normalize(stream, gain)
    inputs = gather_four(normed)
    logits = dot(inputs, router)
    top = jnp.max(jnp.where(chosen_mask, logits, MASKED_SCORE), axis=1, keepdims=True)
    exponent = jnp.where(chosen_mask, jnp.exp(logits - top), 0.0)
    share = exponent / jnp.sum(exponent, axis=1, keepdims=True)
    mine = lax.dynamic_slice_in_dim(share, column * MINE, MINE, axis=1)
    gate_up = dot(inputs, gate_up_weight)
    gate_value, up_value = gate_up[:, :D], gate_up[:, D:]
    hidden = (spread(mine) * jax.nn.silu(gate_value) * up_value).astype(BF16)
    branch = scatter_four(dot(hidden, down_weight))
    cache = (stream, inv_rms, inputs, gate_up, share, mine, hidden)
    return (cache, stream + branch)


def split_low(values):
    high = values.astype(BF16)
    low = (values - high.astype(F32)).astype(BF16)
    return jnp.concatenate([high, low], axis=1)


def expert_backward(upstream, cache, gain, router, gate_up_weight, down_weight, column):
    stream, inv_rms, inputs, gate_up, share, mine, hidden = cache
    gate_value, up_value = gate_up[:, :D], gate_up[:, D:]
    rows = inputs.shape[0]
    out_grad = gather_four(upstream.astype(BF16))
    hidden_grad = dot_across(out_grad, down_weight)
    sigmoid_gate = jax.nn.sigmoid(gate_value)
    silu_gate = gate_value * sigmoid_gate
    share_grad = jnp.sum((hidden_grad * silu_gate * up_value).reshape(rows, MINE, FF), axis=2)
    activation_grad = hidden_grad * spread(mine)
    gate_grad = (
        activation_grad * up_value * sigmoid_gate * (1.0 + gate_value * (1.0 - sigmoid_gate))
    )
    gate_up_grad = jnp.concatenate([gate_grad, activation_grad * silu_gate], axis=1).astype(BF16)
    zeros = jnp.zeros_like(share_grad)
    share_grad = by_col(column, share_grad, zeros, 1)
    logits_grad = share * (share_grad - jnp.sum(share * share_grad, axis=1, keepdims=True))
    logits_low = split_low(logits_grad)
    input_grad = dot_across(gate_up_grad, gate_up_weight)
    input_grad = input_grad + dot_across(logits_low, jnp.concatenate([router, router], axis=1))
    normed_grad = scatter_four(input_grad)
    packed = pack(
        [dot_down(x, gate_up_grad) for x in halves(inputs)]
        + [dot_down(x, out_grad) for x in halves(hidden)]
    )
    router_grad = dot_down(logits_low, inputs)
    router_grad = router_grad[:EXPERTS] + router_grad[EXPERTS:]
    grad_stream, grad_gain = norm_back(upstream, normed_grad, stream, inv_rms, gain)
    return (grad_stream, packed, grad_gain, router_grad)


def sum_over_dp(packed):
    return lax.psum_scatter(packed, "dp", scatter_dimension=0, tiled=True)


def sum_everywhere(values):
    values = values + over_row(values)
    for step in (1, 8, 16, 2, 4):
        values = values + over_dp(values, lambda i, step=step: i ^ step)
    return values


def swap_half(block, column, width):
    own = lax.dynamic_slice_in_dim(block, column * width, width, axis=1)
    other = over_col(lax.dynamic_slice_in_dim(block, (1 - column) * width, width, axis=1))
    return (own, other)


def place_attention(summed, column):
    split = 2 * (Q_HEADS + 2) * HEAD
    parts = (swap_half(summed[:, :split], column, split // 2), swap_half(summed[:, split:], column, HALF))
    return [own.astype(F32) + other.astype(F32) for own, other in parts]


def place_experts(summed, column, data_index):
    own, other = swap_half(summed[:, : 4 * D], column, 2 * D)

    def unfold(block):
        return block.reshape(24, 2, MINE, FF).transpose(1, 2, 0, 3)

    gate_up = by_col(column, unfold(own), unfold(other), 1).astype(F32)
    down = summed[:, 4 * D :]
    upper = (data_index >= 16).astype(jnp.int32)
    former = lax.dynamic_slice_in_dim(down, 12 * upper, 12, axis=0)
    latter = lax.dynamic_slice_in_dim(down, 12 - 12 * upper, 12, axis=0)
    former = over_dp(former, lambda i: 2 * (i % 16) + i // 16)
    latter = over_dp(latter, lambda i: 2 * (i % 16) + 1 - i // 16)
    odd = data_index % 2 == 1
    low, high = jnp.where(odd, latter, former), jnp.where(odd, former, latter)
    down = jnp.stack([low[:, :D], high[:, :D], low[:, D:], high[:, D:]])
    down_other = over_col(half_of(down, 1 - column, 2))
    down = by_col(column, half_of(down, column, 2), down_other, 0).astype(F32)
    return (gate_up[0], gate_up[1], down)


def shards(
    tokens,
    cotangent,
    norm_gains,
    query_weight,
    key_weight,
    value_weight,
    output_weight,
    router_weight,
    gate_weight,
    up_weight,
    down_weight,
    expert_ids,
    seq_lengths,
    seq_owner,
):
    data_index = lax.axis_index("dp")
    row = lax.axis_index("row")
    column = lax.axis_index("col")
    core = data_index % 2
    stream = to_quarter(tokens, column).astype(F32)
    qkv_own = [
        jnp.concatenate([query_weight[i], key_weight[i], value_weight[i]], axis=1)
        for i in range(LAYERS)
    ]
    qkv_weights, out_weights, expert_parts = [None] * LAYERS, [None] * LAYERS, [None] * LAYERS
    for i in range(LAYERS):
        other = attention_weights(qkv_own[i], column, core)
        qkv_weights[i] = by_col(column, qkv_own[i], other, 0)
        other = attention_weights(output_weight[i], column, core)
        out_weights[i] = by_col(column, output_weight[i], other, 1)
        expert_parts[i] = expert_weights(
            gate_weight[i], up_weight[i], down_weight[i], column, data_index
        )
    gains = norm_gains.reshape(2 * LAYERS, HALF)
    router_own = router_weight.transpose(0, 2, 1).reshape(LAYERS * EXPERTS, HALF)
    small = jnp.concatenate([gains, router_own], axis=0)
    small = by_col(column, small, over_col(small), 1)
    gains = small[: 2 * LAYERS].astype(F32).reshape(LAYERS, 2, D)
    routers = small[2 * LAYERS :].reshape(LAYERS, EXPERTS, D).transpose(0, 2, 1)

    segment, position, valid_row, places = segments(seq_lengths, seq_owner, data_index)
    starts = (
        row * 256 + column * QUARTER,
        (1 - row) * 256 + column * QUARTER,
        row * 256 + (1 - column) * QUARTER,
        (1 - row) * 256 + (1 - column) * QUARTER,
    )

    def arranged(x, axis=0):
        return jnp.concatenate(
            [lax.dynamic_slice_in_dim(x, s, QUARTER, axis=axis) for s in starts], axis=axis
        )

    segment, position, places = arranged(segment), arranged(position), arranged(places)
    valid_row = arranged(valid_row.astype(jnp.int32)) > 0
    ids = arranged(expert_ids, 1)
    chosen_masks = jnp.any(
        ids[:, :, :, None] == jnp.arange(EXPERTS, dtype=jnp.int32)[None, None, None, :], axis=2
    )
    rows = 2 * QUARTER
    frequency = jnp.power(
        ROPE_THETA, jnp.arange(HEAD // 2, dtype=F32) * (-2.0 / HEAD)
    )
    angle = position[:rows].astype(F32)[:, None] * frequency[None, :]
    seen_mask = (
        (segment[:rows, None] == segment[None, :])
        & (places[None, :] <= places[:rows, None])
        & valid_row[:rows, None]
    )
    geometry = (jnp.cos(angle), jnp.sin(angle), seen_mask[None], valid_row[:rows][None, :, None])

    caches = []
    for i in range(LAYERS):
        attention_cache, stream = attention_forward(
            stream, gains[i, 0], qkv_weights[i], out_weights[i], geometry
        )
        expert_cache, stream = expert_forward(
            stream, gains[i, 1], routers[i], *expert_parts[i], chosen_masks[i], column
        )
        caches.append((attention_cache, expert_cache))
    block_output = from_quarter(stream.astype(BF16), column)
    upstream = to_quarter(cotangent, column).astype(F32)
    attention_sums, expert_sums, smalls = [None] * LAYERS, [None] * LAYERS, [None] * LAYERS
    for i in reversed(range(LAYERS)):
        attention_cache, expert_cache = caches[i]
        upstream, packed, expert_gain, router_grad = expert_backward(
            upstream, expert_cache, gains[i, 1], routers[i], *expert_parts[i], column
        )
        expert_sums[i] = sum_over_dp(packed)
        upstream, packed, attention_gain = attention_backward(
            upstream, attention_cache, gains[i, 0], qkv_weights[i], out_weights[i], geometry
        )
        attention_sums[i] = sum_over_dp(packed)
        smalls[i] = jnp.concatenate([attention_gain[None], expert_gain[None], router_grad], axis=0)
    grad_tokens = from_quarter(upstream.astype(BF16), column)

    small = jnp.concatenate(smalls, axis=0)
    small = half_of(small, column, 1) + over_col(half_of(small, 1 - column, 1))
    small = sum_everywhere(small).reshape(LAYERS, 2 + EXPERTS, HALF)
    grad_gains = small[:, :2]
    grad_router = small[:, 2:].transpose(0, 2, 1)

    attention = [place_attention(x, column) for x in attention_sums]
    qkv_grad, out_grad = [jnp.stack([x[k] for x in attention]) for k in range(2)]
    parts = [place_experts(x, column, data_index) for x in expert_sums]
    grad_gate, grad_up, grad_down = [jnp.stack([p[k] for p in parts]) for k in range(3)]
    width = Q_HEADS * HEAD
    return (
        block_output,
        grad_tokens,
        grad_gains,
        qkv_grad[:, :, :width],
        qkv_grad[:, :, width : width + HEAD],
        qkv_grad[:, :, width + HEAD :],
        out_grad,
        grad_router,
        grad_gate,
        grad_up,
        grad_down,
    )


def solution(mesh):
    in_specs = (
        P(("dp", "row"), "col"),
        P(("dp", "row"), "col"),
        P(None, None, "col"),
        P(None, "col", "row"),
        P(None, "col", "row"),
        P(None, "col", "row"),
        P(None, "row", "col"),
        P(None, "col", None),
        P(None, None, "col", "row"),
        P(None, None, "col", "row"),
        P(None, None, "row", "col"),
        P(None, "dp", None),
        P(),
        P(),
    )
    out_specs = (
        P(("dp", "row"), "col"),
        P(("dp", "row"), "col"),
        P(None, None, "col"),
        P(None, ("col", "dp"), "row"),
        P(None, ("col", "dp"), "row"),
        P(None, ("col", "dp"), "row"),
        P(None, ("row", "dp"), "col"),
        P(None, "col", None),
        P(None, None, ("col", "dp"), "row"),
        P(None, None, ("col", "dp"), "row"),
        P(None, None, ("row", "dp"), "col"),
    )
    return jax.shard_map(shards, mesh=mesh, in_specs=in_specs, out_specs=out_specs, check_vma=False)
```

time: 2310 us -> 847 us (0.37)
  waiting for transfers between devices: 1210 us -> 364 us
  blocking collectives: 519 us -> 0 us
  local copies, waits for them, and re-layouts: 236 us -> 98.2 us
  starting transfers between devices: 1.93 us -> 116 us
  other arithmetic: 159 us -> 116 us
  matrix products: 155 us -> 125 us
    psum x7 -> x0, waiting for transfers between devices: 549 us -> none  [the longest x2 386 us: expert_forward(): lax.psum((jnp.einsum('esd,edf->esf', expert_rows, gate_weight, preferred_...]
    reduce_scatter x19 -> x4, waiting for transfers between devices: 660 us -> 169 us  [sum_over_dp(): return lax.psum_scatter(packed, 'dp', scatter_dimension=0, tiled=True)]
    psum x15 -> x0, blocking collectives: 381 us -> none  [the longest x1 248 us: shards(): lax.psum((jnp.stack(gain_grads), jnp.stack(router_grads)), ('dp', 'row'))]
    ppermute x0 -> x70, waiting for transfers between devices: none -> 196 us  [the longest x32 103 us: over_col(): return lax.ppermute(x, 'col', SWAP)]
    all_gather x12 -> x0, blocking collectives: 138 us -> none  [the longest x8 86.2 us: rows_whole(): return lax.all_gather(shard_piece, 'row', axis=0, tiled=True)]
    gather x12 -> x0, local copies, waits for them, and re-layouts: 134 us -> none  [the longest x2 27.4 us: expert_backward(): jnp.take(rows_grad.reshape(EXPERTS * CAP, -1), pair_slot, axis=0)]
    ppermute x0 -> x70, starting transfers between devices: none -> 116 us  [the longest x32 68.1 us: over_col(): return lax.ppermute(x, 'col', SWAP)]
    reduce_sum x24 -> x14, other arithmetic: 52.4 us -> 12 us  [the longest x2 4.55 us: expert_backward(): jnp.sum((hidden_grad * silu_gate * up_value).reshape(rows, MINE, FF), axi...]
  transfers between devices with their start and end apart: 26 -> 76, of which waited for: 22 -> 51; matrix products, arithmetic and copies ran while one was open for 7% -> 31% of each run, Pallas kernels for 0% -> 0%
where the time goes in v1:
time: 847 us; the launch traced here: 838 us
  waiting for transfers between devices  364 us (43%)
  matrix products  125 us (15%)
  starting transfers between devices  116 us (14%)
  other arithmetic  116 us (14%)
  local copies, waits for them, and re-layouts  98.2 us (12%)
  between operations  17.7 us (2%)
    reduce_scatter x4, waiting for transfers between devices, sum_over_dp(): return lax.psum_scatter(packed, 'dp', scatter_dimension=0, tiled=True)  169 us
    ppermute x32, waiting for transfers between devices, over_col(): return lax.ppermute(x, 'col', SWAP)  103 us
    ppermute x32, starting transfers between devices, over_col(): return lax.ppermute(x, 'col', SWAP)  68.1 us
    ppermute x17, waiting for transfers between devices, over_row(): return lax.ppermute(x, 'row', SWAP)  59.6 us
    dot_general x14, matrix products, dot_across(): return lax.dot_general(a, b, ACROSS, preferred_element_type=F32)  52.3 us
    dot_general x14, matrix products, dot(): return jnp.dot(a, b, preferred_element_type=F32)  39.4 us
    dot_general x22, matrix products, dot_down(): return lax.dot_general(a, b, DOWNWARD, preferred_element_type=F32)  33.6 us
    concatenate x4, other arithmetic, pack(): return jnp.concatenate([x.astype(BF16) for x in parts], axis=1)  28.3 us
  transfers between devices with their start and end apart: 76, of which 51 were waited for; matrix products, arithmetic and copies ran while one was open for 31% of the time, Pallas kernels for 0%

profile of v1, /device:TPU:6, one launch (start us, length us, event | category | flops | bytes accessed | tf_op | source)
XLA Modules:
  0.0 838.4 jit_solution(7351943672552088802)
XLA Ops:
  7.3 8.8 %fusion.234 = (bf16[1,8,768,384]{3,2,1,0:T(8,128)(2,1)}, bf16[1,8,768,384]{3,2,1,0:T(8,128)(2,1)}) fusion(bf16[2,8,768,384]{3,2,1,0:T(8,128)(2,1)} %param.22), kind=kLoop, calls=%fused_computation.527 | loop fusion | bytes 18874368 | tf_op jit(solution)/shard_map/slice | solution.py:378
  22.0 8.2 fusion.236
  34.6 8.6 %collective-permute-done.12 = bf16[48,3840]{1,0:T(8,128)(2,1)S(1)} collective-permute-done((bf16[48,3840]{1,0:T(8,128)(2,1)S(1)}, bf16[48,3840]{1,0:T(8,128)(2,1)S(1)}, u32[]{:S(2)}, u32[]{:S(2)}) %collective-permute-start.12) | collective-permute-done | bytes 368672 | tf_op jit(solution)/shard_map/ppermute | solution.py:45
  48.9 7.7 collective-permute-done.26
  90.0 10.9 %collective-permute-done.6 = bf16[384,768]{1,0:T(8,128)(2,1)} collective-permute-done((bf16[384,768]{1,0:T(8,128)(2,1)}, bf16[384,768]{1,0:T(8,128)(2,1)}, u32[]{:S(2)}, u32[]{:S(2)}) %collective-permute-start.6) | collective-permute-done | bytes 589856 | tf_op jit(solution)/shard_map/ppermute | solution.py:45
  108.1 8.5 %maximum_select_fusion = bf16[1536,1024]{1,0:T(8,128)(2,1)S(1)} fusion(bf16[768,1024]{1,0:T(8,128)(2,1)S(1)} %maximum_select_fusion.4, bf16[768,128]{1,0:T(8,128)(2,1)S(1)} %get-tuple-element.177, bf16[768,128]{1,0:T(8,128)(2,1)S(1)} %copy-done.59, bf16[768,768]{1,0:T(8,128)(2,1)S(1)} %get-tuple-element.140, pred[]{:T(512)S(6)} %eq.38), kind=kLoop, calls=%fused_computation.30 | loop fusion | flops 26738688 | bytes 6291457 | tf_op jit(solution)/shard_map/jit(_where)/select_n | solution.py:57
  116.7 6.8 collective-permute-done.2
  143.8 9.1 %collective-permute-done.8 = bf16[128,1536]{1,0:T(8,128)(2,1)S(1)} collective-permute-done((bf16[128,1536]{1,0:T(8,128)(2,1)S(1)}, bf16[128,1536]{1,0:T(8,128)(2,1)S(1)}, u32[]{:S(2)}, u32[]{:S(2)}) %collective-permute-start.8) | collective-permute-done | bytes 393248 | tf_op jit(solution)/shard_map/ppermute | solution.py:41
  158.7 7.0 collective-permute-done.20
  166.6 7.3 collective-permute-done.10
  178.4 7.7 fusion.6
  189.7 5.0 fusion.248
  207.0 7.2 collective-permute-done.14
  218.3 8.5 %maximum_select_fusion.1 = bf16[1536,1024]{1,0:T(8,128)(2,1)S(1)} fusion(bf16[768,1024]{1,0:T(8,128)(2,1)S(1)} %maximum_select_fusion.5, bf16[768,128]{1,0:T(8,128)(2,1)S(1)} %copy-done.55, bf16[768,128]{1,0:T(8,128)(2,1)S(1)} %copy-done.57, bf16[768,768]{1,0:T(8,128)(2,1)S(1)} %copy-done.15, pred[]{:T(512)S(6)} %eq.38), kind=kLoop, calls=%fused_computation.36 | loop fusion | flops 26738688 | bytes 6291457 | tf_op jit(solution)/shard_map/jit(_where)/select_n | solution.py:57
  249.0 6.7 collective-permute-done.22
  272.2 7.8 collective-permute-done.24
  283.5 9.2 %fusion.2 = f32[512,3072]{1,0:T(8,128)S(1)} fusion(bf16[512,1536]{1,0:T(8,128)(2,1)} %pad_maximum_fusion.9, bf16[1536,4608]{1,0:T(8,128)(2,1)} %all-gather.5.cloned.1.call-done), kind=kOutput, calls=%fused_computation.4 | convolution fusion | flops 4831838208 | bytes 17301504 | tf_op jit(solution)/shard_map/dot_general | solution.py:29
  295.4 8.3 multiply_multiply_fusion.1
  322.7 9.5 %fusion.249 = (bf16[512,1536]{1,0:T(8,128)(2,1)S(1)}, f32[512,1536]{1,0:T(8,128)S(1)}) fusion(f32[512,1536]{1,0:T(8,128)S(1)} %fusion.159, bf16[1536,4608]{1,0:T(8,128)(2,1)} %all-gather.5.cloned.1.call-done, bf16[512,1536]{1,0:T(8,128)(2,1)S(1)} %get-tuple-element.114, bf16[512,1536]{1,0:T(8,128)(2,1)S(1)} %get-tuple-element.113), kind=kOutput, calls=%fused_computation.542 | convolution fusion | flops 4839702528 | bytes 20447232 | tf_op jit(solution)/shard_map/dot_general | solution.py:33
  337.5 6.6 fusion.250
  387.9 10.2 %collective-permute-done.40 = bf16[128,1536]{1,0:T(8,128)(2,1)S(1)} collective-permute-done((bf16[128,1536]{1,0:T(8,128)(2,1)S(1)}, bf16[128,1536]{1,0:T(8,128)(2,1)S(1)}, u32[]{:S(2)}, u32[]{:S(2)}) %collective-permute-start.40) | collective-permute-done | bytes 393248 | tf_op jit(solution)/shard_map/ppermute | solution.py:41
  410.5 5.2 collective-permute-done.42
  418.9 9.3 %multiply_convert_fusion.2 = (bf16[512,1536]{1,0:T(8,128)(2,1)}, bf16[512,1536]{1,0:T(8,128)(2,1)}, f32[512,1536]{1,0:T(8,128)}) fusion(f32[512,3072]{1,0:T(8,128)} %copy-done.23, f32[512,384]{1,0:T(8,128)S(1)} %copy-done.52, f32[512,384]{1,0:T(8,128)S(1)} %copy-done.50, f32[512,384]{1,0:T(8,128)S(1)} %copy-done.48, f32[512,384]{1,0:T(8,128)S(1)} %copy-done.46, ...), kind=kOutput, calls=%fused_computation.49 | convolution fusion | flops 2437152768 | bytes 22020096 | tf_op jit(solution)/shard_map/dot_general | solution.py:33
  436.0 8.0 fusion.251
  453.7 5.5 collective-permute-done.45
  463.1 8.0 collective-permute-done.47
  508.3 11.4 %pad_maximum_fusion.1 = bf16[768,9216]{1,0:T(8,128)(2,1)} fusion(bf16[768,1536]{1,0:T(8,128)(2,1)S(1)} %convolution_convert_fusion.4, bf16[768,1536]{1,0:T(8,128)(2,1)S(1)} %convolution_convert_fusion.5, bf16[768,3072]{1,0:T(8,128)(2,1)S(1)} %convolution_convert_fusion, bf16[768,3072]{1,0:T(8,128)(2,1)S(1)} %convolution_convert_fusion.1), kind=kLoop, calls=%fused_computation.1 | loop fusion | flops 56623104 | bytes 28311552 | tf_op jit(solution)/shard_map/concatenate | solution.py:74
  533.2 11.4 %pad_maximum_fusion = bf16[768,9216]{1,0:T(8,128)(2,1)} fusion(bf16[768,1536]{1,0:T(8,128)(2,1)S(1)} %convolution_convert_fusion.6, bf16[768,1536]{1,0:T(8,128)(2,1)S(1)} %convolution_convert_fusion.7, bf16[768,3072]{1,0:T(8,128)(2,1)S(1)} %convolution_convert_fusion.2, bf16[768,3072]{1,0:T(8,128)(2,1)S(1)} %convolution_convert_fusion.3), kind=kLoop, calls=%fused_computation | loop fusion | flops 56623104 | bytes 28311552 | tf_op jit(solution)/shard_map/concatenate | solution.py:74
  553.4 5.3 collective-permute-done.49
  560.1 5.8 concatenate.411
  622.1 72.4 %reduce-scatter.11.cloned.1.call-done = bf16[24,9216]{1,0:T(8,128)(2,1)} async-done(((bf16[768,9216]{1,0:T(8,128)(2,1)}), bf16[24,9216]{1,0:T(8,128)(2,1)}) %reduce-scatter.11.cloned.1.call-update) | async-done | bytes 442384 | tf_op jit(solution)/shard_map/reduce_scatter | solution.py:303
  710.3 96.2 %reduce-scatter.9.cloned.1.call-done = bf16[24,9216]{1,0:T(8,128)(2,1)} async-done(((bf16[768,9216]{1,0:T(8,128)(2,1)}), bf16[24,9216]{1,0:T(8,128)(2,1)}) %reduce-scatter.9.cloned.1.call-update) | async-done | bytes 442384 | tf_op jit(solution)/shard_map/reduce_scatter | solution.py:303
  (808 shorter events, 412.6 us)
Async XLA Ops:
  7.2 171.2 %all-gather.3.cloned.1.call-start = ((), (), s32[]{:S(2)}) async-start(), calls=%async_computation.4 | async-start | bytes 14598144 | tf_op jit(solution)/shard_map/all_gather | solution.py:175
  44.2 239.4 %all-gather.5.cloned.1.call-start = ((), (), s32[]{:S(2)}) async-start(), calls=%async_computation.5 | async-start | bytes 14598144 | tf_op jit(solution)/shard_map/all_gather | solution.py:175
  57.5 544.3 %reduce-scatter.7.cloned.1.call-start = ((), (), s32[]{:S(2)}) async-start(), calls=%async_computation.7 | async-start | bytes 5677056 | tf_op jit(solution)/shard_map/reduce_scatter | solution.py:303
  60.9 40.0 %collective-permute-start.3 = (bf16[384,1024]{1,0:T(8,128)(2,1)}, bf16[384,1024]{1,0:T(8,128)(2,1)}, u32[]{:S(2)}, u32[]{:S(2)}) collective-permute-start(bf16[384,1024]{1,0:T(8,128)(2,1)} %fusion.59), channel_id=1, source_target_pairs={{0,1},{1,0},{2,3},{3,2},{4,5},{5,4},{6,7},{7,6},{8,9},{9,8},{10,11... | collective-permute-start | bytes 2359304 | tf_op jit(solution)/shard_map/ppermute | solution.py:45
  65.8 24.0 %collective-permute-start = (bf16[128,768]{1,0:T(8,128)(2,1)}, bf16[128,768]{1,0:T(8,128)(2,1)S(1)}, u32[]{:S(2)}, u32[]{:S(2)}) collective-permute-start(bf16[128,768]{1,0:T(8,128)(2,1)} %get-tuple-element.180), channel_id=1, source_target_pairs={{0,1},{1,0},{2,3},{3,2},{4,5},{5,4},{6,7},{7,6},{8,9},{9,8},{10,11... | collective-permute-start | bytes 589832 | tf_op jit(solution)/shard_map/ppermute | solution.py:45
  66.2 22.0 %collective-permute-start.1 = (bf16[20,768]{1,0:T(8,128)(2,1)S(1)}, bf16[20,768]{1,0:T(8,128)(2,1)}, u32[]{:S(2)}, u32[]{:S(2)}) collective-permute-start(bf16[20,768]{1,0:T(8,128)(2,1)S(1)} %pad_maximum_fusion.49), channel_id=1, source_target_pairs={{0,1},{1,0},{2,3},{3,2},{4,5},{5,4},{6,7},{7,6},{8,9},{9,8},{10,11... | collective-permute-start | bytes 92168 | tf_op jit(solution)/shard_map/ppermute | solution.py:45
  73.9 26.9 %collective-permute-start.6 = (bf16[384,768]{1,0:T(8,128)(2,1)}, bf16[384,768]{1,0:T(8,128)(2,1)}, u32[]{:S(2)}, u32[]{:S(2)}) collective-permute-start(bf16[384,768]{1,0:T(8,128)(2,1)} %dynamic-slice_bitcast_fusion.1), channel_id=1, source_target_pairs={{0,1},{1,0},{2,3},{3,2},{4,5},{5,4},{6,7},{7,6},{8,9},{9,8},{10,11... | collective-permute-start | bytes 1769480 | tf_op jit(solution)/shard_map/ppermute | solution.py:45
  75.3 90.8 %collective-permute-start.17 = (bf16[384,1024]{1,0:T(8,128)(2,1)}, bf16[384,1024]{1,0:T(8,128)(2,1)}, u32[]{:S(2)}, u32[]{:S(2)}) collective-permute-start(bf16[384,1024]{1,0:T(8,128)(2,1)} %fusion.57), channel_id=1, source_target_pairs={{0,1},{1,0},{2,3},{3,2},{4,5},{5,4},{6,7},{7,6},{8,9},{9,8},{10,11... | collective-permute-start | bytes 2359304 | tf_op jit(solution)/shard_map/ppermute | solution.py:45
  101.5 22.0 %collective-permute-start.2 = (bf16[128,1536]{1,0:T(8,128)(2,1)S(1)}, bf16[128,1536]{1,0:T(8,128)(2,1)S(1)}, u32[]{:S(2)}, u32[]{:S(2)}) collective-permute-start(bf16[128,1536]{1,0:T(8,128)(2,1)S(1)} %fusion.62), channel_id=1, source_target_pairs={{0,2},{2,0},{1,3},{3,1},{4,6},{6,4},{5,7},{7,5},{8,10},{10,8},{9,1... | collective-permute-start | bytes 1179656 | tf_op jit(solution)/shard_map/ppermute | solution.py:41
  142.3 23.4 %collective-permute-start.20 = (bf16[384,768]{1,0:T(8,128)(2,1)S(1)}, bf16[384,768]{1,0:T(8,128)(2,1)}, u32[]{:S(2)}, u32[]{:S(2)}) collective-permute-start(bf16[384,768]{1,0:T(8,128)(2,1)S(1)} %dynamic-slice_bitcast_fusion), channel_id=1, source_target_pairs={{0,1},{1,0},{2,3},{3,2},{4,5},{5,4},{6,7},{7,6},{8,9},{9,8},{10,11... | collective-permute-start | bytes 1769480 | tf_op jit(solution)/shard_map/ppermute | solution.py:45
  154.5 19.4 %collective-permute-start.10 = (bf16[128,1536]{1,0:T(8,128)(2,1)S(1)}, bf16[128,1536]{1,0:T(8,128)(2,1)S(1)}, u32[]{:S(2)}, u32[]{:S(2)}) collective-permute-start(bf16[128,1536]{1,0:T(8,128)(2,1)S(1)} %multiply_convert_fusion.8), channel_id=1, source_target_pairs={{0,1},{1,0},{2,3},{3,2},{4,5},{5,4},{6,7},{7,6},{8,9},{9,8},{10,11... | collective-permute-start | bytes 1179656 | tf_op jit(solution)/shard_map/ppermute | solution.py:45
  156.5 20.7 %collective-permute-start.11 = (bf16[128,1536]{1,0:T(8,128)(2,1)S(1)}, bf16[128,1536]{1,0:T(8,128)(2,1)S(1)}, u32[]{:S(2)}, u32[]{:S(2)}) collective-permute-start(bf16[128,1536]{1,0:T(8,128)(2,1)S(1)} %multiply_convert_fusion.8), channel_id=1, source_target_pairs={{0,3},{1,2},{2,1},{3,0},{4,7},{5,6},{6,5},{7,4},{8,11},{9,10},{10,... | collective-permute-start | bytes 1179656 | tf_op jit(solution)/shard_map/ppermute | solution.py:49
  158.7 18.9 %collective-permute-start.9 = (bf16[128,1536]{1,0:T(8,128)(2,1)S(1)}, bf16[128,1536]{1,0:T(8,128)(2,1)S(1)}, u32[]{:S(2)}, u32[]{:S(2)}) collective-permute-start(bf16[128,1536]{1,0:T(8,128)(2,1)S(1)} %multiply_convert_fusion.8), channel_id=1, source_target_pairs={{0,2},{2,0},{1,3},{3,1},{4,6},{6,4},{5,7},{7,5},{8,10},{10,8},{9,1... | collective-permute-start | bytes 1179656 | tf_op jit(solution)/shard_map/ppermute | solution.py:41
  165.7 34.0 %collective-permute-start.21 = (bf16[384,768]{1,0:T(8,128)(2,1)}, bf16[384,768]{1,0:T(8,128)(2,1)}, u32[]{:S(2)}, u32[]{:S(2)}) collective-permute-start(bf16[384,768]{1,0:T(8,128)(2,1)} %collective-permute-done.20), channel_id=1, source_target_pairs={{0,4},{4,0},{8,12},{12,8},{16,20},{20,16},{24,28},{28,24},{32,36},... | collective-permute-start | bytes 1769480 | tf_op jit(solution)/shard_map/ppermute | solution.py:53
  166.1 36.5 %collective-permute-start.18 = (bf16[384,1024]{1,0:T(8,128)(2,1)}, bf16[384,1024]{1,0:T(8,128)(2,1)}, u32[]{:S(2)}, u32[]{:S(2)}) collective-permute-start(bf16[384,1024]{1,0:T(8,128)(2,1)} %collective-permute-done.17), channel_id=1, source_target_pairs={{0,4},{4,0},{8,12},{12,8},{16,20},{20,16},{24,28},{28,24},{32,36},... | collective-permute-start | bytes 2359304 | tf_op jit(solution)/shard_map/ppermute | solution.py:53
  196.6 17.7 %collective-permute-start.14 = (bf16[128,1536]{1,0:T(8,128)(2,1)S(1)}, bf16[128,1536]{1,0:T(8,128)(2,1)S(1)}, u32[]{:S(2)}, u32[]{:S(2)}) collective-permute-start(bf16[128,1536]{1,0:T(8,128)(2,1)S(1)} %get-tuple-element.152), channel_id=1, source_target_pairs={{0,1},{1,0},{2,3},{3,2},{4,5},{5,4},{6,7},{7,6},{8,9},{9,8},{10,11... | collective-permute-start | bytes 1179656 | tf_op jit(solution)/shard_map/ppermute | solution.py:45
  197.9 18.9 %collective-permute-start.15 = (bf16[128,1536]{1,0:T(8,128)(2,1)S(1)}, bf16[128,1536]{1,0:T(8,128)(2,1)S(1)}, u32[]{:S(2)}, u32[]{:S(2)}) collective-permute-start(bf16[128,1536]{1,0:T(8,128)(2,1)S(1)} %get-tuple-element.151), channel_id=1, source_target_pairs={{0,3},{1,2},{2,1},{3,0},{4,7},{5,6},{6,5},{7,4},{8,11},{9,10},{10,... | collective-permute-start | bytes 1179656 | tf_op jit(solution)/shard_map/ppermute | solution.py:49
  247.7 15.5 %collective-permute-start.31 = (bf16[128,768]{1,0:T(8,128)(2,1)S(1)}, bf16[128,768]{1,0:T(8,128)(2,1)S(1)}, u32[]{:S(2)}, u32[]{:S(2)}) collective-permute-start(bf16[128,768]{1,0:T(8,128)(2,1)S(1)} %get-tuple-element.175), channel_id=1, source_target_pairs={{0,1},{1,0},{2,3},{3,2},{4,5},{5,4},{6,7},{7,6},{8,9},{9,8},{10,11... | collective-permute-start | bytes 589832 | tf_op jit(solution)/shard_map/ppermute | solution.py:45
  259.9 20.1 %collective-permute-start.24 = (bf16[128,1536]{1,0:T(8,128)(2,1)}, bf16[128,1536]{1,0:T(8,128)(2,1)}, u32[]{:S(2)}, u32[]{:S(2)}) collective-permute-start(bf16[128,1536]{1,0:T(8,128)(2,1)} %multiply_convert_fusion.6), channel_id=1, source_target_pairs={{0,1},{1,0},{2,3},{3,2},{4,5},{5,4},{6,7},{7,6},{8,9},{9,8},{10,11... | collective-permute-start | bytes 1179656 | tf_op jit(solution)/shard_map/ppermute | solution.py:45
  261.1 19.8 %collective-permute-start.25 = (bf16[128,1536]{1,0:T(8,128)(2,1)}, bf16[128,1536]{1,0:T(8,128)(2,1)}, u32[]{:S(2)}, u32[]{:S(2)}) collective-permute-start(bf16[128,1536]{1,0:T(8,128)(2,1)} %multiply_convert_fusion.6), channel_id=1, source_target_pairs={{0,3},{1,2},{2,1},{3,0},{4,7},{5,6},{6,5},{7,4},{8,11},{9,10},{10,... | collective-permute-start | bytes 1179656 | tf_op jit(solution)/shard_map/ppermute | solution.py:49
  264.1 31.3 %collective-permute-start.32 = (bf16[128,1536]{1,0:T(8,128)(2,1)}, bf16[128,1536]{1,0:T(8,128)(2,1)}, u32[]{:S(2)}, u32[]{:S(2)}) collective-permute-start(bf16[128,1536]{1,0:T(8,128)(2,1)} %maximum_select_fusion.14), channel_id=1, source_target_pairs={{0,2},{2,0},{1,3},{3,1},{4,6},{6,4},{5,7},{7,5},{8,10},{10,8},{9,1... | collective-permute-start | bytes 1179656 | tf_op jit(solution)/shard_map/ppermute | solution.py:41
  264.9 30.5 %collective-permute-start.33 = (bf16[128,1536]{1,0:T(8,128)(2,1)}, bf16[128,1536]{1,0:T(8,128)(2,1)}, u32[]{:S(2)}, u32[]{:S(2)}) collective-permute-start(bf16[128,1536]{1,0:T(8,128)(2,1)} %maximum_select_fusion.14), channel_id=1, source_target_pairs={{0,1},{1,0},{2,3},{3,2},{4,5},{5,4},{6,7},{7,6},{8,9},{9,8},{10,11... | collective-permute-start | bytes 1179656 | tf_op jit(solution)/shard_map/ppermute | solution.py:45
  270.3 25.1 %collective-permute-start.34 = (bf16[128,1536]{1,0:T(8,128)(2,1)}, bf16[128,1536]{1,0:T(8,128)(2,1)}, u32[]{:S(2)}, u32[]{:S(2)}) collective-permute-start(bf16[128,1536]{1,0:T(8,128)(2,1)} %maximum_select_fusion.14), channel_id=1, source_target_pairs={{0,3},{1,2},{2,1},{3,0},{4,7},{5,6},{6,5},{7,4},{8,11},{9,10},{10,... | collective-permute-start | bytes 1179656 | tf_op jit(solution)/shard_map/ppermute | solution.py:49
  355.2 43.7 %collective-permute-start.27 = (bf16[128,1536]{1,0:T(8,128)(2,1)}, bf16[128,1536]{1,0:T(8,128)(2,1)}, u32[]{:S(2)}, u32[]{:S(2)}) collective-permute-start(bf16[128,1536]{1,0:T(8,128)(2,1)} %get-tuple-element.147), channel_id=1, source_target_pairs={{0,2},{2,0},{1,3},{3,1},{4,6},{6,4},{5,7},{7,5},{8,10},{10,8},{9,1... | collective-permute-start | bytes 1179656 | tf_op jit(solution)/shard_map/ppermute | solution.py:41
  357.2 41.7 %collective-permute-start.28 = (bf16[128,1536]{1,0:T(8,128)(2,1)}, bf16[128,1536]{1,0:T(8,128)(2,1)}, u32[]{:S(2)}, u32[]{:S(2)}) collective-permute-start(bf16[128,1536]{1,0:T(8,128)(2,1)} %get-tuple-element.149), channel_id=1, source_target_pairs={{0,1},{1,0},{2,3},{3,2},{4,5},{5,4},{6,7},{7,6},{8,9},{9,8},{10,11... | collective-permute-start | bytes 1179656 | tf_op jit(solution)/shard_map/ppermute | solution.py:45
  358.1 40.8 %collective-permute-start.29 = (bf16[128,1536]{1,0:T(8,128)(2,1)}, bf16[128,1536]{1,0:T(8,128)(2,1)}, u32[]{:S(2)}, u32[]{:S(2)}) collective-permute-start(bf16[128,1536]{1,0:T(8,128)(2,1)} %get-tuple-element.148), channel_id=1, source_target_pairs={{0,3},{1,2},{2,1},{3,0},{4,7},{5,6},{6,5},{7,4},{8,11},{9,10},{10,... | collective-permute-start | bytes 1179656 | tf_op jit(solution)/shard_map/ppermute | solution.py:49
  409.9 202.6 %reduce-scatter.5.cloned.1.call-start = ((), (), s32[]{:S(2)}) async-start(), calls=%async_computation.6 | async-start | bytes 5677056 | tf_op jit(solution)/shard_map/reduce_scatter | solution.py:303
  495.1 199.4 %reduce-scatter.11.cloned.1.call-start = ((), (), s32[]{:S(2)}) async-start(), calls=%async_computation.9 | async-start | bytes 14598144 | tf_op jit(solution)/shard_map/reduce_scatter | solution.py:303
  519.7 286.8 %reduce-scatter.9.cloned.1.call-start = ((), (), s32[]{:S(2)}) async-start(), calls=%async_computation.8 | async-start | bytes 14598144 | tf_op jit(solution)/shard_map/reduce_scatter | solution.py:303
  570.6 20.0 %collective-permute-start.30 = (bf16[128,768]{1,0:T(8,128)(2,1)}, bf16[128,768]{1,0:T(8,128)(2,1)}, u32[]{:S(2)}, u32[]{:S(2)}) collective-permute-start(bf16[128,768]{1,0:T(8,128)(2,1)} %get-tuple-element.173), channel_id=1, source_target_pairs={{0,1},{1,0},{2,3},{3,2},{4,5},{5,4},{6,7},{7,6},{8,9},{9,8},{10,11... | collective-permute-start | bytes 589832 | tf_op jit(solution)/shard_map/ppermute | solution.py:45
  580.4 17.8 %collective-permute-start.50 = (bf16[128,768]{1,0:T(8,128)(2,1)S(1)}, bf16[128,768]{1,0:T(8,128)(2,1)S(1)}, u32[]{:S(2)}, u32[]{:S(2)}) collective-permute-start(bf16[128,768]{1,0:T(8,128)(2,1)S(1)} %get-tuple-element.171), channel_id=1, source_target_pairs={{0,1},{1,0},{2,3},{3,2},{4,5},{5,4},{6,7},{7,6},{8,9},{9,8},{10,11... | collective-permute-start | bytes 589832 | tf_op jit(solution)/shard_map/ppermute | solution.py:45
  706.9 104.7 %collective-permute-start.69 = (bf16[4,12,768]{2,1,0:T(8,128)(2,1)S(1)}, bf16[4,12,768]{2,1,0:T(8,128)(2,1)S(1)}, u32[]{:S(2)}, u32[]{:S(2)}) collective-permute-start(bf16[4,12,768]{2,1,0:T(8,128)(2,1)S(1)} %get-tuple-element.195), channel_id=1, source_target_pairs={{0,1},{1,0},{2,3},{3,2},{4,5},{5,4},{6,7},{7,6},{8,9},{9,8},{10,11... | collective-permute-start | bytes 221192 | tf_op jit(solution)/shard_map/ppermute | solution.py:45
  (229 other events, 1972.4 us)
Sparse Core Ops, SparseCore 0:
  44.3 68.9 all-gather.2
  116.1 66.0 all-gather.4
  410.0 84.7 reduce-scatter.6
  498.4 84.4 reduce-scatter.4
  586.6 107.8 reduce-scatter.10
  698.7 107.7 reduce-scatter.8

commit v2 on v1

--- a/solution.py
+++ b/solution.py
@@ -70,42 +70,50 @@
     return [x[:, :HALF], x[:, HALF:]]
 
 
+def turned(x):
+    return jnp.concatenate([x[:, HALF:], x[:, :HALF]], axis=1)
+
+
+def after(value, *earlier):
+    return lax.optimization_barrier((value, *earlier))[0]
+
+
 def pack(parts):
     return jnp.concatenate([x.astype(BF16) for x in parts], axis=1)
 
 
 def to_quarter(block, column):
     own = half_of(block, column, 0)
-    other = over_col(half_of(block, 1 - column, 0))
-    return by_col(column, own, other, 1)
+    return jnp.concatenate([own, over_col(half_of(block, 1 - column, 0))], axis=1)
 
 
 def from_quarter(block, column):
-    own = half_of(block, column, 1)
-    other = over_col(half_of(block, 1 - column, 1))
-    return by_col(column, own, other, 0)
+    own, other = halves(block)
+    return by_col(column, own, over_col(other), 0)
 
 
 def gather_four(x):
-    return jnp.concatenate([x, over_row(x), over_col(x), over_both(x)], axis=0)
+    other = turned(x)
+    return jnp.concatenate([x, over_row(x), over_col(other), over_both(other)], axis=0)
 
 
 def scatter_four(x):
-    own, row, col, both = [x[i * QUARTER : (i + 1) * QUARTER] for i in range(4)]
-    return (
-        own
-        + over_row(row.astype(BF16)).astype(F32)
-        + over_col(col.astype(BF16)).astype(F32)
-        + over_both(both.astype(BF16)).astype(F32)
-    )
+    row, col, both = [x[i * QUARTER : (i + 1) * QUARTER].astype(BF16) for i in range(1, 4)]
+    return (x[:QUARTER], over_row(row), over_col(turned(col)), over_both(turned(both)))
+
+
+def total(parts):
+    return sum(x.astype(F32) for x in parts)
 
 
 def gather_two(x):
     return jnp.concatenate([x, over_row(x)], axis=0)
 
 
-def scatter_two(x):
-    return x[:QUARTER] + over_row(x[QUARTER:].astype(BF16)).astype(F32)
+def scatter_two(parts):
+    own = jnp.concatenate([x[:QUARTER] for x in parts], axis=1)
+    peer = jnp.concatenate([x[QUARTER:].astype(BF16) for x in parts], axis=1)
+    return (own, over_row(peer))
 
 
 def segments(seq_lengths, seq_owner, data_index):
@@ -152,35 +160,34 @@
     )
 
 
-def expert_weights(gate, up, down, column, data_index):
+def expert_weights(layer, gate, up, down, column, data_index):
     rows = 48
     start = (data_index % 16) * rows
 
     def piece(weight, side):
-        cut = lax.dynamic_slice(weight, (MINE * side, start, 0), (MINE, rows, FF))
-        return cut.transpose(1, 0, 2).reshape(rows, MINE * FF)
+        cut = lax.dynamic_slice(weight, (layer, MINE * side, start, 0), (1, MINE, rows, FF))
+        return [cut[0, e] for e in range(MINE)]
 
     def down_piece(side):
-        place = (MINE * side + data_index // 8, (data_index % 8) * rows, 0)
-        return lax.dynamic_slice(down, place, (1, rows, HALF))[0]
-
-    def pack(side):
-        return jnp.concatenate([piece(gate, side), piece(up, side), down_piece(side)], axis=1)
-
-    other = over_col(pack(1 - column))
-    own = pack(column)
-    mine = data_index // 16 == column
-    gate_up = jnp.where(mine, own[:, : 2 * D], other[:, : 2 * D])
-    downs = by_col(column, own[:, 2 * D :], other[:, 2 * D :], 1)
-    whole = lax.all_gather(jnp.concatenate([gate_up, downs], axis=1), "dp", axis=0, tiled=True)
-    return (whole[:, : 2 * D], whole[:, 2 * D :])
+        place = (layer, MINE * side + data_index // 8, (data_index % 8) * rows, 0)
+        return lax.dynamic_slice(down, place, (1, 1, rows, HALF))[0, 0]
+
+    def packed(side):
+        return jnp.concatenate(piece(gate, side) + piece(up, side) + [down_piece(side)], axis=1)
+
+    other = over_col(packed(1 - column))
+    own = packed(column)
+    gate_up = jnp.where(data_index < 16, own[:, : 2 * D], other[:, : 2 * D])
+    piece_all = jnp.concatenate([gate_up, own[:, 2 * D :], other[:, 2 * D :]], axis=1)
+    whole = lax.all_gather(piece_all, "dp", axis=0, tiled=True)
+    return (other, (whole[:, : 2 * D], whole[:, 2 * D :]))
 
 
 def attention_forward(stream, gain, qkv_weight, out_weight, geometry):
     cosine, sine, seen_mask, row_valid = geometry
     inv_rms, normed = normalize(stream, gain)
     inputs = gather_two(normed)
-    qkv = dot(inputs, qkv_weight)
+    qkv = sum(dot(x, w) for x, w in zip(halves(inputs), qkv_weight))
     rows = inputs.shape[0]
     width = Q_HEADS * HEAD
     key_rot = rotate(qkv[:, width : width + HEAD], cosine, sine).astype(BF16)
@@ -199,9 +206,9 @@
     probabilities = (exponent / denominator).astype(BF16).reshape(Q_HEADS * rows, TOK_DP)
     attended = dot(probabilities, values).reshape(Q_HEADS, rows, HEAD)
     attended = attended.transpose(1, 0, 2).reshape(rows, width).astype(BF16)
-    branch = scatter_two(dot(attended, out_weight))
+    branch = total(scatter_two([dot(attended, w) for w in out_weight]))
     cache = (stream, inv_rms, inputs, query_rot, keys, values, log_total, attended)
-    return (cache, stream + branch)
+    return (cache, stream + branch, pair)
 
 
 def attention_backward(upstream, cache, gain, qkv_weight, out_weight, geometry):
@@ -210,7 +217,7 @@
     rows = inputs.shape[0]
     width = Q_HEADS * HEAD
     out_grad = gather_two(upstream.astype(BF16))
-    attended_grad = dot_across(out_grad, out_weight).astype(BF16)
+    attended_grad = sum(dot_across(x, w) for x, w in zip(halves(out_grad), out_weight)).astype(BF16)
     attended_grad = (
         attended_grad.reshape(rows, Q_HEADS, HEAD).transpose(1, 0, 2).reshape(Q_HEADS * rows, HEAD)
     )
@@ -230,11 +237,13 @@
     query_grad = query_grad.transpose(1, 0, 2).reshape(rows, width)
     key_grad = rotate(pair[:, :HEAD], cosine, -sine)
     qkv_grad = jnp.concatenate([query_grad, key_grad, pair[:, HEAD:]], axis=1).astype(BF16)
-    normed_grad = scatter_two(dot_across(qkv_grad, qkv_weight))
+    parts = scatter_two([dot_across(qkv_grad, w) for w in qkv_weight])
     packed = pack(
         [dot_down(x, qkv_grad) for x in halves(inputs)]
         + [dot_down(attended, x) for x in halves(out_grad)]
     )
+    packed, *parts = lax.optimization_barrier((packed, *parts))
+    normed_grad = total(parts)
     grad_stream, grad_gain = norm_back(upstream, normed_grad, stream, inv_rms, gain)
     return (grad_stream, packed, grad_gain)
 
@@ -257,7 +266,7 @@
     gate_up = dot(inputs, gate_up_weight)
     gate_value, up_value = gate_up[:, :D], gate_up[:, D:]
     hidden = (spread(mine) * jax.nn.silu(gate_value) * up_value).astype(BF16)
-    branch = scatter_four(dot(hidden, down_weight))
+    branch = total(scatter_four(dot(hidden, down_weight)))
     cache = (stream, inv_rms, inputs, gate_up, share, mine, hidden)
     return (cache, stream + branch)
 
@@ -268,15 +277,23 @@
     return jnp.concatenate([high, low], axis=1)
 
 
-def expert_backward(upstream, cache, gain, router, gate_up_weight, down_weight, column):
+def expert_backward(
+    upstream, cache, gain, router, gate_up_weight, down_weight, column, gathered=None
+):
     stream, inv_rms, inputs, gate_up, share, mine, hidden = cache
     gate_value, up_value = gate_up[:, :D], gate_up[:, D:]
-    rows = inputs.shape[0]
-    out_grad = gather_four(upstream.astype(BF16))
+    out_grad = gather_four(upstream.astype(BF16)) if gathered is None else gathered
     hidden_grad = dot_across(out_grad, down_weight)
     sigmoid_gate = jax.nn.sigmoid(gate_value)
     silu_gate = gate_value * sigmoid_gate
-    share_grad = jnp.sum((hidden_grad * silu_gate * up_value).reshape(rows, MINE, FF), axis=2)
+    weighed = hidden_grad * silu_gate * up_value
+    share_grad = jnp.concatenate(
+        [
+            jnp.sum(weighed[:, e * FF : (e + 1) * FF], axis=1, keepdims=True)
+            for e in range(MINE)
+        ],
+        axis=1,
+    )
     activation_grad = hidden_grad * spread(mine)
     gate_grad = (
         activation_grad * up_value * sigmoid_gate * (1.0 + gate_value * (1.0 - sigmoid_gate))
@@ -288,11 +305,13 @@
     logits_low = split_low(logits_grad)
     input_grad = dot_across(gate_up_grad, gate_up_weight)
     input_grad = input_grad + dot_across(logits_low, jnp.concatenate([router, router], axis=1))
-    normed_grad = scatter_four(input_grad)
+    parts = scatter_four(input_grad)
     packed = pack(
         [dot_down(x, gate_up_grad) for x in halves(inputs)]
         + [dot_down(x, out_grad) for x in halves(hidden)]
     )
+    packed, *parts = lax.optimization_barrier((packed, *parts))
+    normed_grad = total(parts)
     router_grad = dot_down(logits_low, inputs)
     router_grad = router_grad[:EXPERTS] + router_grad[EXPERTS:]
     grad_stream, grad_gain = norm_back(upstream, normed_grad, stream, inv_rms, gain)
@@ -301,6 +320,33 @@
 
 def sum_over_dp(packed):
     return lax.psum_scatter(packed, "dp", scatter_dimension=0, tiled=True)
+
+
+def exchange(blocks, size, mine, target):
+    own = lax.dynamic_index_in_dim(blocks, mine, 0, keepdims=False).astype(F32)
+    for k in range(1, size):
+        block = lax.dynamic_index_in_dim(blocks, (mine + k) % size, 0, keepdims=False)
+        own = own + over_dp(block, lambda i, k=k: target(i, k)).astype(F32)
+    return own
+
+
+def sum_by_steps(packed, data_index):
+    along_x, along_z, core = data_index // 8, data_index // 2 % 4, data_index % 2
+
+    def x_step(blocks):
+        return exchange(blocks, 4, along_x, lambda i, k: (i // 8 + k) % 4 * 8 + i % 8)
+
+    def z_step(blocks):
+        return exchange(
+            blocks, 4, along_z, lambda i, k: i // 8 * 8 + (i // 2 % 4 + k) % 4 * 2 + i % 2
+        )
+
+    blocks = packed.reshape(4, 4, 2, 24, -1).transpose(2, 0, 1, 3, 4)
+    summed = exchange(blocks, 2, core, lambda i, k: i ^ 1).astype(BF16)
+    split = summed.shape[-1] // 2
+    former = x_step(summed[..., :split]).astype(BF16)
+    latter = z_step(summed[..., split:].transpose(1, 0, 2, 3)).astype(BF16)
+    return jnp.concatenate([z_step(former), x_step(latter)], axis=1).astype(BF16)
 
 
 def sum_everywhere(values):
@@ -310,23 +356,24 @@
     return values
 
 
-def swap_half(block, column, width):
-    own = lax.dynamic_slice_in_dim(block, column * width, width, axis=1)
-    other = over_col(lax.dynamic_slice_in_dim(block, (1 - column) * width, width, axis=1))
-    return (own, other)
-
-
-def place_attention(summed, column):
-    split = 2 * (Q_HEADS + 2) * HEAD
-    parts = (swap_half(summed[:, :split], column, split // 2), swap_half(summed[:, split:], column, HALF))
-    return [own.astype(F32) + other.astype(F32) for own, other in parts]
+def place_attention(summed):
+    split = (Q_HEADS + 2) * HEAD
+    ends = (0, split, 2 * split, 2 * split + HALF, 2 * split + 2 * HALF)
+    parts = [summed[:, a:b] for a, b in zip(ends[:-1], ends[1:])]
+    qkv = parts[0].astype(F32) + over_col(parts[1]).astype(F32)
+    return (qkv, parts[2].astype(F32) + over_col(parts[3]).astype(F32))
 
 
 def place_experts(summed, column, data_index):
-    own, other = swap_half(summed[:, : 4 * D], column, 2 * D)
+    own, other = summed[:, : 2 * D], over_col(summed[:, 2 * D : 4 * D])
 
     def unfold(block):
-        return block.reshape(24, 2, MINE, FF).transpose(1, 2, 0, 3)
+        return jnp.stack(
+            [
+                jnp.stack([block[:, (k * MINE + e) * FF : (k * MINE + e + 1) * FF] for e in range(MINE)])
+                for k in range(2)
+            ]
+        )
 
     gate_up = by_col(column, unfold(own), unfold(other), 1).astype(F32)
     down = summed[:, 4 * D :]
@@ -338,8 +385,7 @@
     odd = data_index % 2 == 1
     low, high = jnp.where(odd, latter, former), jnp.where(odd, former, latter)
     down = jnp.stack([low[:, :D], high[:, :D], low[:, D:], high[:, D:]])
-    down_other = over_col(half_of(down, 1 - column, 2))
-    down = by_col(column, half_of(down, column, 2), down_other, 0).astype(F32)
+    down = by_col(column, down[:, :, :HALF], over_col(down[:, :, HALF:]), 0).astype(F32)
     return (gate_up[0], gate_up[1], down)
 
 
@@ -363,24 +409,24 @@
     row = lax.axis_index("row")
     column = lax.axis_index("col")
     core = data_index % 2
+    expert_parts, attention_parts = [None] * LAYERS, [None] * LAYERS
+
+    def load_experts(i, where):
+        return expert_weights(i, gate_weight, up_weight, down_weight, column, where)
+
+    def load_attention(i, where):
+        own = jnp.concatenate([query_weight[i], key_weight[i], value_weight[i]], axis=1)
+        other = attention_weights(own, column, where)
+        out_other = attention_weights(output_weight[i], column, after(where, other))
+        return ((own, other), (output_weight[i], out_other))
+
+    first_piece, expert_parts[0] = load_experts(0, data_index)
     stream = to_quarter(tokens, column).astype(F32)
-    qkv_own = [
-        jnp.concatenate([query_weight[i], key_weight[i], value_weight[i]], axis=1)
-        for i in range(LAYERS)
-    ]
-    qkv_weights, out_weights, expert_parts = [None] * LAYERS, [None] * LAYERS, [None] * LAYERS
-    for i in range(LAYERS):
-        other = attention_weights(qkv_own[i], column, core)
-        qkv_weights[i] = by_col(column, qkv_own[i], other, 0)
-        other = attention_weights(output_weight[i], column, core)
-        out_weights[i] = by_col(column, output_weight[i], other, 1)
-        expert_parts[i] = expert_weights(
-            gate_weight[i], up_weight[i], down_weight[i], column, data_index
-        )
+    attention_parts[0] = load_attention(0, after(core, stream))
     gains = norm_gains.reshape(2 * LAYERS, HALF)
     router_own = router_weight.transpose(0, 2, 1).reshape(LAYERS * EXPERTS, HALF)
     small = jnp.concatenate([gains, router_own], axis=0)
-    small = by_col(column, small, over_col(small), 1)
+    small = jnp.concatenate([small, over_col(small)], axis=1)
     gains = small[: 2 * LAYERS].astype(F32).reshape(LAYERS, 2, D)
     routers = small[2 * LAYERS :].reshape(LAYERS, EXPERTS, D).transpose(0, 2, 1)
 
@@ -416,37 +462,59 @@
     geometry = (jnp.cos(angle), jnp.sin(angle), seen_mask[None], valid_row[:rows][None, :, None])
 
     caches = []
+    gathered = None
     for i in range(LAYERS):
-        attention_cache, stream = attention_forward(
-            stream, gains[i, 0], qkv_weights[i], out_weights[i], geometry
-        )
+        attention_cache, stream, pair = attention_forward(
+            stream, gains[i, 0], *attention_parts[i], geometry
+        )
+        if i == 0:
+            _, expert_parts[1] = load_experts(1, after(data_index, first_piece, pair))
+            attention_parts[1] = load_attention(1, after(core, pair))
         expert_cache, stream = expert_forward(
             stream, gains[i, 1], routers[i], *expert_parts[i], chosen_masks[i], column
         )
+        if i == 0:
+            upstream = to_quarter(after(cotangent, expert_cache[2]), column)
+            gathered = gather_four(upstream)
         caches.append((attention_cache, expert_cache))
     block_output = from_quarter(stream.astype(BF16), column)
-    upstream = to_quarter(cotangent, column).astype(F32)
+    upstream = upstream.astype(F32)
     attention_sums, expert_sums, smalls = [None] * LAYERS, [None] * LAYERS, [None] * LAYERS
+    waiting = None
     for i in reversed(range(LAYERS)):
         attention_cache, expert_cache = caches[i]
         upstream, packed, expert_gain, router_grad = expert_backward(
-            upstream, expert_cache, gains[i, 1], routers[i], *expert_parts[i], column
-        )
-        expert_sums[i] = sum_over_dp(packed)
+            upstream,
+            expert_cache,
+            gains[i, 1],
+            routers[i],
+            *expert_parts[i],
+            column,
+            gathered if i == LAYERS - 1 else None,
+        )
+        if waiting is None:
+            expert_sums[i] = sum_over_dp(packed)
+        else:
+            summed = sum_over_dp(pack([packed, waiting]))
+            expert_sums[i] = summed[:, : 6 * D]
+            attention_sums[i + 1] = summed[:, 6 * D :]
         upstream, packed, attention_gain = attention_backward(
-            upstream, attention_cache, gains[i, 0], qkv_weights[i], out_weights[i], geometry
-        )
-        attention_sums[i] = sum_over_dp(packed)
+            upstream, attention_cache, gains[i, 0], *attention_parts[i], geometry
+        )
+        if i > 0:
+            waiting = packed
+        else:
+            attention_sums[i] = sum_by_steps(packed, data_index)
         smalls[i] = jnp.concatenate([attention_gain[None], expert_gain[None], router_grad], axis=0)
     grad_tokens = from_quarter(upstream.astype(BF16), column)
 
     small = jnp.concatenate(smalls, axis=0)
-    small = half_of(small, column, 1) + over_col(half_of(small, 1 - column, 1))
+    small = small[:, :HALF] + over_col(small[:, HALF:])
     small = sum_everywhere(small).reshape(LAYERS, 2 + EXPERTS, HALF)
     grad_gains = small[:, :2]
     grad_router = small[:, 2:].transpose(0, 2, 1)
 
-    attention = [place_attention(x, column) for x in attention_sums]
+    attention = [place_attention(x) for x in attention_sums]
     qkv_grad, out_grad = [jnp.stack([x[k] for x in attention]) for k in range(2)]
     parts = [place_experts(x, column, data_index) for x in expert_sums]
     grad_gate, grad_up, grad_down = [jnp.stack([p[k] for p in parts]) for k in range(3)]

time: 847 us -> 718 us (0.85)
  waiting for transfers between devices: 364 us -> 223 us
  matrix products: 125 us -> 145 us
  local copies, waits for them, and re-layouts: 98.2 us -> 86.5 us
    reduce_scatter x4 -> x2, waiting for transfers between devices: 169 us -> 0.04 us  [sum_over_dp(): return lax.psum_scatter(packed, 'dp', scatter_dimension=0, tiled=True)]
    ppermute x8, waiting for transfers between devices: 14.1 us -> 51.2 us  [over_both(): return lax.ppermute(x, ('row', 'col'), DIAGONAL)]
    ppermute x32, waiting for transfers between devices: 103 us -> 79.2 us  [over_col(): return lax.ppermute(x, 'col', SWAP)]
    ppermute x13 -> x26, waiting for transfers between devices: 18.9 us -> 41.7 us  [over_dp(): return lax.ppermute(x, 'dp', [(i, target(i)) for i in range(N_DP)])]
    select_n x10 -> x4, other arithmetic: 21.6 us -> 1.72 us  [by_col(): jnp.where(column == 0, jnp.concatenate([own, other], axis=axis), jnp.conc...]
    slice x22 -> x41, local copies, waits for them, and re-layouts: 30 us -> 15.1 us  [the longest x2 3.28 us: scatter_four(): x[:QUARTER]]
    ppermute x13 -> x26, starting transfers between devices: 16.8 us -> 31.2 us  [over_dp(): return lax.ppermute(x, 'dp', [(i, target(i)) for i in range(N_DP)])]
    unnamed x377 -> x412, local copies, waits for them, and re-layouts: 18.8 us -> 32.9 us
  transfers between devices with their start and end apart: 76 -> 87, of which waited for: 51 -> 42; matrix products, arithmetic and copies ran while one was open for 31% -> 40% of each run, Pallas kernels for 0% -> 0%
where the time goes in v2:
time: 718 us; the launch traced here: 706 us
  waiting for transfers between devices  223 us (31%)
  matrix products  145 us (20%)
  starting transfers between devices  122 us (17%)
  other arithmetic  111 us (15%)
  local copies, waits for them, and re-layouts  86.5 us (12%)
  between operations  17.8 us (2%)
    ppermute x32, waiting for transfers between devices, over_col(): return lax.ppermute(x, 'col', SWAP)  79.2 us
    ppermute x32, starting transfers between devices, over_col(): return lax.ppermute(x, 'col', SWAP)  62.4 us
    dot_general x18, matrix products, dot_across(): return lax.dot_general(a, b, ACROSS, preferred_element_type=F32)  58.5 us
    ppermute x8, waiting for transfers between devices, over_both(): return lax.ppermute(x, ('row', 'col'), DIAGONAL)  51.2 us
    ppermute x17, waiting for transfers between devices, over_row(): return lax.ppermute(x, 'row', SWAP)  50.6 us
    dot_general x18, matrix products, dot(): return jnp.dot(a, b, preferred_element_type=F32)  47 us
    ppermute x26, waiting for transfers between devices, over_dp(): return lax.ppermute(x, 'dp', [(i, target(i)) for i in range(N_DP)])  41.7 us
    dot_general x22, matrix products, dot_down(): return lax.dot_general(a, b, DOWNWARD, preferred_element_type=F32)  39.6 us
  transfers between devices with their start and end apart: 87, of which 42 were waited for; matrix products, arithmetic and copies ran while one was open for 40% of the time, Pallas kernels for 0%

profile of v2, /device:TPU:6, one launch (start us, length us, event | category | flops | bytes accessed | tf_op | source)
XLA Modules:
  0.0 706.0 jit_solution(4163420302099804270)
XLA Ops:
  42.8 15.3 %collective-permute-done.3 = bf16[384,1024]{1,0:T(8,128)(2,1)} collective-permute-done((bf16[384,1024]{1,0:T(8,128)(2,1)}, bf16[384,1024]{1,0:T(8,128)(2,1)}, u32[]{:S(2)}, u32[]{:S(2)}) %collective-permute-start.3) | collective-permute-done | bytes 786464 | tf_op jit(solution)/shard_map/ppermute | solution.py:45
  63.4 6.6 collective-permute-done.2
  77.2 4.9 collective-permute-done.5
  95.8 9.8 %collective-permute-done.26 = bf16[48,3840]{1,0:T(8,128)(2,1)S(1)} collective-permute-done((bf16[48,3840]{1,0:T(8,128)(2,1)S(1)}, bf16[48,3840]{1,0:T(8,128)(2,1)S(1)}, u32[]{:S(2)}, u32[]{:S(2)}) %collective-permute-start.26) | collective-permute-done | bytes 368672 | tf_op jit(solution)/shard_map/ppermute | solution.py:45
  119.6 9.3 %collective-permute-done.6 = bf16[384,768]{1,0:T(8,128)(2,1)S(1)} collective-permute-done((bf16[384,768]{1,0:T(8,128)(2,1)S(1)}, bf16[384,768]{1,0:T(8,128)(2,1)S(1)}, u32[]{:S(2)}, u32[]{:S(2)}) %collective-permute-start.6) | collective-permute-done | bytes 589856 | tf_op jit(solution)/shard_map/ppermute | solution.py:45
  137.8 8.5 %collective-permute-done.8 = bf16[128,1536]{1,0:T(8,128)(2,1)} collective-permute-done((bf16[128,1536]{1,0:T(8,128)(2,1)}, bf16[128,1536]{1,0:T(8,128)(2,1)}, u32[]{:S(2)}, u32[]{:S(2)}) %collective-permute-start.8) | collective-permute-done | bytes 393248 | tf_op jit(solution)/shard_map/ppermute | solution.py:41
  152.6 11.2 %collective-permute-done.17 = bf16[384,1024]{1,0:T(8,128)(2,1)} collective-permute-done((bf16[384,1024]{1,0:T(8,128)(2,1)S(1)}, bf16[384,1024]{1,0:T(8,128)(2,1)}, u32[]{:S(2)}, u32[]{:S(2)}) %collective-permute-start.17) | collective-permute-done | bytes 786464 | tf_op jit(solution)/shard_map/ppermute | solution.py:45
  163.8 16.2 %collective-permute-done.11 = bf16[128,1536]{1,0:T(8,128)(2,1)S(1)} collective-permute-done((bf16[128,1536]{1,0:T(8,128)(2,1)S(1)}, bf16[128,1536]{1,0:T(8,128)(2,1)S(1)}, u32[]{:S(2)}, u32[]{:S(2)}) %collective-permute-start.11) | collective-permute-done | bytes 393248 | tf_op jit(solution)/shard_map/ppermute | solution.py:49
  181.4 7.7 %fusion.6 = f32[512,3072]{1,0:T(8,128)S(1)} fusion(bf16[512,1536]{1,0:T(8,128)(2,1)S(1)} %pad_maximum_fusion.10, bf16[1536,4608]{1,0:T(8,128)(2,1)} %all-gather.3.cloned.1.call-done), kind=kOutput, calls=%fused_computation.9 | convolution fusion | flops 4831838208 | bytes 17301504 | tf_op jit(solution)/shard_map/dot_general | solution.py:29
  192.7 7.1 %fusion.273 = (bf16[512,1536]{1,0:T(8,128)(2,1)S(1)}, f32[512,1536]{1,0:T(8,128)}) fusion(bf16[512,1536]{1,0:T(8,128)(2,1)S(1)} %fusion.26, bf16[1536,4608]{1,0:T(8,128)(2,1)} %all-gather.3.cloned.1.call-done), kind=kOutput, calls=%fused_computation.675 | convolution fusion | flops 2416705536 | bytes 11010048 | tf_op jit(solution)/shard_map/dot_general | solution.py:29
  212.5 10.0 %collective-permute-done.15 = bf16[128,1536]{1,0:T(8,128)(2,1)} collective-permute-done((bf16[128,1536]{1,0:T(8,128)(2,1)}, bf16[128,1536]{1,0:T(8,128)(2,1)}, u32[]{:S(2)}, u32[]{:S(2)}) %collective-permute-start.15) | collective-permute-done | bytes 393248 | tf_op jit(solution)/shard_map/ppermute | solution.py:49
  228.1 10.1 %collective-permute-done.20 = bf16[384,768]{1,0:T(8,128)(2,1)} collective-permute-done((bf16[384,768]{1,0:T(8,128)(2,1)}, bf16[384,768]{1,0:T(8,128)(2,1)}, u32[]{:S(2)}, u32[]{:S(2)}) %collective-permute-start.20) | collective-permute-done | bytes 589856 | tf_op jit(solution)/shard_map/ppermute | solution.py:45
  238.4 5.7 collective-permute-done.16
  286.8 16.1 %collective-permute-done.25 = bf16[128,1536]{1,0:T(8,128)(2,1)S(1)} collective-permute-done((bf16[128,1536]{1,0:T(8,128)(2,1)S(1)}, bf16[128,1536]{1,0:T(8,128)(2,1)S(1)}, u32[]{:S(2)}, u32[]{:S(2)}) %collective-permute-start.25) | collective-permute-done | bytes 393248 | tf_op jit(solution)/shard_map/ppermute | solution.py:49
  304.4 9.2 %fusion.2 = f32[512,3072]{1,0:T(8,128)S(1)} fusion(bf16[512,1536]{1,0:T(8,128)(2,1)} %pad_maximum_fusion.12, bf16[1536,4608]{1,0:T(8,128)(2,1)} %all-gather.5.cloned.1.call-done), kind=kOutput, calls=%fused_computation.5 | convolution fusion | flops 4831838208 | bytes 17301504 | tf_op jit(solution)/shard_map/dot_general | solution.py:29
  314.2 9.0 %multiply_multiply_fusion.1 = (f32[512,1536]{1,0:T(8,128)S(1)}, f32[512,1536]{1,0:T(8,128)}) fusion(f32[512,3072]{1,0:T(8,128)S(1)} %fusion.2, bf16[1536,4608]{1,0:T(8,128)(2,1)} %all-gather.5.cloned.1.call-done, bf16[128,1536]{1,0:T(8,128)(2,1)} %collective-permute-done.34, bf16[128,1536]{1,0:T(8,128)(2,1)} %collective-permute-done.33, ...), kind=kOutput, calls=%fused_computation.54 | convolution fusion | flops 2428502016 | bytes 18874368 | tf_op jit(solution)/shard_map/dot_general | solution.py:33
  330.8 9.5 %fusion.274 = (bf16[512,1536]{1,0:T(8,128)(2,1)S(1)}, f32[512,1536]{1,0:T(8,128)}) fusion(f32[512,1536]{1,0:T(8,128)S(1)} %fusion.163, bf16[1536,4608]{1,0:T(8,128)(2,1)} %all-gather.5.cloned.1.call-done, bf16[512,1536]{1,0:T(8,128)(2,1)S(1)} %get-tuple-element.148, bf16[512,1536]{1,0:T(8,128)(2,1)S(1)} %get-tuple-element.147), kind=kOutput, calls=%fused_computation.676 | convolution fusion | flops 4839702528 | bytes 20447232 | tf_op jit(solution)/shard_map/dot_general | solution.py:33
  348.0 5.3 collective-permute-start.36
  359.8 11.4 %pad_maximum_fusion.1 = bf16[768,9216]{1,0:T(8,128)(2,1)} fusion(bf16[768,1536]{1,0:T(8,128)(2,1)S(1)} %convolution_convert_fusion.6, bf16[768,1536]{1,0:T(8,128)(2,1)S(1)} %convolution_convert_fusion.7, bf16[768,3072]{1,0:T(8,128)(2,1)S(1)} %convolution_convert_fusion.2, bf16[768,3072]{1,0:T(8,128)(2,1)S(1)} %convolution_convert_fusion.3), kind=kLoop, calls=%fused_computation.1 | loop fusion | flops 56623104 | bytes 28311552 | tf_op jit(solution)/shard_map/concatenate | solution.py:82
  374.3 7.3 %fusion.275 = (bf16[512,1536]{1,0:T(8,128)(2,1)S(1)}, f32[512,1536]{1,0:T(8,128)}) fusion(bf16[512,1536]{1,0:T(8,128)(2,1)} %copy-done.87, bf16[1536,4608]{1,0:T(8,128)(2,1)} %all-gather.5.cloned.1.call-done), kind=kOutput, calls=%fused_computation.677 | convolution fusion | flops 2416705536 | bytes 11010048 | tf_op jit(solution)/shard_map/dot_general | solution.py:29
  409.2 5.0 collective-permute-start.39
  432.5 4.9 collective-permute-done.40
  446.1 8.9 %collective-permute-done.43 = bf16[128,1536]{1,0:T(8,128)(2,1)S(1)} collective-permute-done((bf16[128,1536]{1,0:T(8,128)(2,1)S(1)}, bf16[128,1536]{1,0:T(8,128)(2,1)S(1)}, u32[]{:S(2)}, u32[]{:S(2)}) %collective-permute-start.43) | collective-permute-done | bytes 393248 | tf_op jit(solution)/shard_map/ppermute | solution.py:49
  456.0 8.1 %multiply_convert_fusion.2 = (bf16[512,1536]{1,0:T(8,128)(2,1)}, bf16[512,1536]{1,0:T(8,128)(2,1)}, f32[512,1536]{1,0:T(8,128)S(1)}) fusion(f32[512,3072]{1,0:T(8,128)S(1)} %bitcast.479, f32[512,384]{1,0:T(8,128)S(1)} %copy-done.72, f32[512,384]{1,0:T(8,128)S(1)} %copy-done.66, f32[512,384]{1,0:T(8,128)S(1)} %copy-done.70, f32[512,384]{1,0:T(8,128)S(1)} %copy-done.68, ...), kind=kOutput, calls=%fused_computation.50 | convolution fusion | flops 2437152768 | bytes 22020096 | tf_op jit(solution)/shard_map/dot_general | solution.py:33
  465.5 9.8 %fusion.276 = (bf16[512,1536]{1,0:T(8,128)(2,1)S(1)}, f32[512,1536]{1,0:T(8,128)}) fusion(f32[512,1536]{1,0:T(8,128)S(1)} %fusion.167, bf16[1536,4608]{1,0:T(8,128)(2,1)} %all-gather.3.cloned.1.call-done, bf16[512,1536]{1,0:T(8,128)(2,1)} %get-tuple-element.146, bf16[512,1536]{1,0:T(8,128)(2,1)} %get-tuple-element.145), kind=kOutput, calls=%fused_computation.678 | convolution fusion | flops 4839702528 | bytes 20447232 | tf_op jit(solution)/shard_map/dot_general | solution.py:33
  491.9 8.4 %pad_maximum_fusion.2 = bf16[768,9216]{1,0:T(8,128)(2,1)S(1)} fusion(bf16[768,1536]{1,0:T(8,128)(2,1)} %convolution_convert_fusion.4, bf16[768,1536]{1,0:T(8,128)(2,1)S(1)} %convolution_convert_fusion.5, bf16[768,3072]{1,0:T(8,128)(2,1)S(1)} %convolution_convert_fusion, bf16[768,3072]{1,0:T(8,128)(2,1)S(1)} %convolution_convert_fusion.1), kind=kLoop, calls=%fused_computation.2 | loop fusion | flops 56623104 | bytes 28311552 | tf_op jit(solution)/shard_map/concatenate | solution.py:82
  501.6 11.7 %pad_maximum_fusion = bf16[768,12800]{1,0:T(8,128)(2,1)} fusion(bf16[768,3584]{1,0:T(8,128)(2,1)S(1)} %bitcast.469, bf16[768,9216]{1,0:T(8,128)(2,1)S(1)} %pad_maximum_fusion.2), kind=kLoop, calls=%fused_computation | loop fusion | flops 39321600 | bytes 39321600 | tf_op jit(solution)/shard_map/concatenate | solution.py:82
  521.0 5.3 collective-permute-done.47
  584.2 6.9 collective-permute-done.55
  617.4 4.8 collective-permute-done.65
  623.5 7.7 %collective-permute-done.66 = bf16[4,24,1792]{2,1,0:T(8,128)(2,1)S(1)} collective-permute-done((bf16[4,24,1792]{2,1,0:T(8,128)(2,1)S(1)}, bf16[4,24,1792]{2,1,0:T(8,128)(2,1)S(1)}, u32[]{:S(2)}, u32[]{:S(2)}) %collective-permute-start.66) | collective-permute-done | bytes 344096 | tf_op jit(solution)/shard_map/ppermute | solution.py:53
  661.7 4.8 collective-permute-done.81
  (905 shorter events, 411.6 us)
Async XLA Ops:
  7.2 174.2 %all-gather.3.cloned.1.call-start = ((), (), s32[]{:S(2)}) async-start(), calls=%async_computation.2 | async-start | bytes 14598144 | tf_op jit(solution)/shard_map/all_gather | solution.py:182
  9.3 30.0 %collective-permute-start.1 = (bf16[20,768]{1,0:T(8,128)(2,1)}, bf16[20,768]{1,0:T(8,128)(2,1)S(1)}, u32[]{:S(2)}, u32[]{:S(2)}) collective-permute-start(bf16[20,768]{1,0:T(8,128)(2,1)} %pad_maximum_fusion.77), channel_id=1, source_target_pairs={{0,1},{1,0},{2,3},{3,2},{4,5},{5,4},{6,7},{7,6},{8,9},{9,8},{10,11... | collective-permute-start | bytes 92168 | tf_op jit(solution)/shard_map/ppermute | solution.py:45
  25.2 51.1 %collective-permute-start.12 = (bf16[48,3840]{1,0:T(8,128)(2,1)}, bf16[48,3840]{1,0:T(8,128)(2,1)}, u32[]{:S(2)}, u32[]{:S(2)}) collective-permute-start(bf16[48,3840]{1,0:T(8,128)(2,1)} %bitcast_dynamic-update-slice_fusion.1), channel_id=1, source_target_pairs={{0,1},{1,0},{2,3},{3,2},{4,5},{5,4},{6,7},{7,6},{8,9},{9,8},{10,11... | collective-permute-start | bytes 1105928 | tf_op jit(solution)/shard_map/ppermute | solution.py:45
  36.0 22.1 %collective-permute-start.3 = (bf16[384,1024]{1,0:T(8,128)(2,1)}, bf16[384,1024]{1,0:T(8,128)(2,1)}, u32[]{:S(2)}, u32[]{:S(2)}) collective-permute-start(bf16[384,1024]{1,0:T(8,128)(2,1)} %constant_dynamic-slice_fusion.19), channel_id=1, source_target_pairs={{0,1},{1,0},{2,3},{3,2},{4,5},{5,4},{6,7},{7,6},{8,9},{9,8},{10,11... | collective-permute-start | bytes 2359304 | tf_op jit(solution)/shard_map/ppermute | solution.py:45
  93.8 210.5 %all-gather.5.cloned.1.call-start = ((), (), s32[]{:S(2)}) async-start(), calls=%async_computation.3 | async-start | bytes 14598144 | tf_op jit(solution)/shard_map/all_gather | solution.py:182
  106.5 545.4 %reduce-scatter.5.cloned.1.call-start = ((), (), s32[]{:S(2)}) async-start(), calls=%async_computation.5 | async-start | bytes 14598144 | tf_op jit(solution)/shard_map/reduce_scatter | solution.py:322
  135.7 28.1 %collective-permute-start.17 = (bf16[384,1024]{1,0:T(8,128)(2,1)S(1)}, bf16[384,1024]{1,0:T(8,128)(2,1)}, u32[]{:S(2)}, u32[]{:S(2)}) collective-permute-start(bf16[384,1024]{1,0:T(8,128)(2,1)S(1)} %constant_dynamic-slice_fusion.13), channel_id=1, source_target_pairs={{0,1},{1,0},{2,3},{3,2},{4,5},{5,4},{6,7},{7,6},{8,9},{9,8},{10,11... | collective-permute-start | bytes 2359304 | tf_op jit(solution)/shard_map/ppermute | solution.py:45
  148.3 31.8 %collective-permute-start.11 = (bf16[128,1536]{1,0:T(8,128)(2,1)S(1)}, bf16[128,1536]{1,0:T(8,128)(2,1)S(1)}, u32[]{:S(2)}, u32[]{:S(2)}) collective-permute-start(bf16[128,1536]{1,0:T(8,128)(2,1)S(1)} %pad_maximum_fusion.36), channel_id=1, source_target_pairs={{0,3},{1,2},{2,1},{3,0},{4,7},{5,6},{6,5},{7,4},{8,11},{9,10},{10,... | collective-permute-start | bytes 1179656 | tf_op jit(solution)/shard_map/ppermute | solution.py:49
  149.5 30.5 %collective-permute-start.10 = (bf16[128,1536]{1,0:T(8,128)(2,1)S(1)}, bf16[128,1536]{1,0:T(8,128)(2,1)S(1)}, u32[]{:S(2)}, u32[]{:S(2)}) collective-permute-start(bf16[128,1536]{1,0:T(8,128)(2,1)S(1)} %pad_maximum_fusion.36), channel_id=1, source_target_pairs={{0,1},{1,0},{2,3},{3,2},{4,5},{5,4},{6,7},{7,6},{8,9},{9,8},{10,11... | collective-permute-start | bytes 1179656 | tf_op jit(solution)/shard_map/ppermute | solution.py:45
  151.1 28.9 %collective-permute-start.9 = (bf16[128,1536]{1,0:T(8,128)(2,1)S(1)}, bf16[128,1536]{1,0:T(8,128)(2,1)S(1)}, u32[]{:S(2)}, u32[]{:S(2)}) collective-permute-start(bf16[128,1536]{1,0:T(8,128)(2,1)S(1)} %multiply_convert_fusion.8), channel_id=1, source_target_pairs={{0,2},{2,0},{1,3},{3,1},{4,6},{6,4},{5,7},{7,5},{8,10},{10,8},{9,1... | collective-permute-start | bytes 1179656 | tf_op jit(solution)/shard_map/ppermute | solution.py:41
  163.8 41.8 %collective-permute-start.18 = (bf16[384,1024]{1,0:T(8,128)(2,1)}, bf16[384,1024]{1,0:T(8,128)(2,1)}, u32[]{:S(2)}, u32[]{:S(2)}) collective-permute-start(bf16[384,1024]{1,0:T(8,128)(2,1)} %collective-permute-done.17), channel_id=1, source_target_pairs={{0,4},{4,0},{8,12},{12,8},{16,20},{20,16},{24,28},{28,24},{32,36},... | collective-permute-start | bytes 2359304 | tf_op jit(solution)/shard_map/ppermute | solution.py:53
  201.4 21.0 %collective-permute-start.15 = (bf16[128,1536]{1,0:T(8,128)(2,1)}, bf16[128,1536]{1,0:T(8,128)(2,1)}, u32[]{:S(2)}, u32[]{:S(2)}) collective-permute-start(bf16[128,1536]{1,0:T(8,128)(2,1)} %pad_maximum_fusion.38), channel_id=1, source_target_pairs={{0,3},{1,2},{2,1},{3,0},{4,7},{5,6},{6,5},{7,4},{8,11},{9,10},{10,... | collective-permute-start | bytes 1179656 | tf_op jit(solution)/shard_map/ppermute | solution.py:49
  203.9 20.3 %collective-permute-start.13 = (bf16[128,1536]{1,0:T(8,128)(2,1)}, bf16[128,1536]{1,0:T(8,128)(2,1)}, u32[]{:S(2)}, u32[]{:S(2)}) collective-permute-start(bf16[128,1536]{1,0:T(8,128)(2,1)} %slice.1144), channel_id=1, source_target_pairs={{0,2},{2,0},{1,3},{3,1},{4,6},{6,4},{5,7},{7,5},{8,10},{10,8},{9,1... | collective-permute-start | bytes 1179656 | tf_op jit(solution)/shard_map/ppermute | solution.py:41
  210.9 27.3 %collective-permute-start.20 = (bf16[384,768]{1,0:T(8,128)(2,1)}, bf16[384,768]{1,0:T(8,128)(2,1)}, u32[]{:S(2)}, u32[]{:S(2)}) collective-permute-start(bf16[384,768]{1,0:T(8,128)(2,1)} %dynamic-slice_bitcast_fusion.1), channel_id=1, source_target_pairs={{0,1},{1,0},{2,3},{3,2},{4,5},{5,4},{6,7},{7,6},{8,9},{9,8},{10,11... | collective-permute-start | bytes 1769480 | tf_op jit(solution)/shard_map/ppermute | solution.py:45
  238.2 22.4 %collective-permute-start.21 = (bf16[384,768]{1,0:T(8,128)(2,1)}, bf16[384,768]{1,0:T(8,128)(2,1)}, u32[]{:S(2)}, u32[]{:S(2)}) collective-permute-start(bf16[384,768]{1,0:T(8,128)(2,1)} %collective-permute-done.20), channel_id=1, source_target_pairs={{0,4},{4,0},{8,12},{12,8},{16,20},{20,16},{24,28},{28,24},{32,36},... | collective-permute-start | bytes 1769480 | tf_op jit(solution)/shard_map/ppermute | solution.py:53
  278.5 24.3 %collective-permute-start.25 = (bf16[128,1536]{1,0:T(8,128)(2,1)S(1)}, bf16[128,1536]{1,0:T(8,128)(2,1)S(1)}, u32[]{:S(2)}, u32[]{:S(2)}) collective-permute-start(bf16[128,1536]{1,0:T(8,128)(2,1)S(1)} %pad_maximum_fusion.41), channel_id=1, source_target_pairs={{0,3},{1,2},{2,1},{3,0},{4,7},{5,6},{6,5},{7,4},{8,11},{9,10},{10,... | collective-permute-start | bytes 1179656 | tf_op jit(solution)/shard_map/ppermute | solution.py:49
  280.8 22.3 %collective-permute-start.24 = (bf16[128,1536]{1,0:T(8,128)(2,1)S(1)}, bf16[128,1536]{1,0:T(8,128)(2,1)S(1)}, u32[]{:S(2)}, u32[]{:S(2)}) collective-permute-start(bf16[128,1536]{1,0:T(8,128)(2,1)S(1)} %pad_maximum_fusion.41), channel_id=1, source_target_pairs={{0,1},{1,0},{2,3},{3,2},{4,5},{5,4},{6,7},{7,6},{8,9},{9,8},{10,11... | collective-permute-start | bytes 1179656 | tf_op jit(solution)/shard_map/ppermute | solution.py:45
  281.1 21.9 %collective-permute-start.23 = (bf16[128,1536]{1,0:T(8,128)(2,1)S(1)}, bf16[128,1536]{1,0:T(8,128)(2,1)S(1)}, u32[]{:S(2)}, u32[]{:S(2)}) collective-permute-start(bf16[128,1536]{1,0:T(8,128)(2,1)S(1)} %multiply_convert_fusion.6), channel_id=1, source_target_pairs={{0,2},{2,0},{1,3},{3,1},{4,6},{6,4},{5,7},{7,5},{8,10},{10,8},{9,1... | collective-permute-start | bytes 1179656 | tf_op jit(solution)/shard_map/ppermute | solution.py:41
  284.3 29.9 %collective-permute-start.34 = (bf16[128,1536]{1,0:T(8,128)(2,1)}, bf16[128,1536]{1,0:T(8,128)(2,1)}, u32[]{:S(2)}, u32[]{:S(2)}) collective-permute-start(bf16[128,1536]{1,0:T(8,128)(2,1)} %get-tuple-element.249), channel_id=1, source_target_pairs={{0,3},{1,2},{2,1},{3,0},{4,7},{5,6},{6,5},{7,4},{8,11},{9,10},{10,... | collective-permute-start | bytes 1179656 | tf_op jit(solution)/shard_map/ppermute | solution.py:49
  286.4 27.7 %collective-permute-start.33 = (bf16[128,1536]{1,0:T(8,128)(2,1)}, bf16[128,1536]{1,0:T(8,128)(2,1)}, u32[]{:S(2)}, u32[]{:S(2)}) collective-permute-start(bf16[128,1536]{1,0:T(8,128)(2,1)} %get-tuple-element.249), channel_id=1, source_target_pairs={{0,1},{1,0},{2,3},{3,2},{4,5},{5,4},{6,7},{7,6},{8,9},{9,8},{10,11... | collective-permute-start | bytes 1179656 | tf_op jit(solution)/shard_map/ppermute | solution.py:45
  348.0 25.3 %collective-permute-start.36 = (bf16[128,1536]{1,0:T(8,128)(2,1)}, bf16[128,1536]{1,0:T(8,128)(2,1)}, u32[]{:S(2)}, u32[]{:S(2)}) collective-permute-start(bf16[128,1536]{1,0:T(8,128)(2,1)} %pad_maximum_fusion.46), channel_id=1, source_target_pairs={{0,1},{1,0},{2,3},{3,2},{4,5},{5,4},{6,7},{7,6},{8,9},{9,8},{10,11... | collective-permute-start | bytes 1179656 | tf_op jit(solution)/shard_map/ppermute | solution.py:45
  354.0 19.3 %collective-permute-start.37 = (bf16[128,1536]{1,0:T(8,128)(2,1)}, bf16[128,1536]{1,0:T(8,128)(2,1)}, u32[]{:S(2)}, u32[]{:S(2)}) collective-permute-start(bf16[128,1536]{1,0:T(8,128)(2,1)} %pad_maximum_fusion.47), channel_id=1, source_target_pairs={{0,3},{1,2},{2,1},{3,0},{4,7},{5,6},{6,5},{7,4},{8,11},{9,10},{10,... | collective-permute-start | bytes 1179656 | tf_op jit(solution)/shard_map/ppermute | solution.py:49
  373.3 299.7 %reduce-scatter.3.cloned.1.call-start = ((), (), s32[]{:S(2)}) async-start(), calls=%async_computation.4 | async-start | bytes 20275200 | tf_op jit(solution)/shard_map/reduce_scatter | solution.py:322
  387.9 50.4 %collective-permute-start.29 = (bf16[128,1536]{1,0:T(8,128)(2,1)}, bf16[128,1536]{1,0:T(8,128)(2,1)}, u32[]{:S(2)}, u32[]{:S(2)}) collective-permute-start(bf16[128,1536]{1,0:T(8,128)(2,1)} %pad_maximum_fusion.43), channel_id=1, source_target_pairs={{0,3},{1,2},{2,1},{3,0},{4,7},{5,6},{6,5},{7,4},{8,11},{9,10},{10,... | collective-permute-start | bytes 1179656 | tf_op jit(solution)/shard_map/ppermute | solution.py:49
  391.9 46.4 %collective-permute-start.28 = (bf16[128,1536]{1,0:T(8,128)(2,1)}, bf16[128,1536]{1,0:T(8,128)(2,1)}, u32[]{:S(2)}, u32[]{:S(2)}) collective-permute-start(bf16[128,1536]{1,0:T(8,128)(2,1)} %pad_maximum_fusion.42), channel_id=1, source_target_pairs={{0,1},{1,0},{2,3},{3,2},{4,5},{5,4},{6,7},{7,6},{8,9},{9,8},{10,11... | collective-permute-start | bytes 1179656 | tf_op jit(solution)/shard_map/ppermute | solution.py:45
  391.9 46.4 %collective-permute-start.27 = (bf16[128,1536]{1,0:T(8,128)(2,1)}, bf16[128,1536]{1,0:T(8,128)(2,1)}, u32[]{:S(2)}, u32[]{:S(2)}) collective-permute-start(bf16[128,1536]{1,0:T(8,128)(2,1)} %slice.1176), channel_id=1, source_target_pairs={{0,2},{2,0},{1,3},{3,1},{4,6},{6,4},{5,7},{7,5},{8,10},{10,8},{9,1... | collective-permute-start | bytes 1179656 | tf_op jit(solution)/shard_map/ppermute | solution.py:41
  477.0 24.5 %collective-permute-start.45 = (bf16[128,1536]{1,0:T(8,128)(2,1)}, bf16[128,1536]{1,0:T(8,128)(2,1)}, u32[]{:S(2)}, u32[]{:S(2)}) collective-permute-start(bf16[128,1536]{1,0:T(8,128)(2,1)} %pad_maximum_fusion.50), channel_id=1, source_target_pairs={{0,1},{1,0},{2,3},{3,2},{4,5},{5,4},{6,7},{7,6},{8,9},{9,8},{10,11... | collective-permute-start | bytes 1179656 | tf_op jit(solution)/shard_map/ppermute | solution.py:45
  478.4 23.2 %collective-permute-start.46 = (bf16[128,1536]{1,0:T(8,128)(2,1)}, bf16[128,1536]{1,0:T(8,128)(2,1)S(1)}, u32[]{:S(2)}, u32[]{:S(2)}) collective-permute-start(bf16[128,1536]{1,0:T(8,128)(2,1)} %pad_maximum_fusion.51), channel_id=1, source_target_pairs={{0,3},{1,2},{2,1},{3,0},{4,7},{5,6},{6,5},{7,4},{8,11},{9,10},{10,... | collective-permute-start | bytes 1179656 | tf_op jit(solution)/shard_map/ppermute | solution.py:49
  480.1 21.5 %collective-permute-start.44 = (bf16[128,1536]{1,0:T(8,128)(2,1)}, bf16[128,1536]{1,0:T(8,128)(2,1)}, u32[]{:S(2)}, u32[]{:S(2)}) collective-permute-start(bf16[128,1536]{1,0:T(8,128)(2,1)} %slice.1221), channel_id=1, source_target_pairs={{0,2},{2,0},{1,3},{3,1},{4,6},{6,4},{5,7},{7,5},{8,10},{10,8},{9,1... | collective-permute-start | bytes 1179656 | tf_op jit(solution)/shard_map/ppermute | solution.py:41
  562.7 41.8 %collective-permute-start.58 = (bf16[4,4,24,3584]{3,2,1,0:T(8,128)(2,1)}, bf16[4,4,24,3584]{3,2,1,0:T(8,128)(2,1)}, u32[]{:S(2)}, u32[]{:S(2)}) collective-permute-start(bf16[4,4,24,3584]{3,2,1,0:T(8,128)(2,1)} %dynamic-slice_bitcast_fusion), channel_id=1, source_target_pairs={{0,4},{4,0},{8,12},{12,8},{16,20},{20,16},{24,28},{28,24},{32,36},... | collective-permute-start | bytes 8257544 | tf_op jit(solution)/shard_map/ppermute | solution.py:53
  565.8 27.0 %collective-permute-start.30 = (bf16[128,768]{1,0:T(8,128)(2,1)S(1)}, bf16[128,768]{1,0:T(8,128)(2,1)S(1)}, u32[]{:S(2)}, u32[]{:S(2)}) collective-permute-start(bf16[128,768]{1,0:T(8,128)(2,1)S(1)} %get-tuple-element.245), channel_id=1, source_target_pairs={{0,1},{1,0},{2,3},{3,2},{4,5},{5,4},{6,7},{7,6},{8,9},{9,8},{10,11... | collective-permute-start | bytes 589832 | tf_op jit(solution)/shard_map/ppermute | solution.py:45
  577.3 23.2 %collective-permute-start.50 = (bf16[128,768]{1,0:T(8,128)(2,1)S(1)}, bf16[128,768]{1,0:T(8,128)(2,1)S(1)}, u32[]{:S(2)}, u32[]{:S(2)}) collective-permute-start(bf16[128,768]{1,0:T(8,128)(2,1)S(1)} %get-tuple-element.241), channel_id=1, source_target_pairs={{0,1},{1,0},{2,3},{3,2},{4,5},{5,4},{6,7},{7,6},{8,9},{9,8},{10,11... | collective-permute-start | bytes 589832 | tf_op jit(solution)/shard_map/ppermute | solution.py:45
  (255 other events, 2550.3 us)
Sparse Core Ops, SparseCore 0:
  94.0 66.8 all-gather.2
  163.1 66.0 all-gather.4
  373.4 112.3 reduce-scatter.4
  513.5 136.3 reduce-scatter.2

commit v3 on v1

v3 whole, which is shorter than its diff:
```python
import jax
import jax.numpy as jnp
import numpy as np
from jax import lax
from jax.experimental import pallas as pl
from jax.experimental.pallas import tpu as pltpu
from jax.sharding import PartitionSpec as P

D = 1536
HALF = D // 2
HEAD = 128
Q_HEADS = 6
EXPERTS = 8
MINE = 4
FF = 384
LAYERS = 2
TOK_DP = 512
QUARTER = 128
EPSILON = 1e-06
ROPE_THETA = 1000000.0
MASKED_SCORE = -1e30
ACROSS = (((1,), (1,)), ((), ()))
DOWNWARD = (((0,), (0,)), ((), ()))
SWAP = [(0, 1), (1, 0)]
DIAGONAL = [(0, 3), (1, 2), (2, 1), (3, 0)]
N_DP = 32
SAME_CORE = [[2 * k + core for k in range(16)] for core in range(2)]
PIECE = 48
CORE_ROWS = 384
QKV = (Q_HEADS + 2) * HEAD
VMEM_LIMIT = 48 << 20
WIDE = 512
STEPS = D // WIDE
PARTS = WIDE // 128
BF16 = jnp.bfloat16
F32 = jnp.float32


def whole(shape):
    return pl.BlockSpec(shape, lambda j: (0,) * len(shape))


BLOCK = (QUARTER, D)
ALL = (TOK_DP, D)
LANES = (TOK_DP, 128)
SLAB = pl.BlockSpec((TOK_DP, WIDE), lambda j: (0, j))


def dot(a, b):
    return jnp.dot(a, b, preferred_element_type=F32)


def dot_across(a, b):
    return lax.dot_general(a, b, ACROSS, preferred_element_type=F32)


def dot_down(a, b):
    return lax.dot_general(a, b, DOWNWARD, preferred_element_type=F32)


def over_row(x):
    return lax.ppermute(x, "row", SWAP)


def over_col(x):
    return lax.ppermute(x, "col", SWAP)


def over_both(x):
    return lax.ppermute(x, ("row", "col"), DIAGONAL)


def over_dp(x, target):
    return lax.ppermute(x, "dp", [(i, target(i)) for i in range(N_DP)])


def by_col(column, own, other, axis):
    return jnp.where(
        column == 0,
        jnp.concatenate([own, other], axis=axis),
        jnp.concatenate([other, own], axis=axis),
    )


def half_of(x, index, axis):
    size = x.shape[axis] // 2
    return lax.dynamic_slice_in_dim(x, index * size, size, axis=axis)


def halves(x):
    return [x[:, :HALF], x[:, HALF:]]


def turned(x):
    return jnp.concatenate([x[:, HALF:], x[:, :HALF]], axis=1)


def tied(*values):
    return lax.optimization_barrier(values)


def pack(parts):
    return jnp.concatenate([x.astype(BF16) for x in parts], axis=1)


def to_quarter(block, column):
    own = half_of(block, column, 0)
    return jnp.concatenate([own, over_col(half_of(block, 1 - column, 0))], axis=1)


def from_quarter(block, column):
    own, other = halves(block)
    return by_col(column, own, over_col(other), 0)


def gather_four(x):
    other = turned(x)
    return (x, over_row(x), over_col(other), over_both(other))


def total(parts):
    return sum(x.astype(F32) for x in parts)


def gather_two(x):
    return (x, over_row(x))


def segments(seq_lengths, seq_owner, data_index):
    owned_len = jnp.where(seq_owner == data_index, seq_lengths, 0)
    seq_ends = jnp.cumsum(owned_len)
    places = jnp.arange(TOK_DP, dtype=jnp.int32)
    finished = (seq_ends[None, :] <= places[:, None]).astype(jnp.int32)
    segment = jnp.sum(finished, axis=1)
    starts = jnp.sum(finished * owned_len[None, :], axis=1)
    valid_row = places < jnp.sum(owned_len)
    position = jnp.where(valid_row, places - starts, 0)
    return (segment, position, valid_row, places)


def normalize(stream, gain):
    inv_rms = lax.rsqrt(jnp.mean(stream * stream, axis=1, keepdims=True) + EPSILON)
    return (inv_rms, (stream * inv_rms * gain).astype(BF16))


def norm_back(upstream, grad_normed, stream, inv_rms, gain):
    scaled = gain * grad_normed
    dots = jnp.sum(scaled * stream, axis=1, keepdims=True)
    grad_stream = upstream + inv_rms * scaled - stream * (inv_rms * inv_rms * inv_rms * dots / D)
    return grad_stream


def pieces_kernel(layer, place, gate, up, down, query, key, value, out, *rest):
    own, other, *extra, sems = rest
    column = lax.axis_index("col")
    index = place[0]
    start = pl.multiple_of((index % 16) * PIECE, 16)
    down_start = pl.multiple_of((index % 8) * PIECE, 16)
    width = Q_HEADS * HEAD
    moves = []
    for side, target in ((column, own), (1 - column, other)):
        for k, weight in enumerate((gate, up)):
            for e in range(MINE):
                moves.append(
                    (
                        weight.at[layer, side * MINE + e, pl.ds(start, PIECE), :],
                        target.at[:, pl.ds((k * MINE + e) * FF, FF)],
                    )
                )
        moves.append(
            (
                down.at[layer, side * MINE + index // 8, pl.ds(down_start, PIECE), :],
                target.at[:, pl.ds(2 * D, HALF)],
            )
        )
    if extra:
        qkv_own, out_own, out_send, *parts = extra
        upper = pl.multiple_of(index % 2 * CORE_ROWS, 128)
        out_start = pl.multiple_of(index // 2 * PIECE, 16)
        offset = 0
        for weight, size in ((query, width), (key, HEAD), (value, HEAD)):
            columns = pl.ds(offset, size)
            moves.append((weight.at[layer], qkv_own.at[:, columns]))
            for k, target in enumerate(parts):
                moves.append((weight.at[k, pl.ds(start, PIECE), :], target.at[:, columns]))
            offset += size
        moves.append((out.at[layer], out_own))
        moves.append((out.at[layer, pl.ds(upper, CORE_ROWS), :], out_send))
        for k, target in enumerate(parts):
            moves.append(
                (
                    out.at[k, pl.ds(out_start, PIECE), pl.ds(upper, CORE_ROWS)],
                    target.at[:, pl.ds(QKV, CORE_ROWS)],
                )
            )
    copies = [pltpu.make_async_copy(a, b, sems.at[i]) for i, (a, b) in enumerate(moves)]
    for copy in copies:
        copy.start()
    for copy in copies:
        copy.wait()


def take_pieces(layer, place, weights, first):
    shapes = [(PIECE, 2 * D + HALF)] * 2
    if first:
        shapes += [(HALF, QKV), (HALF, HALF), (CORE_ROWS, HALF)]
        shapes += [(PIECE, QKV + CORE_ROWS)] * LAYERS
    anywhere = pl.BlockSpec(memory_space=pl.ANY)
    inside = pl.BlockSpec(memory_space=pltpu.VMEM)
    return pl.pallas_call(
        lambda *refs: pieces_kernel(layer, *refs),
        out_shape=[jax.ShapeDtypeStruct(x, BF16) for x in shapes],
        in_specs=[pl.BlockSpec(memory_space=pltpu.SMEM)] + [anywhere] * 7,
        out_specs=[inside] * len(shapes),
        scratch_shapes=[pltpu.SemaphoreType.DMA((31,))],
        compiler_params=pltpu.CompilerParams(vmem_limit_bytes=VMEM_LIMIT),
        name="take_pieces",
    )(place.reshape(1), *weights)


def gather_all(piece):
    return lax.all_gather(piece, "dp", axis=0, tiled=True)


def expert_piece(own, other, data_index):
    gate_up = jnp.where(data_index < 16, own[:, : 2 * D], other[:, : 2 * D])
    return jnp.concatenate([gate_up, own[:, 2 * D :], other[:, 2 * D :]], axis=1)


def attention_piece(own, other, data_index):
    qkv = jnp.where(data_index < 16, own[:, :QKV], other[:, :QKV])
    return jnp.concatenate([qkv, own[:, QKV:], other[:, QKV:]], axis=1)


def attention_whole(gathered):
    outs = []
    for k in range(2):
        part = gathered[:, QKV + k * CORE_ROWS : QKV + (k + 1) * CORE_ROWS]
        part = part.reshape(16, 2, PIECE, CORE_ROWS).transpose(0, 2, 1, 3)
        outs.append(part.reshape(HALF, HALF))
    return (gathered, outs)


def turn(x, cosine, sine):
    return x * cosine + pltpu.roll(x, HEAD // 2, 1) * sine


def rotate_kernel(cosine, sine, *rest):
    *parts, query, pair = rest
    values = parts[0][...]
    for x in parts[1:]:
        values = values + x[...].astype(F32)
    for h in range(Q_HEADS + 1):
        target, column = (query, h * HEAD) if h < Q_HEADS else (pair, 0)
        rotated = turn(values[:, h * HEAD : (h + 1) * HEAD], cosine[...], sine[...])
        target[:, column : column + HEAD] = rotated.astype(BF16)
    pair[:, HEAD:] = values[:, (Q_HEADS + 1) * HEAD :].astype(BF16)


def local_call(kernel, shapes, operands, name, specs=None):
    outs = [jax.ShapeDtypeStruct(*x) for x in shapes]
    specs = specs or {}
    return pl.pallas_call(
        kernel,
        grid=(1,),
        in_specs=[specs.get(k) or whole(x.shape) for k, x in enumerate(operands)],
        out_specs=[whole(x.shape) for x in outs],
        out_shape=outs,
        compiler_params=pltpu.CompilerParams(vmem_limit_bytes=VMEM_LIMIT),
        cost_estimate=pl.CostEstimate(flops=4 << 30, bytes_accessed=8 << 20, transcendentals=1 << 20),
        name=name,
    )(*operands)


PAIR_ROWS = 2 * QUARTER


def rotate_parts(parts, geometry):
    cosine, sine = geometry[:2]
    return local_call(
        rotate_kernel,
        [((PAIR_ROWS, Q_HEADS * HEAD), BF16), ((PAIR_ROWS, 2 * HEAD), BF16)],
        [cosine, sine, *parts],
        "rotate_heads",
    )


def keys_values(own, far):
    return [
        jnp.concatenate([x[:, k * HEAD : (k + 1) * HEAD] for x in (own, far)], axis=0)
        for k in range(2)
    ]


def attention_kernel(query, own, far, seen, valid, side, *rest):
    out_own, out_first, out_second, attended, log_total, near, peer = rest
    keys, values = keys_values(own[...], far[...])
    mask = seen[...] > 0.0
    real = valid[...]
    lanes = lax.broadcasted_iota(jnp.int32, (PAIR_ROWS, 128), 1)
    logs = jnp.zeros((PAIR_ROWS, 128), F32)
    for h in range(Q_HEADS):
        columns = slice(h * HEAD, (h + 1) * HEAD)
        scores = dot_across(query[:, columns], keys) * HEAD ** (-0.5)
        scores = jnp.where(mask, scores, MASKED_SCORE)
        top = jnp.where(real > 0.0, jnp.max(scores, axis=1, keepdims=True), 0.0)
        exponent = jnp.where(mask, jnp.exp(scores - top), 0.0)
        denominator = jnp.sum(exponent, axis=1, keepdims=True) + (1.0 - real)
        attended[:, columns] = dot((exponent / denominator).astype(BF16), values).astype(BF16)
        logs = jnp.where(lanes == h, top + jnp.log(denominator), logs)
    log_total[...] = logs
    first, second = attended[:, :CORE_ROWS], attended[:, CORE_ROWS:]
    straight = side[0, 0] == 0
    left = jnp.where(straight, first, second)
    right = jnp.where(straight, second, first)
    for k, x in enumerate(
        (dot(attended[...], out_own[...]), dot(left, out_first[...]) + dot(right, out_second[...]))
    ):
        columns = slice(k * HALF, (k + 1) * HALF)
        near[:, columns] = x[:QUARTER]
        peer[:, columns] = x[QUARTER:].astype(BF16)


def attention_forward(parts, geometry, meanwhile):
    _, _, seen, valid = geometry
    query, pair = rotate_parts(parts, geometry)
    far = over_col(pair)
    pair, far, (side, *out_parts) = meanwhile(pair, far)
    side = jnp.broadcast_to(jnp.asarray(side, jnp.int32), (1, 1))
    smem = pl.BlockSpec(memory_space=pltpu.SMEM)
    attended, log_total, near, peer = local_call(
        attention_kernel,
        [
            ((PAIR_ROWS, Q_HEADS * HEAD), BF16),
            ((PAIR_ROWS, 128), F32),
            (BLOCK, F32),
            (BLOCK, BF16),
        ],
        [query, pair, far, seen, valid, side, *out_parts],
        "attention_forward",
        {5: smem},
    )
    return ((query, pair, far, log_total, attended), (near, over_row(peer)))


def attention_back_kernel(cosine, sine, seen, upstream, peer, out_own, out_other, *rest):
    query, own, far, log_total, out_grad, query_grad, pair_own, pair_far = rest
    out_grad[:QUARTER, :] = upstream[...]
    out_grad[QUARTER:, :] = peer[...]
    keys, values = keys_values(own[...], far[...])
    mask = seen[...] > 0.0
    attended_grad = dot_across(out_grad[:, :HALF], out_own[...])
    attended_grad = (attended_grad + dot_across(out_grad[:, HALF:], out_other[...])).astype(BF16)
    key_grad = jnp.zeros((TOK_DP, HEAD), F32)
    value_grad = jnp.zeros((TOK_DP, HEAD), F32)
    for h in range(Q_HEADS):
        columns = slice(h * HEAD, (h + 1) * HEAD)
        head, grad = query[:, columns], attended_grad[:, columns]
        scores = dot_across(head, keys) * HEAD ** (-0.5)
        shift = log_total[:, h : h + 1]
        weights = jnp.where(mask, jnp.exp(scores - shift), 0.0)
        weight_grad = dot_across(grad, values)
        value_grad += dot_down(weights.astype(BF16), grad)
        inner = jnp.sum(weight_grad * weights, axis=1, keepdims=True)
        score_grad = (weights * (weight_grad - inner)).astype(BF16)
        key_grad += dot_down(score_grad, head)
        part = turn(dot(score_grad, keys) * HEAD ** (-0.5), cosine[...], -sine[...])
        query_grad[:, columns] = part.astype(BF16)
    key_grad = key_grad * HEAD ** (-0.5)
    pair_own[:, :HEAD] = key_grad[:PAIR_ROWS]
    pair_own[:, HEAD:] = value_grad[:PAIR_ROWS]
    pair_far[:, :HEAD] = key_grad[PAIR_ROWS:].astype(BF16)
    pair_far[:, HEAD:] = value_grad[PAIR_ROWS:].astype(BF16)


def input_grad_kernel(cosine, sine, query_grad, own, far, inputs, weight, *rest):
    qkv_grad, near, peer, grad_gain = rest
    pair = own[...] + far[...].astype(F32)
    qkv_grad[:, : Q_HEADS * HEAD] = query_grad[...]
    key_grad = turn(pair[:, :HEAD], cosine[...], -sine[...])
    qkv_grad[:, Q_HEADS * HEAD : QKV - HEAD] = key_grad.astype(BF16)
    qkv_grad[:, QKV - HEAD :] = pair[:, HEAD:].astype(BF16)
    partial = dot_across(qkv_grad[...], weight[...])
    near[...] = partial[:QUARTER]
    peer[...] = partial[QUARTER:].astype(BF16)
    grad_gain[...] = jnp.sum(inputs[...].astype(F32) * partial, axis=0, keepdims=True)


def attention_grads_kernel(inputs, attended, qkv_grad, out_grad, order, send, keep):
    def product(left, right, column):
        turned_left = dot_across(order[...], left).astype(BF16)
        result = dot(turned_left, right).astype(BF16)
        columns = slice(column, column + result.shape[1])
        send[:, columns] = result[:CORE_ROWS]
        keep[:, columns] = result[CORE_ROWS:]

    for k in range(2):
        half = slice(k * HALF, (k + 1) * HALF)
        product(inputs[:, half], qkv_grad[...], k * (QKV + HALF))
        product(attended[...], out_grad[:, half], k * (QKV + HALF) + QKV)


def attention_grads(*operands):
    return pl.pallas_call(
        attention_grads_kernel,
        out_shape=[jax.ShapeDtypeStruct((CORE_ROWS, 2 * (QKV + HALF)), BF16)] * 2,
        compiler_params=pltpu.CompilerParams(vmem_limit_bytes=VMEM_LIMIT),
        cost_estimate=pl.CostEstimate(
            flops=4 * QUARTER * HALF * 6 * HALF, bytes_accessed=10 << 20, transcendentals=0
        ),
        name="attention_weight_grads",
    )(*operands)


def attention_backward(upstream, cache, gain, weights, geometry, order, meanwhile, finish):
    cosine, sine, seen, _ = geometry
    stream, inv_rms, inputs, query, pair, far, log_total, attended = cache
    gathered, out_weight = weights
    out_grads = meanwhile(gather_two(upstream.astype(BF16)))
    width = Q_HEADS * HEAD
    out_grad, query_grad, pair_own, pair_far = local_call(
        attention_back_kernel,
        [
            ((PAIR_ROWS, D), BF16),
            ((PAIR_ROWS, width), BF16),
            ((PAIR_ROWS, 2 * HEAD), F32),
            ((PAIR_ROWS, 2 * HEAD), BF16),
        ],
        [cosine, sine, seen, *out_grads, *out_weight, query, pair, far, log_total],
        "attention_backward",
    )
    qkv_grad, near, peer, grad_gain = local_call(
        input_grad_kernel,
        [((PAIR_ROWS, QKV), BF16), (BLOCK, F32), (BLOCK, BF16), ((1, D), F32)],
        [cosine, sine, query_grad, pair_own, over_col(pair_far), inputs, gathered],
        "attention_input_grad",
        {6: pl.BlockSpec((D, QKV), lambda j: (0, 0))},
    )
    parts = (near, over_row(peer))
    packed = attention_grads(inputs, attended, qkv_grad, out_grad, order)
    parts = finish(parts, packed, grad_gain[0] / gain)
    return norm_back(upstream, total(parts), stream, inv_rms, gain)


def send_blocks(values, own, row, col, both):
    own[...] = values[:QUARTER, :]
    row[...] = values[QUARTER : 2 * QUARTER, :].astype(BF16)
    for k, target in ((2, col), (3, both)):
        block = values[k * QUARTER : (k + 1) * QUARTER, :].astype(BF16)
        target[:, :HALF] = block[:, HALF:]
        target[:, HALF:] = block[:, :HALF]


def join_blocks(blocks, target):
    for k, block in enumerate(blocks):
        target[k * QUARTER : (k + 1) * QUARTER, :] = block[...]


def share_of(share, step, k):
    lanes = lax.broadcasted_iota(jnp.int32, share.shape, 1)
    mine = lanes == lax.axis_index("col") * MINE + (step * PARTS + k) // 3
    return (mine, jnp.sum(jnp.where(mine, share, 0.0), axis=1, keepdims=True))


def forward_kernel(x0, x1, x2, x3, chosen, router, wg, wu, wd, *rest):
    inputs, gate, up, hidden, share, own, row, col, both, total_ref = rest
    step = pl.program_id(0)

    @pl.when(step == 0)
    def _():
        join_blocks((x0, x1, x2, x3), inputs)
        logits = dot_across(inputs[...], router[...])
        picked = chosen[...] > 0.0
        top = jnp.max(jnp.where(picked, logits, MASKED_SCORE), axis=1, keepdims=True)
        exponent = jnp.where(picked, jnp.exp(jnp.where(picked, logits - top, 0.0)), 0.0)
        share[...] = exponent / jnp.sum(exponent, axis=1, keepdims=True)

    x = inputs[...]
    gate_value = dot(x, wg[...])
    up_value = dot(x, wu[...])
    gate[...] = gate_value
    up[...] = up_value
    low = (gate_value / (1.0 + jnp.exp(-gate_value))) * up_value
    for k in range(PARTS):
        part = slice(k * 128, (k + 1) * 128)
        hidden[:, part] = (share_of(share[...], step, k)[1] * low[:, part]).astype(BF16)
    result = dot(hidden[...], wd[...])

    @pl.when(step == 0)
    def _():
        total_ref[...] = result

    @pl.when(step > 0)
    def _():
        total_ref[...] += result

    @pl.when(step == STEPS - 1)
    def _():
        send_blocks(total_ref[...], own, row, col, both)


def weight_specs():
    return [
        pl.BlockSpec((D, WIDE), lambda j: (0, j)),
        pl.BlockSpec((D, WIDE), lambda j: (0, STEPS + j)),
        pl.BlockSpec((WIDE, D), lambda j: (j, 2)),
    ]


COST = pl.CostEstimate(flops=6 * TOK_DP * D * D, bytes_accessed=24 << 20, transcendentals=TOK_DP * D)


def send_four(blocks):
    own, row, col, both = blocks
    return (own, over_row(row), over_col(col), over_both(both))


def expert_forward(stream, gain, router, weights, chosen, meanwhile):
    inv_rms, normed = normalize(stream, gain)
    gathered = meanwhile(gather_four(normed))
    weights = weights[0]
    out = pl.pallas_call(
        forward_kernel,
        grid=(STEPS,),
        in_specs=[whole(BLOCK)] * 4 + [whole(LANES), whole((128, D))] + weight_specs(),
        out_specs=[whole(ALL), SLAB, SLAB, SLAB, whole(LANES)] + [whole(BLOCK)] * 4,
        out_shape=[
            jax.ShapeDtypeStruct(ALL, BF16),
            jax.ShapeDtypeStruct(ALL, F32),
            jax.ShapeDtypeStruct(ALL, F32),
            jax.ShapeDtypeStruct(ALL, BF16),
            jax.ShapeDtypeStruct(LANES, F32),
            jax.ShapeDtypeStruct(BLOCK, F32),
        ]
        + [jax.ShapeDtypeStruct(BLOCK, BF16)] * 3,
        scratch_shapes=[pltpu.VMEM(ALL, F32)],
        compiler_params=pltpu.CompilerParams(vmem_limit_bytes=VMEM_LIMIT),
        cost_estimate=COST,
        name="experts_forward",
    )(*gathered, chosen, router, weights, weights, weights)
    inputs, gate, up, hidden, share, own, row, col, both = out
    return ((stream, inv_rms, inputs, gate, up, share, hidden), (own, row, col, both))


def backward_kernel(y0, y1, y2, y3, gate, up, share, router, wg, wu, wd, *rest):
    grads, gate_grad, up_grad, logits_grad, own, row, col, both, total_ref, share_grad = rest
    step = pl.program_id(0)

    @pl.when(step == 0)
    def _():
        join_blocks((y0, y1, y2, y3), grads)
        share_grad[...] = jnp.zeros_like(share_grad)

    hidden_grad = dot_across(grads[...], wd[...])
    gate_value, up_value = gate[...], up[...]
    sigmoid = 1.0 / (1.0 + jnp.exp(-gate_value))
    silu = gate_value * sigmoid
    weighed = hidden_grad * silu * up_value
    slope = hidden_grad * up_value * sigmoid * (1.0 + gate_value * (1.0 - sigmoid))
    through_up = hidden_grad * silu
    for k in range(PARTS):
        part = slice(k * 128, (k + 1) * 128)
        lanes, mine = share_of(share[...], step, k)
        share_grad[...] += jnp.where(
            lanes, jnp.sum(weighed[:, part], axis=1, keepdims=True), 0.0
        )
        gate_grad[:, part] = (mine * slope[:, part]).astype(BF16)
        up_grad[:, part] = (mine * through_up[:, part]).astype(BF16)
    low_gate, low_up = gate_grad[...], up_grad[...]
    result = dot_across(low_gate, wg[...]) + dot_across(low_up, wu[...])

    @pl.when(step == 0)
    def _():
        total_ref[...] = result

    @pl.when(step > 0)
    def _():
        total_ref[...] += result

    @pl.when(step == STEPS - 1)
    def _():
        part = share_grad[...]
        inner = jnp.sum(share[...] * part, axis=1, keepdims=True)
        exact = share[...] * (part - inner)
        high = exact.astype(BF16)
        low = (exact - high.astype(F32)).astype(BF16)
        logits_grad[:, :128] = high
        logits_grad[:, 128:] = low
        through = dot(high, router[...]) + dot(low, router[...])
        send_blocks(total_ref[...] + through, own, row, col, both)


def grads_kernel(inputs, hidden, gate_grad, up_grad, out_grad, order_x, order_h, *rest):
    *arrived, packed, turned_ref = rest
    step = pl.program_id(0)

    for at in range(6):

        @pl.when(step == at)
        def _(at=at):
            if at in (0, 2):
                turned_ref[...] = dot_across(order_x[...], inputs[...]).astype(BF16)
            if at >= 4:
                turned_ref[...] = dot_across(order_h[...], hidden[...]).astype(BF16)
            right = (gate_grad, up_grad, gate_grad, up_grad, out_grad, out_grad)[at]
            result = dot(turned_ref[...], right[...])
            for x in arrived:
                result = result + x[...].astype(F32)
            packed[...] = result.astype(packed.dtype)


def weight_grads(inputs, hidden, gate_grad, up_grad, out_grad, orders, half, arrived):
    def left(place):
        return pl.BlockSpec((TOK_DP, HALF), lambda j: (0, place(j)))

    tile = pl.BlockSpec((CORE_ROWS, D), lambda j: (0, j))
    rows = pl.BlockSpec((CORE_ROWS, HALF), lambda j: (half, 0))
    return pl.pallas_call(
        grads_kernel,
        grid=(6,),
        in_specs=[
            left(lambda j: jnp.minimum(j // 2, 1)),
            left(lambda j: jnp.maximum(j - 4, 0)),
        ]
        + [whole(ALL)] * 3
        + [rows] * 2
        + [tile] * len(arrived),
        out_specs=tile,
        out_shape=jax.ShapeDtypeStruct((CORE_ROWS, 6 * D), F32 if arrived else BF16),
        scratch_shapes=[pltpu.VMEM((CORE_ROWS, TOK_DP), BF16)],
        compiler_params=pltpu.CompilerParams(vmem_limit_bytes=VMEM_LIMIT),
        cost_estimate=pl.CostEstimate(
            flops=4 * TOK_DP * D * D, bytes_accessed=24 << 20, transcendentals=0
        ),
        name="expert_weight_grads",
    )(inputs, hidden, gate_grad, up_grad, out_grad, *orders, *arrived)


def expert_backward(upstream, cache, gain, router, weights, orders, gathered, settle):
    stream, inv_rms, inputs, gate, up, share, hidden = cache
    out = pl.pallas_call(
        backward_kernel,
        grid=(STEPS,),
        in_specs=[whole(BLOCK)] * 4
        + [SLAB, SLAB, whole(LANES), whole((128, D))]
        + weight_specs(),
        out_specs=[whole(ALL), SLAB, SLAB, whole((TOK_DP, 256))] + [whole(BLOCK)] * 4,
        out_shape=[jax.ShapeDtypeStruct(ALL, BF16)] * 3
        + [jax.ShapeDtypeStruct((TOK_DP, 256), BF16), jax.ShapeDtypeStruct(BLOCK, F32)]
        + [jax.ShapeDtypeStruct(BLOCK, BF16)] * 3,
        scratch_shapes=[pltpu.VMEM(ALL, F32), pltpu.VMEM(LANES, F32)],
        compiler_params=pltpu.CompilerParams(vmem_limit_bytes=VMEM_LIMIT),
        cost_estimate=COST,
        name="experts_backward",
    )(*gathered, gate, up, share, router, weights, weights, weights)
    out_grad, gate_grad, up_grad, logits_grad, own, row, col, both = out
    parts = settle(send_four((own, row, col, both)))
    operands = (inputs, hidden, gate_grad, up_grad, out_grad, orders)
    packed = weight_grads(*operands, 0, [])
    packed, *parts = tied(packed, *parts)
    arrived = over_dp(packed, lambda i: i ^ 1)
    normed_grad = total(parts)
    router_grad = dot_down(logits_grad, inputs)
    router_grad = router_grad[:EXPERTS] + router_grad[128 : 128 + EXPERTS]
    grad_stream = norm_back(upstream, normed_grad, stream, inv_rms, gain)
    grad_gain = jnp.sum(normed_grad * stream * inv_rms, axis=0)


    def finish(*values):
        return tied(weight_grads(*operands, 1, [arrived]), *values)

    return (grad_stream, finish, grad_gain, router_grad)


def exchange_orders(data_index):
    along_x, along_z, core = data_index // 8, data_index // 2 % 4, data_index % 2
    rows = np.arange(HALF, dtype=np.int32)
    block, inner = rows // 24, rows % 24
    side = jnp.where(block < 16, 1 - core, core)
    straight = block % 16 * 2 + side
    target = (along_x + block // 4) % 4 * 8 + (along_z + block) % 4 * 2 + side
    source = jnp.arange(HALF, dtype=jnp.int32)
    by_core, units, by_steps = [
        (x[:, None] == source[None, :]).astype(BF16)
        for x in (
            straight * 24 + inner,
            inner // 12 * FF + straight * 12 + inner % 12,
            target * 24 + inner,
        )
    ]
    return ([by_core, units], by_steps)


def shift_x(x, k):
    return over_dp(x, lambda i: (i // 8 + k) % 4 * 8 + i % 8)


def shift_z(x, k):
    return over_dp(x, lambda i: i // 8 * 8 + (i // 2 % 4 + k) % 4 * 2 + i % 2)


def sum_pairs(*sets):
    got = [over_dp(x[0], lambda i: i ^ 1) for x in sets]
    return [total((x[1], y)).astype(BF16) for x, y in zip(sets, got)]


def sum_round(values, shifts):
    rows = values[0].shape[0] // 4
    blocks = [[x[k * rows : (k + 1) * rows] for k in range(4)] for x in values]
    got = [
        [x[0]] + [shift(x[k], k) for k in range(1, 4)] for x, shift in zip(blocks, shifts)
    ]
    return [total(x).astype(BF16) for x in got]


def sum_over_cores(values):
    return lax.psum_scatter(
        values, "dp", scatter_dimension=0, tiled=True, axis_index_groups=SAME_CORE
    )


def sum_everywhere(values):
    values = values + over_row(values)
    for step in (1, 8, 16, 2, 4):
        values = values + over_dp(values, lambda i, step=step: i ^ step)
    return values


def place(expert_own, expert_other, attention, column):
    wide = 2 * D
    far = [expert_other[:, :wide]] if expert_other is not None else []
    far += [other for _, other in attention]
    if expert_own is not None:
        far += [expert_own[:, wide:][:, HALF:], expert_other[:, wide:][:, HALF:]]
    got = over_col(jnp.concatenate(far, axis=1))
    ends, offset = [], 0
    for x in far:
        ends.append(got[:, offset : offset + x.shape[1]])
        offset += x.shape[1]
    results = []
    if expert_own is not None:
        gate_up = [
            jnp.stack([block[:, e * FF : (e + 1) * FF] for e in range(2 * MINE)])
            for block in (expert_own[:, :wide], ends[0])
        ]
        near = [x[:, wide : wide + HALF] for x in (expert_own, expert_other)]
        down = [
            jnp.stack([x[k * 12 : (k + 1) * 12] for x in pair for k in range(2)])
            for pair in (near, ends[-2:])
        ]
        results = [
            by_col(column, gate_up[0][k * MINE : (k + 1) * MINE], gate_up[1][k * MINE : (k + 1) * MINE], 0)
            for k in range(2)
        ] + [by_col(column, *down, 0)]
        results = [x.astype(F32) for x in results]
        ends = ends[1:-2]
    sums = [total((own, x)) for (own, _), x in zip(attention, ends)]
    return (results, [(x[:, :QKV], x[:, QKV:]) for x in sums])


def shards(
    tokens,
    cotangent,
    norm_gains,
    query_weight,
    key_weight,
    value_weight,
    output_weight,
    router_weight,
    gate_weight,
    up_weight,
    down_weight,
    expert_ids,
    seq_lengths,
    seq_owner,
):
    data_index = lax.axis_index("dp")
    row = lax.axis_index("row")
    column = lax.axis_index("col")
    core = data_index % 2
    weights = (
        gate_weight, up_weight, down_weight, query_weight, key_weight, value_weight, output_weight
    )

    squares = jnp.sum(jnp.square(tokens.astype(F32)), axis=1)
    small = jnp.concatenate(
        [
            norm_gains.reshape(2 * LAYERS, HALF).astype(F32),
            router_weight.transpose(0, 2, 1).reshape(LAYERS * EXPERTS, HALF).astype(F32),
            jnp.pad(squares, (0, HALF - 2 * QUARTER))[None],
        ],
        axis=0,
    )
    small, index = tied(small, data_index)
    small_far = over_col(small)
    own, other, qkv_own, out_own, out_send, *attention_own = take_pieces(0, index, weights, True)
    squares = small[-1, : 2 * QUARTER] + small_far[-1, : 2 * QUARTER]
    inv_rms = lax.rsqrt(squares / D + EPSILON)[:, None]
    normed = (tokens.astype(F32) * inv_rms * small[0]).astype(BF16)
    normed_pair = (normed, over_row(normed))
    piece = expert_piece(own, over_col(other), data_index)
    piece, out_send, *normed_pair = tied(piece, out_send, *normed_pair)
    expert_parts = [gather_all(piece)]
    near, away = [
        jnp.concatenate([half_of(x, side, 0) for x in normed_pair], axis=0)
        for side in (column, 1 - column)
    ]
    partial = dot(jnp.concatenate([near, away], axis=0), qkv_own)
    qkv_far = over_col(partial[2 * QUARTER :].astype(BF16))
    out_sent = over_col(out_send)
    qkv = partial[: 2 * QUARTER]
    qkv, data_index, seq_lengths, expert_ids = tied(qkv, data_index, seq_lengths, expert_ids)
    loaded = take_pieces(1, data_index, weights, False)
    small = jnp.concatenate([small[:-1], small_far[:-1]], axis=1)
    gains = small[: 2 * LAYERS].reshape(LAYERS, 2, D)
    routers = small[2 * LAYERS :].reshape(LAYERS, EXPERTS, D).astype(BF16)
    routers = jnp.pad(routers, ((0, 0), (0, 128 - EXPERTS), (0, 0)))

    segment, position, valid_row, places = segments(seq_lengths, seq_owner, data_index)
    starts = (
        row * 256 + column * QUARTER,
        (1 - row) * 256 + column * QUARTER,
        row * 256 + (1 - column) * QUARTER,
        (1 - row) * 256 + (1 - column) * QUARTER,
    )

    def arranged(x, axis=0):
        return jnp.concatenate(
            [lax.dynamic_slice_in_dim(x, s, QUARTER, axis=axis) for s in starts], axis=axis
        )

    segment, position, places = arranged(segment), arranged(position), arranged(places)
    valid_row = arranged(valid_row.astype(jnp.int32)) > 0
    ids = arranged(expert_ids, 1)
    lanes = jnp.arange(128, dtype=jnp.int32)
    chosen = jnp.any(ids[:, :, :, None] == lanes, axis=2).astype(F32)
    rows = 2 * QUARTER
    frequency = jnp.power(
        ROPE_THETA, jnp.arange(HEAD // 2, dtype=F32) * (-2.0 / HEAD)
    )
    angle = position[:rows].astype(F32)[:, None] * frequency[None, :]
    seen_mask = (
        (segment[:rows, None] == segment[None, :])
        & (places[None, :] <= places[:rows, None])
        & valid_row[:rows, None]
    )
    cosine, sine = jnp.cos(angle), jnp.sin(angle)
    geometry = (
        jnp.concatenate([cosine, cosine], axis=1),
        jnp.concatenate([-sine, sine], axis=1),
        seen_mask.astype(F32),
        valid_row[:rows].astype(F32)[:, None],
    )

    by_core, by_steps = exchange_orders(data_index)
    attention_other = [None] * LAYERS

    def first_out(pair, pair_far):
        nonlocal out_sent, by_core, by_steps, routers, chosen, far, loaded
        values = tied(
            pair, pair_far, out_sent, tokens, attention_own[1], by_steps, routers, chosen,
            *by_core, *loaded
        )
        pair, pair_far, out_sent, rest, attention_own[1], by_steps, routers, chosen = values[:8]
        by_core, loaded = values[8:10], list(values[10:])
        attention_other[1] = over_col(attention_own[1])
        far = to_quarter(rest, column)[:, HALF:]
        return (pair, pair_far, (core, out_own, out_sent, over_dp(out_sent, lambda i: i ^ 1)))

    far = None
    cache, parts = attention_forward([qkv, qkv_far], geometry, first_out)
    stream = jnp.concatenate([half_of(tokens, column, 0), far], axis=1).astype(F32)
    quarter_rms = half_of(inv_rms, column, 0)
    far_normed = (far.astype(F32) * quarter_rms * gains[0, 0, HALF:]).astype(BF16)
    attention_caches = [(stream, quarter_rms, None) + cache]
    stream = stream + total(parts)
    second_attention = attention_piece(attention_own[1], attention_other[1], data_index)

    def load_second(gathered):
        nonlocal second_attention, upstream
        upstream = to_quarter(cotangent, column)
        second_attention, expert_parts[0], loaded[1], upstream, *gathered = tied(
            second_attention, expert_parts[0], loaded[1], upstream, *gathered
        )
        loaded.append(over_col(loaded[1]))
        return gathered

    upstream = None
    expert_cache, sends = expert_forward(
        stream, gains[0, 1], routers[0], expert_parts, chosen[0], load_second
    )
    stream = stream + total(send_four(sends))
    caches = [expert_cache]
    second_weights = attention_whole(gather_all(second_attention))
    second_piece = expert_piece(loaded[0], loaded[2], data_index)

    inv_rms, normed = normalize(stream, gains[1, 0])
    inputs = jnp.concatenate(gather_two(normed), axis=0)
    qkv, second_piece = tied(dot(inputs, second_weights[0][:, :QKV]), second_piece)
    expert_parts.append(gather_all(second_piece))
    first_inputs = []

    def start_back(pair, pair_far):
        pair, pair_far, attention_own[0], source = tied(
            pair, pair_far, attention_own[0], far_normed
        )
        attention_other[0] = over_col(attention_own[0])
        first_inputs.append(source)
        first_inputs.append(over_row(source))
        out_own, out_other = second_weights[1]
        return (pair, pair_far, (0, out_own, out_other[:CORE_ROWS], out_other[CORE_ROWS:]))

    cache, parts = attention_forward([qkv], geometry, start_back)
    attention_caches.append((stream, inv_rms, inputs) + cache)
    inputs = jnp.concatenate([near, jnp.concatenate(first_inputs, axis=0)], axis=1)
    attention_caches[0] = attention_caches[0][:2] + (inputs,) + attention_caches[0][3:]
    stream = stream + total(parts)
    first_attention = attention_piece(attention_own[0], attention_other[0], data_index)

    def load_last(gathered):
        nonlocal first_attention, upstream
        first_attention, expert_parts[1], upstream, *gathered = tied(
            first_attention, expert_parts[1], upstream, *gathered
        )
        return gathered

    expert_cache, sends = expert_forward(
        stream, gains[1, 1], routers[1], expert_parts[1:], chosen[1], load_last
    )
    caches.append(expert_cache)
    first_whole = gather_all(first_attention)
    gathered = gather_four(upstream)

    upstream, finish_second, expert_gain, router_grad = expert_backward(
        upstream.astype(F32),
        caches[1],
        gains[1, 1],
        routers[1],
        expert_parts[1],
        by_core,
        gathered,
        lambda x: x,
    )
    smalls = [None, expert_gain[None], router_grad]
    waiting = None

    def start_first(out_grads):
        nonlocal first_whole, expert_sum
        expert_sum, first_whole, *out_grads = finish_second(first_whole, *out_grads)
        expert_sum = sum_over_cores(expert_sum)
        return out_grads

    expert_sum = None

    def keep(parts, packed, attention_gain):
        nonlocal waiting
        waiting = packed
        smalls[0] = attention_gain[None]
        return parts

    upstream = attention_backward(
        upstream,
        attention_caches[1],
        gains[1, 0],
        second_weights,
        geometry,
        by_steps,
        start_first,
        keep,
    )
    gathered = gather_four(upstream.astype(BF16))
    second_sum = sum_pairs(waiting)
    second_sum, *gathered = tied(*second_sum, *gathered)
    second_sum = sum_round([second_sum], (shift_x,))

    def settle(parts):
        nonlocal second_sum
        second_sum, *parts = tied(*second_sum, *parts)
        second_sum = sum_round([second_sum], (shift_z,))[0]
        return parts

    upstream, finish_first, expert_gain, router_grad = expert_backward(
        upstream,
        caches[0],
        gains[0, 1],
        routers[0],
        expert_parts[0],
        by_core,
        gathered,
        settle,
    )
    first_weights = attention_whole(first_whole)
    first_sum = None
    last = None

    def start_sum(out_grads):
        nonlocal sends, first_sum, expert_sum
        values = finish_first(expert_sum, *sends, *out_grads)
        first_sum, expert_sum, sends, out_grads = values[0], values[1], values[2:6], values[6:]
        first_sum = sum_over_cores(first_sum)
        return out_grads

    def keep_last(parts, packed, attention_gain):
        nonlocal last, second_sum
        *last, second_sum, own, peer = tied(*packed, second_sum, *parts)
        last = sum_pairs(last)
        smalls[:0] = [attention_gain[None], expert_gain[None], router_grad]
        return (own, peer)

    upstream = attention_backward(
        upstream,
        attention_caches[0],
        gains[0, 0],
        first_weights,
        geometry,
        by_steps,
        start_sum,
        keep_last,
    )
    block_output = from_quarter((stream + total(send_four(sends))).astype(BF16), column)
    small = jnp.concatenate(smalls, axis=0)
    small = small[:, :HALF] + over_col(small[:, HALF:])
    small = sum_everywhere(small).reshape(LAYERS, 2 + EXPERTS, HALF)
    small, expert_sum, last = tied(small, expert_sum, *last)

    def columns(values):
        return [
            jnp.concatenate(
                [
                    values[:, k * 2 * D : (k + 1) * 2 * D],
                    values[:, (4 + k) * D : (5 + k) * D],
                ],
                axis=1,
            ).astype(BF16)
            for k in range(2)
        ]

    last = sum_round([last], (shift_x,))
    second, _ = place(*columns(expert_sum), [], column)
    last, *second = tied(*last, *second)
    last = sum_round([last], (shift_z,))[0]
    half = QKV + HALF
    first, ((qkv_second, out_second), (qkv_first, out_first)) = place(
        *columns(first_sum), [(x[:, :half], x[:, half:]) for x in (second_sum, last)], column
    )
    grad_tokens = from_quarter(upstream.astype(BF16), column)

    grad_gains = small[:, :2]
    grad_router = small[:, 2:].transpose(0, 2, 1)

    qkv_grad = jnp.stack([qkv_first, qkv_second])
    out_grad = jnp.stack([out_first, out_second])
    grad_gate, grad_up, grad_down = [jnp.stack([x, y]) for x, y in zip(first, second)]
    width = Q_HEADS * HEAD
    return (
        block_output,
        grad_tokens,
        grad_gains,
        qkv_grad[:, :, :width],
        qkv_grad[:, :, width : width + HEAD],
        qkv_grad[:, :, width + HEAD :],
        out_grad,
        grad_router,
        grad_gate,
        grad_up,
        grad_down,
    )


def solution(mesh):
    in_specs = (
        P(("dp", "row"), "col"),
        P(("dp", "row"), "col"),
        P(None, None, "col"),
        P(None, "col", "row"),
        P(None, "col", "row"),
        P(None, "col", "row"),
        P(None, "row", "col"),
        P(None, "col", None),
        P(None, None, "col", "row"),
        P(None, None, "col", "row"),
        P(None, None, "row", "col"),
        P(None, "dp", None),
        P(),
        P(),
    )
    out_specs = (
        P(("dp", "row"), "col"),
        P(("dp", "row"), "col"),
        P(None, None, "col"),
        P(None, ("col", "dp"), "row"),
        P(None, ("col", "dp"), "row"),
        P(None, ("col", "dp"), "row"),
        P(None, ("row", "dp"), "col"),
        P(None, "col", None),
        P(None, None, ("col", "dp"), "row"),
        P(None, None, ("col", "dp"), "row"),
        P(None, None, ("row", "dp"), "col"),
    )
    return jax.shard_map(shards, mesh=mesh, in_specs=in_specs, out_specs=out_specs, check_vma=False)
```

time: 847 us -> 695 us (0.82)
  Pallas kernels: 0 us -> 160 us
  matrix products: 125 us -> 6.3 us
  waiting for transfers between devices: 364 us -> 277 us
  other arithmetic: 116 us -> 47.1 us
  starting transfers between devices: 116 us -> 95.2 us
  local copies, waits for them, and re-layouts: 98.2 us -> 81.4 us
    reduce_scatter x4 -> x0, waiting for transfers between devices: 169 us -> none  [sum_over_dp(): return lax.psum_scatter(packed, 'dp', scatter_dimension=0, tiled=True)]
    pallas_call x0 -> x20, Pallas kernels: none -> 160 us  [the longest x4 48.4 us: weight_grads(): pl.pallas_call(grads_kernel, grid=(6,), in_specs=[left(lambda j: jnp.mini...]
    ppermute x13 -> x22, waiting for transfers between devices: 18.9 us -> 75.2 us  [over_dp(): return lax.ppermute(x, 'dp', [(i, target(i)) for i in range(N_DP)])]
    dot_general x14 -> x0, matrix products: 52.3 us -> none  [dot_across(): return lax.dot_general(a, b, ACROSS, preferred_element_type=F32)]
    dot_general x14 -> x2, matrix products: 39.4 us -> 5.12 us  [dot(): return jnp.dot(a, b, preferred_element_type=F32)]
    dot_general x22 -> x2, matrix products: 33.6 us -> 1.18 us  [dot_down(): return lax.dot_general(a, b, DOWNWARD, preferred_element_type=F32)]
    unnamed x377 -> x363, local copies, waits for them, and re-layouts: 18.8 us -> 48 us
    concatenate x17 -> x20, other arithmetic: 35.2 us -> 8.41 us  [the longest x4 1.63 us: turned(): return jnp.concatenate([x[:, HALF:], x[:, :HALF]], axis=1)]
  transfers between devices with their start and end apart: 76 -> 80, of which waited for: 51 -> 44; matrix products, arithmetic and copies ran while one was open for 31% -> 11% of each run, Pallas kernels for 0% -> 23%
where the time goes in v3:
time: 695 us; the launch traced here: 684 us
  waiting for transfers between devices  277 us (40%)
  Pallas kernels  160 us (23%)
  starting transfers between devices  95.2 us (14%)
  local copies, waits for them, and re-layouts  81.4 us (12%)
  other arithmetic  47.1 us (7%)
  between operations  16.9 us (2%)
    ppermute x26, waiting for transfers between devices, over_col(): return lax.ppermute(x, 'col', SWAP)  96.1 us
    ppermute x22, waiting for transfers between devices, over_dp(): return lax.ppermute(x, 'dp', [(i, target(i)) for i in range(N_DP)])  75.2 us
    ppermute x18, waiting for transfers between devices, over_row(): return lax.ppermute(x, 'row', SWAP)  59.4 us
    ppermute x26, starting transfers between devices, over_col(): return lax.ppermute(x, 'col', SWAP)  49.4 us
    pallas_call x4, Pallas kernels, weight_grads(): pl.pallas_call(grads_kernel, grid=(6,), in_specs=[left(lambda j: jnp.mini...  48.4 us
    unnamed x363, local copies, waits for them, and re-layouts  48 us
    pallas_call x8, Pallas kernels, local_call(): pl.pallas_call(kernel, grid=(1,), in_specs=[specs.get(k) or whole(x.shape...  32.4 us
    pallas_call x2, Pallas kernels, expert_backward(): pl.pallas_call(backward_kernel, grid=(STEPS,), in_specs=[whole(BLOCK)] *...  31.9 us
  transfers between devices with their start and end apart: 80, of which 44 were waited for; matrix products, arithmetic and copies ran while one was open for 11% of the time, Pallas kernels for 23%

profile of v3, /device:TPU:6, one launch (start us, length us, event | category | flops | bytes accessed | tf_op | source)
XLA Modules:
  0.0 683.9 jit_solution(16625858139948798873)
XLA Ops:
  20.5 9.9 %collective-permute-done.1 = f32[21,768]{1,0:T(8,128)S(1)} collective-permute-done((f32[21,768]{1,0:T(8,128)S(1)}, f32[21,768]{1,0:T(8,128)S(1)}, u32[]{:S(2)}, u32[]{:S(2)}) %collective-permute-start.1) | collective-permute-done | bytes 64544 | tf_op jit(solution)/shard_map/ppermute | solution.py:66
  33.7 7.6 %collective-permute-done.2 = bf16[256,768]{1,0:T(8,128)(2,1)} collective-permute-done((bf16[256,768]{1,0:T(8,128)(2,1)S(1)}, bf16[256,768]{1,0:T(8,128)(2,1)}, u32[]{:S(2)}, u32[]{:S(2)}) %collective-permute-start.2) | collective-permute-done | bytes 393248 | tf_op jit(solution)/shard_map/ppermute | solution.py:62
  63.9 8.8 %collective-permute-done.3.rest_1_ = bf16[256,1024]{1,0:T(8,128)(2,1)} collective-permute-done((bf16[256,1024]{1,0:T(8,128)(2,1)}, bf16[256,1024]{1,0:T(8,128)(2,1)}, u32[]{:S(2)}, u32[]{:S(2)}) %collective-permute-start.3) | collective-permute-done | bytes 524320 | tf_op jit(solution)/shard_map/ppermute | solution.py:66
  94.5 7.2 %attention_forward.2 = (bf16[256,768]{1,0:T(8,128)(2,1)S(1)}, f32[256,128]{1,0:T(8,128)S(1)}, f32[128,1536]{1,0:T(8,128)S(1)}, bf16[128,1536]{1,0:T(8,128)(2,1)}) custom-call(bf16[256,768]{1,0:T(8,128)(2,1)S(1)} %copy-done.81, bf16[256,256]{1,0:T(8,128)(2,1)S(1)} %copy-done.62, bf16[256,256]{1,0:T(8,128)(2,1)S(1)} %copy-done.65, ...), custom_call_target="tpu_custom_call" | custom-call | flops 4294967296 | bytes 8388608 | tf_op jit(solution)/shard_map/attention_forward/pallas_call | solution.py:263
  110.0 11.4 %collective-permute-done.9 = bf16[48,1408]{1,0:T(8,128)(2,1)} collective-permute-done((bf16[48,1408]{1,0:T(8,128)(2,1)}, bf16[48,1408]{1,0:T(8,128)(2,1)}, u32[]{:S(2)}, u32[]{:S(2)}) %collective-permute-start.9) | collective-permute-done | bytes 135200 | tf_op jit(solution)/shard_map/ppermute | solution.py:66
  130.0 8.7 %collective-permute-done.12.x2 = bf16[128,1536]{1,0:T(8,128)(2,1)S(1)} collective-permute-done((bf16[128,1536]{1,0:T(8,128)(2,1)}, bf16[128,1536]{1,0:T(8,128)(2,1)S(1)}, u32[]{:S(2)}, u32[]{:S(2)}) %collective-permute-start.12) | collective-permute-done | bytes 393248 | tf_op jit(solution)/shard_map/ppermute | solution.py:66
  151.6 14.8 %experts_forward.2 = (bf16[512,1536]{1,0:T(8,128)(2,1)S(1)}, f32[512,1536]{1,0:T(8,128)}, f32[512,1536]{1,0:T(8,128)}, bf16[512,1536]{1,0:T(8,128)(2,1)}, f32[51...) custom-call(bf16[128,1536]{1,0:T(8,128)(2,1)S(1)} %copy-done.7, ...), custom_call_target="tpu_custom_call" | custom-call | flops 7247757312 | bytes 25165824 | tf_op jit(solution)/shard_map/experts_forward/pallas_call | solution.py:522
  171.3 7.3 %collective-permute-done.14 = bf16[128,1536]{1,0:T(8,128)(2,1)S(1)} collective-permute-done((bf16[128,1536]{1,0:T(8,128)(2,1)S(1)}, bf16[128,1536]{1,0:T(8,128)(2,1)S(1)}, u32[]{:S(2)}, u32[]{:S(2)}) %collective-permute-start.14) | collective-permute-done | bytes 393248 | tf_op jit(solution)/shard_map/ppermute | solution.py:62
  178.6 7.6 %collective-permute-done.15 = bf16[128,1536]{1,0:T(8,128)(2,1)S(1)} collective-permute-done((bf16[128,1536]{1,0:T(8,128)(2,1)S(1)}, bf16[128,1536]{1,0:T(8,128)(2,1)S(1)}, u32[]{:S(2)}, u32[]{:S(2)}) %collective-permute-start.15) | collective-permute-done | bytes 393248 | tf_op jit(solution)/shard_map/ppermute | solution.py:66
  191.6 8.4 %collective-permute-done.17 = bf16[128,1536]{1,0:T(8,128)(2,1)} collective-permute-done((bf16[128,1536]{1,0:T(8,128)(2,1)}, bf16[128,1536]{1,0:T(8,128)(2,1)}, u32[]{:S(2)}, u32[]{:S(2)}) %collective-permute-start.17) | collective-permute-done | bytes 393248 | tf_op jit(solution)/shard_map/ppermute | solution.py:62
  227.1 8.0 %collective-permute-done.21 = bf16[48,1408]{1,0:T(8,128)(2,1)S(1)} collective-permute-done((bf16[48,1408]{1,0:T(8,128)(2,1)S(1)}, bf16[48,1408]{1,0:T(8,128)(2,1)S(1)}, u32[]{:S(2)}, u32[]{:S(2)}) %collective-permute-start.21) | collective-permute-done | bytes 135200 | tf_op jit(solution)/shard_map/ppermute | solution.py:66
  243.0 8.1 %collective-permute-done.23.x2 = bf16[128,1536]{1,0:T(8,128)(2,1)} collective-permute-done((bf16[128,1536]{1,0:T(8,128)(2,1)}, bf16[128,1536]{1,0:T(8,128)(2,1)}, u32[]{:S(2)}, u32[]{:S(2)}) %collective-permute-start.23) | collective-permute-done | bytes 393248 | tf_op jit(solution)/shard_map/ppermute | solution.py:66
  256.2 16.8 %all-gather.9.cloned.1.call-done.wg.wu.wd = bf16[1536,4608]{1,0:T(8,128)(2,1)} async-done(((bf16[48,4608]{1,0:T(8,128)(2,1)}), bf16[1536,4608]{1,0:T(8,128)(2,1)}) %all-gather.9.cloned.1.call-update) | async-done | bytes 14155792 | tf_op jit(solution)/shard_map/all_gather | solution.py:222
  277.6 15.0 %experts_forward.3 = (bf16[512,1536]{1,0:T(8,128)(2,1)S(1)}, f32[512,1536]{1,0:T(8,128)}, f32[512,1536]{1,0:T(8,128)}, bf16[512,1536]{1,0:T(8,128)(2,1)}, f32[51...) custom-call(bf16[128,1536]{1,0:T(8,128)(2,1)} %multiply_convert_fusi, ...), custom_call_target="tpu_custom_call" | custom-call | flops 7247757312 | bytes 25165824 | tf_op jit(solution)/shard_map/experts_forward/pallas_call | solution.py:522
  295.8 16.3 %experts_backward.2 = (bf16[512,1536]{1,0:T(8,128)(2,1)S(1)}, bf16[512,1536]{1,0:T(8,128)(2,1)}, bf16[512,1536]{1,0:T(8,128)(2,1)}, bf16[512,256]{1,0:T(8,128)(2...) custom-call(bf16[128,1536]{1,0:T(8,128)(2,1)S(1)} %pad_maximum_fusio, ...), custom_call_target="tpu_custom_call" | custom-call | flops 7247757312 | bytes 25165824 | tf_op jit(solution)/shard_map/experts_backward/pallas_call | solution.py:641
  318.0 10.8 %expert_weight_grads.4 = bf16[384,9216]{1,0:T(8,128)(2,1)} custom-call(bf16[512,1536]{1,0:T(8,128)(2,1)S(1)} %get-tuple-element.233.inputs, bf16[512,1536]{1,0:T(8,128)(2,1)S(1)} %copy-done.14, bf16[512,1536]{1,0:T(8,128)(2,1)} %get-tuple-element.240.gate_grad, bf16[512,1536]{1,0:T(8,128)(2,1)} %get-tuple-element.241.up_grad, bf16[512,1536]{1,0:T(8,128)(2,1)} %copy-done.15, ...), custom_call_target="tpu_custom_call" | custom-call | flops 4831838208 | bytes 25165824 | tf_op jit(solution)/shard_map/expert_weight_grads/pallas_call | solution.py:618
  340.4 8.6 %collective-permute-done.31.rest_0_ = bf16[384,9216]{1,0:T(8,128)(2,1)S(1)} collective-permute-done((bf16[384,9216]{1,0:T(8,128)(2,1)}, bf16[384,9216]{1,0:T(8,128)(2,1)S(1)}, u32[]{:S(2)}, u32[]{:S(2)}) %collective-permute-start.31) | collective-permute-done | bytes 7077920 | tf_op jit(solution)/shard_map/ppermute | solution.py:74
  351.9 13.6 %expert_weight_grads.5 = f32[384,9216]{1,0:T(8,128)} custom-call(bf16[512,1536]{1,0:T(8,128)(2,1)S(1)} %get-tuple-element.233.inputs, bf16[512,1536]{1,0:T(8,128)(2,1)S(1)} %copy-done.14, bf16[512,1536]{1,0:T(8,128)(2,1)} %get-tuple-element.240.gate_grad, bf16[512,1536]{1,0:T(8,128)(2,1)} %get-tuple-element.241.up_grad, bf16[512,1536]{1,0:T(8,128)(2,1)} %copy-done.15, ...), custom_call_target="tpu_custom_call" | custom-call | flops 4831838208 | bytes 25165824 | tf_op jit(solution)/shard_map/expert_weight_grads/pallas_call | solution.py:618
  386.5 6.2 attention_weight_grads.2
  393.0 11.4 %collective-permute-done.35 = bf16[128,1536]{1,0:T(8,128)(2,1)S(1)} collective-permute-done((bf16[128,1536]{1,0:T(8,128)(2,1)S(1)}, bf16[128,1536]{1,0:T(8,128)(2,1)S(1)}, u32[]{:S(2)}, u32[]{:S(2)}) %collective-permute-start.35) | collective-permute-done | bytes 393248 | tf_op jit(solution)/shard_map/ppermute | solution.py:62
  409.6 9.4 %collective-permute-done.37.y2 = bf16[128,1536]{1,0:T(8,128)(2,1)S(1)} collective-permute-done((bf16[128,1536]{1,0:T(8,128)(2,1)S(1)}, bf16[128,1536]{1,0:T(8,128)(2,1)S(1)}, u32[]{:S(2)}, u32[]{:S(2)}) %collective-permute-start.37) | collective-permute-done | bytes 393248 | tf_op jit(solution)/shard_map/ppermute | solution.py:66
  419.0 7.1 %collective-permute-done.38.y3 = bf16[128,1536]{1,0:T(8,128)(2,1)S(1)} collective-permute-done((bf16[128,1536]{1,0:T(8,128)(2,1)S(1)}, bf16[128,1536]{1,0:T(8,128)(2,1)S(1)}, u32[]{:S(2)}, u32[]{:S(2)}) %collective-permute-start.38) | collective-permute-done | bytes 393248 | tf_op jit(solution)/shard_map/ppermute | solution.py:70
  430.5 15.6 %experts_backward.3 = (bf16[512,1536]{1,0:T(8,128)(2,1)S(1)}, bf16[512,1536]{1,0:T(8,128)(2,1)}, bf16[512,1536]{1,0:T(8,128)(2,1)}, bf16[512,256]{1,0:T(8,128)(2...) custom-call(bf16[128,1536]{1,0:T(8,128)(2,1)S(1)} %get-tuple-element, ...), custom_call_target="tpu_custom_call" | custom-call | flops 7247757312 | bytes 25165824 | tf_op jit(solution)/shard_map/experts_backward/pallas_call | solution.py:641
  450.0 10.5 %expert_weight_grads.6 = bf16[384,9216]{1,0:T(8,128)(2,1)} custom-call(bf16[512,1536]{1,0:T(8,128)(2,1)S(1)} %copy-done.2, bf16[512,1536]{1,0:T(8,128)(2,1)S(1)} %copy-done.12, bf16[512,1536]{1,0:T(8,128)(2,1)} %get-tuple-element.275.gate_grad, bf16[512,1536]{1,0:T(8,128)(2,1)} %get-tuple-element.276.up_grad, bf16[512,1536]{1,0:T(8,128)(2,1)} %copy-done.13, ...), custom_call_target="tpu_custom_call" | custom-call | flops 4831838208 | bytes 25165824 | tf_op jit(solution)/shard_map/expert_weight_grads/pallas_call | solution.py:618
  468.5 6.9 %collective-permute-done.44 = bf16[128,1536]{1,0:T(8,128)(2,1)S(1)} collective-permute-done((bf16[128,1536]{1,0:T(8,128)(2,1)S(1)}, bf16[128,1536]{1,0:T(8,128)(2,1)S(1)}, u32[]{:S(2)}, u32[]{:S(2)}) %collective-permute-start.44) | collective-permute-done | bytes 393248 | tf_op jit(solution)/shard_map/ppermute | solution.py:70
  477.2 9.7 %collective-permute-done.45.rest_0_ = bf16[384,9216]{1,0:T(8,128)(2,1)S(1)} collective-permute-done((bf16[384,9216]{1,0:T(8,128)(2,1)}, bf16[384,9216]{1,0:T(8,128)(2,1)S(1)}, u32[]{:S(2)}, u32[]{:S(2)}) %collective-permute-start.45) | collective-permute-done | bytes 7077920 | tf_op jit(solution)/shard_map/ppermute | solution.py:74
  489.9 13.5 %expert_weight_grads.7 = f32[384,9216]{1,0:T(8,128)} custom-call(bf16[512,1536]{1,0:T(8,128)(2,1)S(1)} %copy-done.2, bf16[512,1536]{1,0:T(8,128)(2,1)S(1)} %copy-done.12, bf16[512,1536]{1,0:T(8,128)(2,1)} %get-tuple-element.275.gate_grad, bf16[512,1536]{1,0:T(8,128)(2,1)} %get-tuple-element.276.up_grad, bf16[512,1536]{1,0:T(8,128)(2,1)} %copy-done.13, ...), custom_call_target="tpu_custom_call" | custom-call | flops 4831838208 | bytes 25165824 | tf_op jit(solution)/shard_map/expert_weight_grads/pallas_call | solution.py:618
  505.3 6.9 %collective-permute-done.51 = bf16[128,768]{1,0:T(8,128)(2,1)S(1)} collective-permute-done((bf16[128,768]{1,0:T(8,128)(2,1)S(1)}, bf16[128,768]{1,0:T(8,128)(2,1)S(1)}, u32[]{:S(2)}, u32[]{:S(2)}) %collective-permute-start.51) | collective-permute-done | bytes 196640 | tf_op jit(solution)/shard_map/ppermute | solution.py:62
  553.2 6.3 attention_weight_grads.3
  564.4 16.7 %collective-permute-done.59 = f32[20,768]{1,0:T(8,128)S(1)} collective-permute-done((f32[20,768]{1,0:T(8,128)S(1)}, f32[20,768]{1,0:T(8,128)S(1)}, u32[]{:S(2)}, u32[]{:S(2)}) %collective-permute-start.59) | collective-permute-done | bytes 61472 | tf_op jit(solution)/shard_map/ppermute | solution.py:62
  621.4 20.6 %collective-permute-done.66 = bf16[96,3584]{1,0:T(8,128)(2,1)S(1)} collective-permute-done((bf16[96,3584]{1,0:T(8,128)(2,1)S(1)}, bf16[96,3584]{1,0:T(8,128)(2,1)S(1)}, u32[]{:S(2)}, u32[]{:S(2)}) %collective-permute-start.66) | collective-permute-done | bytes 688160 | tf_op jit(solution)/shard_map/ppermute | solution.py:74
  662.2 8.8 %collective-permute-done.73 = bf16[24,8192]{1,0:T(8,128)(2,1)S(1)} collective-permute-done((bf16[24,8192]{1,0:T(8,128)(2,1)S(1)}, bf16[24,8192]{1,0:T(8,128)(2,1)S(1)}, u32[]{:S(2)}, u32[]{:S(2)}) %collective-permute-start.73) | collective-permute-done | bytes 393248 | tf_op jit(solution)/shard_map/ppermute | solution.py:66
  (708 shorter events, 328.5 us)
Async XLA Ops:
  7.2 138.3 %all-gather.5.cloned.1.call-start = ((), (), s32[]{:S(2)}) async-start(), calls=%async_computation.2 | async-start | bytes 14598144 | tf_op jit(solution)/shard_map/all_gather | solution.py:222
  41.3 158.7 %all-gather.7.cloned.1.call-start = ((), (), s32[]{:S(2)}) async-start(), calls=%async_computation.3 | async-start | bytes 5677056 | tf_op jit(solution)/shard_map/all_gather | solution.py:222
  43.2 65.1 %collective-permute-start.10 = (bf16[128,768]{1,0:T(8,128)(2,1)}, bf16[128,768]{1,0:T(8,128)(2,1)}, u32[]{:S(2)}, u32[]{:S(2)}) collective-permute-start(bf16[128,768]{1,0:T(8,128)(2,1)} %get-tuple-element.494), channel_id=1, source_target_pairs={{0,1},{1,0},{2,3},{3,2},{4,5},{5,4},{6,7},{7,6},{8,9},{9,8},{10,11... | collective-permute-start | bytes 589832 | tf_op jit(solution)/shard_map/ppermute | solution.py:66
  56.3 27.1 %collective-permute-start.5 = (bf16[384,768]{1,0:T(8,128)(2,1)}, bf16[384,768]{1,0:T(8,128)(2,1)}, u32[]{:S(2)}, u32[]{:S(2)}) collective-permute-start(bf16[384,768]{1,0:T(8,128)(2,1)} %get-tuple-element.185), channel_id=1, source_target_pairs={{0,1},{1,0},{2,3},{3,2},{4,5},{5,4},{6,7},{7,6},{8,9},{9,8},{10,11... | collective-permute-start | bytes 1769480 | tf_op jit(solution)/shard_map/ppermute | solution.py:66
  102.4 19.8 %collective-permute-start.8 = (bf16[128,1536]{1,0:T(8,128)(2,1)}, bf16[128,1536]{1,0:T(8,128)(2,1)}, u32[]{:S(2)}, u32[]{:S(2)}) collective-permute-start(bf16[128,1536]{1,0:T(8,128)(2,1)} %get-tuple-element.197), channel_id=1, source_target_pairs={{0,2},{2,0},{1,3},{3,1},{4,6},{6,4},{5,7},{7,5},{8,10},{10,8},{9,1... | collective-permute-start | bytes 1179656 | tf_op jit(solution)/shard_map/ppermute | solution.py:62
  126.9 18.5 %collective-permute-start.13 = (bf16[128,1536]{1,0:T(8,128)(2,1)}, bf16[128,1536]{1,0:T(8,128)(2,1)}, u32[]{:S(2)}, u32[]{:S(2)}) collective-permute-start(bf16[128,1536]{1,0:T(8,128)(2,1)} %pad_maximum_fusion.8), channel_id=1, source_target_pairs={{0,3},{1,2},{2,1},{3,0},{4,7},{5,6},{6,5},{7,4},{8,11},{9,10},{10,... | collective-permute-start | bytes 1179656 | tf_op jit(solution)/shard_map/ppermute | solution.py:70
  145.5 127.5 %all-gather.9.cloned.1.call-start = ((), (), s32[]{:S(2)}) async-start(), calls=%async_computation.4 | async-start | bytes 14598144 | tf_op jit(solution)/shard_map/all_gather | solution.py:222
  149.5 21.7 %collective-permute-start.18 = (bf16[48,3840]{1,0:T(8,128)(2,1)S(1)}, bf16[48,3840]{1,0:T(8,128)(2,1)S(1)}, u32[]{:S(2)}, u32[]{:S(2)}) collective-permute-start(bf16[48,3840]{1,0:T(8,128)(2,1)S(1)} %copy-done.60), channel_id=1, source_target_pairs={{0,1},{1,0},{2,3},{3,2},{4,5},{5,4},{6,7},{7,6},{8,9},{9,8},{10,11... | collective-permute-start | bytes 1105928 | tf_op jit(solution)/shard_map/ppermute | solution.py:66
  167.7 18.5 %collective-permute-start.15 = (bf16[128,1536]{1,0:T(8,128)(2,1)S(1)}, bf16[128,1536]{1,0:T(8,128)(2,1)S(1)}, u32[]{:S(2)}, u32[]{:S(2)}) collective-permute-start(bf16[128,1536]{1,0:T(8,128)(2,1)S(1)} %get-tuple-element.210), channel_id=1, source_target_pairs={{0,1},{1,0},{2,3},{3,2},{4,5},{5,4},{6,7},{7,6},{8,9},{9,8},{10,11... | collective-permute-start | bytes 1179656 | tf_op jit(solution)/shard_map/ppermute | solution.py:66
  169.3 19.3 %collective-permute-start.16 = (bf16[128,1536]{1,0:T(8,128)(2,1)S(1)}, bf16[128,1536]{1,0:T(8,128)(2,1)S(1)}, u32[]{:S(2)}, u32[]{:S(2)}) collective-permute-start(bf16[128,1536]{1,0:T(8,128)(2,1)S(1)} %get-tuple-element.211), channel_id=1, source_target_pairs={{0,3},{1,2},{2,1},{3,0},{4,7},{5,6},{6,5},{7,4},{8,11},{9,10},{10,... | collective-permute-start | bytes 1179656 | tf_op jit(solution)/shard_map/ppermute | solution.py:70
  204.2 161.3 %all-gather.11.cloned.1.call-start = ((), (), s32[]{:S(2)}) async-start(), calls=%async_computation.5 | async-start | bytes 5677056 | tf_op jit(solution)/shard_map/all_gather | solution.py:222
  273.0 231.1 %reduce-scatter.7.cloned.1.call-start = ((), (), s32[]{:S(2)}) async-start(), calls=%async_computation.6 | async-start | bytes 15040512
  273.1 22.7 %collective-permute-start.26 = (bf16[128,1536]{1,0:T(8,128)(2,1)S(1)}, bf16[128,1536]{1,0:T(8,128)(2,1)S(1)}, u32[]{:S(2)}, u32[]{:S(2)}) collective-permute-start(bf16[128,1536]{1,0:T(8,128)(2,1)S(1)} %pad_maximum_fusion.10), channel_id=1, source_target_pairs={{0,1},{1,0},{2,3},{3,2},{4,5},{5,4},{6,7},{7,6},{8,9},{9,8},{10,11... | collective-permute-start | bytes 1179656 | tf_op jit(solution)/shard_map/ppermute | solution.py:66
  276.2 19.6 %collective-permute-start.27 = (bf16[128,1536]{1,0:T(8,128)(2,1)S(1)}, bf16[128,1536]{1,0:T(8,128)(2,1)S(1)}, u32[]{:S(2)}, u32[]{:S(2)}) collective-permute-start(bf16[128,1536]{1,0:T(8,128)(2,1)S(1)} %pad_maximum_fusion.10), channel_id=1, source_target_pairs={{0,3},{1,2},{2,1},{3,0},{4,7},{5,6},{6,5},{7,4},{8,11},{9,10},{10,... | collective-permute-start | bytes 1179656 | tf_op jit(solution)/shard_map/ppermute | solution.py:70
  315.2 18.8 %collective-permute-start.29 = (bf16[128,1536]{1,0:T(8,128)(2,1)S(1)}, bf16[128,1536]{1,0:T(8,128)(2,1)S(1)}, u32[]{:S(2)}, u32[]{:S(2)}) collective-permute-start(bf16[128,1536]{1,0:T(8,128)(2,1)S(1)} %get-tuple-element.247), channel_id=1, source_target_pairs={{0,1},{1,0},{2,3},{3,2},{4,5},{5,4},{6,7},{7,6},{8,9},{9,8},{10,11... | collective-permute-start | bytes 1179656 | tf_op jit(solution)/shard_map/ppermute | solution.py:66
  316.8 19.8 %collective-permute-start.30 = (bf16[128,1536]{1,0:T(8,128)(2,1)S(1)}, bf16[128,1536]{1,0:T(8,128)(2,1)S(1)}, u32[]{:S(2)}, u32[]{:S(2)}) collective-permute-start(bf16[128,1536]{1,0:T(8,128)(2,1)S(1)} %get-tuple-element.248), channel_id=1, source_target_pairs={{0,3},{1,2},{2,1},{3,0},{4,7},{5,6},{6,5},{7,4},{8,11},{9,10},{10,... | collective-permute-start | bytes 1179656 | tf_op jit(solution)/shard_map/ppermute | solution.py:70
  340.4 25.0 %collective-permute-start.32 = (bf16[128,1536]{1,0:T(8,128)(2,1)S(1)}, bf16[128,1536]{1,0:T(8,128)(2,1)}, u32[]{:S(2)}, u32[]{:S(2)}) collective-permute-start(bf16[128,1536]{1,0:T(8,128)(2,1)S(1)} %fusion.51.upstream), channel_id=1, source_target_pairs={{0,2},{2,0},{1,3},{3,1},{4,6},{6,4},{5,7},{7,5},{8,10},{10,8},{9,1... | collective-permute-start | bytes 1179656 | tf_op jit(solution)/shard_map/ppermute | solution.py:62
  365.5 292.5 %reduce-scatter.9.cloned.1.call-start = ((), (), s32[]{:S(2)}) async-start(), calls=%async_computation.7 | async-start | bytes 15040512
  406.3 19.8 %collective-permute-start.38 = (bf16[128,1536]{1,0:T(8,128)(2,1)S(1)}, bf16[128,1536]{1,0:T(8,128)(2,1)S(1)}, u32[]{:S(2)}, u32[]{:S(2)}) collective-permute-start(bf16[128,1536]{1,0:T(8,128)(2,1)S(1)} %pad_maximum_fusion.11), channel_id=1, source_target_pairs={{0,3},{1,2},{2,1},{3,0},{4,7},{5,6},{6,5},{7,4},{8,11},{9,10},{10,... | collective-permute-start | bytes 1179656 | tf_op jit(solution)/shard_map/ppermute | solution.py:70
  427.5 33.0 %collective-permute-start.39 = (bf16[96,3584]{1,0:T(8,128)(2,1)}, bf16[96,3584]{1,0:T(8,128)(2,1)S(1)}, u32[]{:S(2)}, u32[]{:S(2)}) collective-permute-start(bf16[96,3584]{1,0:T(8,128)(2,1)} %get-tuple-element.410), channel_id=1, source_target_pairs={{0,32},{4,36},{8,40},{12,44},{16,48},{20,52},{24,56},{28,60},{32,6... | collective-permute-start | bytes 2064392 | tf_op jit(solution)/shard_map/ppermute | solution.py:74
  428.0 34.6 %collective-permute-start.40 = (bf16[96,3584]{1,0:T(8,128)(2,1)}, bf16[96,3584]{1,0:T(8,128)(2,1)}, u32[]{:S(2)}, u32[]{:S(2)}) collective-permute-start(bf16[96,3584]{1,0:T(8,128)(2,1)} %get-tuple-element.412), channel_id=1, source_target_pairs={{0,64},{4,68},{8,72},{12,76},{16,80},{20,84},{24,88},{28,92},{32,9... | collective-permute-start | bytes 2064392 | tf_op jit(solution)/shard_map/ppermute | solution.py:74
  430.4 35.5 %collective-permute-start.41 = (bf16[96,3584]{1,0:T(8,128)(2,1)}, bf16[96,3584]{1,0:T(8,128)(2,1)}, u32[]{:S(2)}, u32[]{:S(2)}) collective-permute-start(bf16[96,3584]{1,0:T(8,128)(2,1)} %get-tuple-element.411), channel_id=1, source_target_pairs={{0,96},{4,100},{8,104},{12,108},{16,112},{20,116},{24,120},{28,124... | collective-permute-start | bytes 2064392 | tf_op jit(solution)/shard_map/ppermute | solution.py:74
  447.2 21.3 %collective-permute-start.42 = (bf16[128,1536]{1,0:T(8,128)(2,1)S(1)}, bf16[128,1536]{1,0:T(8,128)(2,1)S(1)}, u32[]{:S(2)}, u32[]{:S(2)}) collective-permute-start(bf16[128,1536]{1,0:T(8,128)(2,1)S(1)} %get-tuple-element.280), channel_id=1, source_target_pairs={{0,2},{2,0},{1,3},{3,1},{4,6},{6,4},{5,7},{7,5},{8,10},{10,8},{9,1... | collective-permute-start | bytes 1179656 | tf_op jit(solution)/shard_map/ppermute | solution.py:62
  447.6 20.9 %collective-permute-start.43 = (bf16[128,1536]{1,0:T(8,128)(2,1)S(1)}, bf16[128,1536]{1,0:T(8,128)(2,1)S(1)}, u32[]{:S(2)}, u32[]{:S(2)}) collective-permute-start(bf16[128,1536]{1,0:T(8,128)(2,1)S(1)} %get-tuple-element.281), channel_id=1, source_target_pairs={{0,1},{1,0},{2,3},{3,2},{4,5},{5,4},{6,7},{7,6},{8,9},{9,8},{10,11... | collective-permute-start | bytes 1179656 | tf_op jit(solution)/shard_map/ppermute | solution.py:66
  477.2 26.2 %collective-permute-start.46 = (bf16[128,1536]{1,0:T(8,128)(2,1)S(1)}, bf16[128,1536]{1,0:T(8,128)(2,1)S(1)}, u32[]{:S(2)}, u32[]{:S(2)}) collective-permute-start(bf16[128,1536]{1,0:T(8,128)(2,1)S(1)} %get-tuple-element.303.upstream), channel_id=1, source_target_pairs={{0,2},{2,0},{1,3},{3,1},{4,6},{6,4},{5,7},{7,5},{8,10},{10,8},{9,1... | collective-permute-start | bytes 1179656 | tf_op jit(solution)/shard_map/ppermute | solution.py:62
  559.5 51.2 %collective-permute-start.65 = (bf16[384,3584]{1,0:T(8,128)(2,1)}, bf16[384,3584]{1,0:T(8,128)(2,1)}, u32[]{:S(2)}, u32[]{:S(2)}) collective-permute-start(bf16[384,3584]{1,0:T(8,128)(2,1)} %get-tuple-element.325), channel_id=1, source_target_pairs={{0,4},{4,0},{8,12},{12,8},{16,20},{20,16},{24,28},{28,24},{32,36},... | collective-permute-start | bytes 8257544 | tf_op jit(solution)/shard_map/ppermute | solution.py:74
  559.5 30.3 %collective-permute-start.47 = (bf16[128,1536]{1,0:T(8,128)(2,1)S(1)}, bf16[128,1536]{1,0:T(8,128)(2,1)S(1)}, u32[]{:S(2)}, u32[]{:S(2)}) collective-permute-start(bf16[128,1536]{1,0:T(8,128)(2,1)S(1)} %copy-done.56), channel_id=1, source_target_pairs={{0,2},{2,0},{1,3},{3,1},{4,6},{6,4},{5,7},{7,5},{8,10},{10,8},{9,1... | collective-permute-start | bytes 1179656 | tf_op jit(solution)/shard_map/ppermute | solution.py:62
  559.6 30.2 %collective-permute-start.48 = (bf16[128,1536]{1,0:T(8,128)(2,1)S(1)}, bf16[128,1536]{1,0:T(8,128)(2,1)S(1)}, u32[]{:S(2)}, u32[]{:S(2)}) collective-permute-start(bf16[128,1536]{1,0:T(8,128)(2,1)S(1)} %copy-done.54), channel_id=1, source_target_pairs={{0,1},{1,0},{2,3},{3,2},{4,5},{5,4},{6,7},{7,6},{8,9},{9,8},{10,11... | collective-permute-start | bytes 1179656 | tf_op jit(solution)/shard_map/ppermute | solution.py:66
  562.1 27.8 %collective-permute-start.49 = (bf16[128,1536]{1,0:T(8,128)(2,1)S(1)}, bf16[128,1536]{1,0:T(8,128)(2,1)S(1)}, u32[]{:S(2)}, u32[]{:S(2)}) collective-permute-start(bf16[128,1536]{1,0:T(8,128)(2,1)S(1)} %copy-done.52), channel_id=1, source_target_pairs={{0,3},{1,2},{2,1},{3,0},{4,7},{5,6},{6,5},{7,4},{8,11},{9,10},{10,... | collective-permute-start | bytes 1179656 | tf_op jit(solution)/shard_map/ppermute | solution.py:70
  614.8 27.2 %collective-permute-start.66 = (bf16[96,3584]{1,0:T(8,128)(2,1)S(1)}, bf16[96,3584]{1,0:T(8,128)(2,1)S(1)}, u32[]{:S(2)}, u32[]{:S(2)}) collective-permute-start(bf16[96,3584]{1,0:T(8,128)(2,1)S(1)} %get-tuple-element.407), channel_id=1, source_target_pairs={{0,32},{4,36},{8,40},{12,44},{16,48},{20,52},{24,56},{28,60},{32,6... | collective-permute-start | bytes 2064392 | tf_op jit(solution)/shard_map/ppermute | solution.py:74
  616.9 25.0 %collective-permute-start.67 = (bf16[96,3584]{1,0:T(8,128)(2,1)S(1)}, bf16[96,3584]{1,0:T(8,128)(2,1)S(1)}, u32[]{:S(2)}, u32[]{:S(2)}) collective-permute-start(bf16[96,3584]{1,0:T(8,128)(2,1)S(1)} %get-tuple-element.409), channel_id=1, source_target_pairs={{0,64},{4,68},{8,72},{12,76},{16,80},{20,84},{24,88},{28,92},{32,9... | collective-permute-start | bytes 2064392 | tf_op jit(solution)/shard_map/ppermute | solution.py:74
  618.7 26.9 %collective-permute-start.68 = (bf16[96,3584]{1,0:T(8,128)(2,1)S(1)}, bf16[96,3584]{1,0:T(8,128)(2,1)S(1)}, u32[]{:S(2)}, u32[]{:S(2)}) collective-permute-start(bf16[96,3584]{1,0:T(8,128)(2,1)S(1)} %get-tuple-element.408), channel_id=1, source_target_pairs={{0,96},{4,100},{8,104},{12,108},{16,112},{20,116},{24,120},{28,124... | collective-permute-start | bytes 2064392 | tf_op jit(solution)/shard_map/ppermute | solution.py:74
  (203 other events, 1667.0 us)
Sparse Core Ops, SparseCore 0:
  41.5 68.8 all-gather.4
  145.6 48.7 all-gather.6
  204.3 68.6 all-gather.8
  275.1 46.9 all-gather.10
  365.6 112.8 reduce-scatter.6
  504.3 107.1 reduce-scatter.8

commit v4 on v3

--- a/solution.py
+++ b/solution.py
@@ -99,6 +99,10 @@
     return lax.optimization_barrier(values)
 
 
+def later(index, value):
+    return index + (value[0, 0].astype(F32) * 0.0).astype(jnp.int32)
+
+
 def pack(parts):
     return jnp.concatenate([x.astype(BF16) for x in parts], axis=1)
 
@@ -156,7 +160,9 @@
     index = place[0]
     start = pl.multiple_of((index % 16) * PIECE, 16)
     down_start = pl.multiple_of((index % 8) * PIECE, 16)
-    width = Q_HEADS * HEAD
+    upper = pl.multiple_of(index % 2 * CORE_ROWS, 128)
+    out_start = pl.multiple_of(index // 2 * PIECE, 16)
+    heads = ((query, Q_HEADS * HEAD), (key, HEAD), (value, HEAD))
     moves = []
     for side, target in ((column, own), (1 - column, other)):
         for k, weight in enumerate((gate, up)):
@@ -173,26 +179,26 @@
                 target.at[:, pl.ds(2 * D, HALF)],
             )
         )
+        moves.append(
+            (
+                out.at[1 - layer, pl.ds(out_start, PIECE), pl.ds(upper, CORE_ROWS)],
+                target.at[:, pl.ds(2 * D + HALF, CORE_ROWS)],
+            )
+        )
+        offset = 2 * D + HALF + CORE_ROWS
+        for weight, size in heads:
+            moves.append(
+                (weight.at[1 - layer, pl.ds(start, PIECE), :], target.at[:, pl.ds(offset, size)])
+            )
+            offset += size
     if extra:
-        qkv_own, out_own, out_send, *parts = extra
-        upper = pl.multiple_of(index % 2 * CORE_ROWS, 128)
-        out_start = pl.multiple_of(index // 2 * PIECE, 16)
+        qkv_own, out_own, out_send = extra
         offset = 0
-        for weight, size in ((query, width), (key, HEAD), (value, HEAD)):
-            columns = pl.ds(offset, size)
-            moves.append((weight.at[layer], qkv_own.at[:, columns]))
-            for k, target in enumerate(parts):
-                moves.append((weight.at[k, pl.ds(start, PIECE), :], target.at[:, columns]))
+        for weight, size in heads:
+            moves.append((weight.at[layer], qkv_own.at[:, pl.ds(offset, size)]))
             offset += size
         moves.append((out.at[layer], out_own))
         moves.append((out.at[layer, pl.ds(upper, CORE_ROWS), :], out_send))
-        for k, target in enumerate(parts):
-            moves.append(
-                (
-                    out.at[k, pl.ds(out_start, PIECE), pl.ds(upper, CORE_ROWS)],
-                    target.at[:, pl.ds(QKV, CORE_ROWS)],
-                )
-            )
     copies = [pltpu.make_async_copy(a, b, sems.at[i]) for i, (a, b) in enumerate(moves)]
     for copy in copies:
         copy.start()
@@ -201,11 +207,10 @@
 
 
 def take_pieces(layer, place, weights, first):
-    shapes = [(PIECE, 2 * D + HALF)] * 2
+    shapes = [(PIECE, 2 * D + HALF + CORE_ROWS + QKV)] * 2
     if first:
         shapes += [(HALF, QKV), (HALF, HALF), (CORE_ROWS, HALF)]
-        shapes += [(PIECE, QKV + CORE_ROWS)] * LAYERS
-    anywhere = pl.BlockSpec(memory_space=pl.ANY)
+    anywhere = pl.BlockSpec(memory_space=pltpu.HBM)
     inside = pl.BlockSpec(memory_space=pltpu.VMEM)
     return pl.pallas_call(
         lambda *refs: pieces_kernel(layer, *refs),
@@ -222,34 +227,72 @@
     return lax.all_gather(piece, "dp", axis=0, tiled=True)
 
 
-def expert_piece(own, other, data_index):
-    gate_up = jnp.where(data_index < 16, own[:, : 2 * D], other[:, : 2 * D])
-    return jnp.concatenate([gate_up, own[:, 2 * D :], other[:, 2 * D :]], axis=1)
-
-
-def attention_piece(own, other, data_index):
-    qkv = jnp.where(data_index < 16, own[:, :QKV], other[:, :QKV])
-    return jnp.concatenate([qkv, own[:, QKV:], other[:, QKV:]], axis=1)
-
-
-def attention_whole(gathered):
-    outs = []
+def piece_kernel(place, own, other, packed):
+    gate_up = 2 * D
+    outs = gate_up + HALF
+    qkv = outs + CORE_ROWS
+    near = place[0] < 16
+    packed[:, :gate_up] = jnp.where(near, own[:, :gate_up], other[:, :gate_up])
+    offset = gate_up
+    for lower, upper in ((gate_up, outs), (outs, qkv)):
+        for x in (own, other):
+            packed[:, offset : offset + upper - lower] = x[:, lower:upper]
+            offset += upper - lower
+    packed[:, offset:] = jnp.where(near, own[:, qkv:], other[:, qkv:])
+
+
+def whole_piece(own, other, data_index):
+    return local_call(
+        piece_kernel,
+        [((PIECE, 3 * D + HALF + QKV), BF16)],
+        [data_index.reshape(1), own, other],
+        "whole_piece",
+        {0: pl.BlockSpec(memory_space=pltpu.SMEM)},
+    )[0]
+
+
+def first_product_kernel(own, peer, weight, near, away, near_rows):
+    column = lax.axis_index("col")
+    for k, side in enumerate((column, 1 - column)):
+        start = pl.multiple_of(side * QUARTER, QUARTER)
+        rows = jnp.concatenate([x[pl.ds(start, QUARTER), :] for x in (own, peer)], axis=0)
+        result = dot(rows, weight[...])
+        if k == 0:
+            near_rows[...] = rows
+            near[...] = result
+        else:
+            away[...] = result.astype(BF16)
+
+
+def first_product(own, peer, weight):
+    return local_call(
+        first_product_kernel,
+        [((PAIR_ROWS, QKV), F32), ((PAIR_ROWS, QKV), BF16), ((PAIR_ROWS, HALF), BF16)],
+        [own, peer, weight],
+        "first_product",
+    )
+
+
+OUT_SPEC = pl.BlockSpec((D, HALF), lambda j: (0, 6))
+QKV_SPECS = [pl.BlockSpec((D, 256), lambda j, k=k: (0, 21 + k)) for k in range(4)]
+
+
+def output_weight(gathered, target):
     for k in range(2):
-        part = gathered[:, QKV + k * CORE_ROWS : QKV + (k + 1) * CORE_ROWS]
-        part = part.reshape(16, 2, PIECE, CORE_ROWS).transpose(0, 2, 1, 3)
-        outs.append(part.reshape(HALF, HALF))
-    return (gathered, outs)
+        for row in range(16):
+            for side in range(2):
+                start = (row * 2 + side) * PIECE
+                target[
+                    row * PIECE : (row + 1) * PIECE,
+                    k * HALF + side * CORE_ROWS : k * HALF + (side + 1) * CORE_ROWS,
+                ] = gathered[start : start + PIECE, k * CORE_ROWS : (k + 1) * CORE_ROWS]
 
 
 def turn(x, cosine, sine):
     return x * cosine + pltpu.roll(x, HEAD // 2, 1) * sine
 
 
-def rotate_kernel(cosine, sine, *rest):
-    *parts, query, pair = rest
-    values = parts[0][...]
-    for x in parts[1:]:
-        values = values + x[...].astype(F32)
+def write_heads(values, cosine, sine, query, pair):
     for h in range(Q_HEADS + 1):
         target, column = (query, h * HEAD) if h < Q_HEADS else (pair, 0)
         rotated = turn(values[:, h * HEAD : (h + 1) * HEAD], cosine[...], sine[...])
@@ -257,7 +300,19 @@
     pair[:, HEAD:] = values[:, (Q_HEADS + 1) * HEAD :].astype(BF16)
 
 
-def local_call(kernel, shapes, operands, name, specs=None):
+def first_heads_kernel(cosine, sine, near, far, query, pair):
+    write_heads(near[...] + far[...].astype(F32), cosine, sine, query, pair)
+
+
+def heads_kernel(cosine, sine, own, peer, *rest):
+    *weights, query, pair, inputs = rest
+    inputs[:QUARTER, :] = own[...]
+    inputs[QUARTER:, :] = peer[...]
+    values = jnp.concatenate([dot(inputs[...], w[...]) for w in weights], axis=1)
+    write_heads(values, cosine, sine, query, pair)
+
+
+def local_call(kernel, shapes, operands, name, specs=None, scratch=()):
     outs = [jax.ShapeDtypeStruct(*x) for x in shapes]
     specs = specs or {}
     return pl.pallas_call(
@@ -266,6 +321,7 @@
         in_specs=[specs.get(k) or whole(x.shape) for k, x in enumerate(operands)],
         out_specs=[whole(x.shape) for x in outs],
         out_shape=outs,
+        scratch_shapes=scratch,
         compiler_params=pltpu.CompilerParams(vmem_limit_bytes=VMEM_LIMIT),
         cost_estimate=pl.CostEstimate(flops=4 << 30, bytes_accessed=8 << 20, transcendentals=1 << 20),
         name=name,
@@ -273,15 +329,21 @@
 
 
 PAIR_ROWS = 2 * QUARTER
-
-
-def rotate_parts(parts, geometry):
-    cosine, sine = geometry[:2]
+HEAD_SHAPES = [((PAIR_ROWS, Q_HEADS * HEAD), BF16), ((PAIR_ROWS, 2 * HEAD), BF16)]
+OUT_SCRATCH = [pltpu.VMEM((HALF, D), BF16)]
+
+
+def first_heads(near, far, geometry):
+    return local_call(first_heads_kernel, HEAD_SHAPES, [*geometry[:2], near, far], "first_heads")
+
+
+def make_heads(own, peer, weights, geometry):
     return local_call(
-        rotate_kernel,
-        [((PAIR_ROWS, Q_HEADS * HEAD), BF16), ((PAIR_ROWS, 2 * HEAD), BF16)],
-        [cosine, sine, *parts],
-        "rotate_heads",
+        heads_kernel,
+        HEAD_SHAPES + [((PAIR_ROWS, D), BF16)],
+        [*geometry[:2], own, peer] + [weights] * 4,
+        "make_heads",
+        {4 + k: x for k, x in enumerate(QKV_SPECS)},
     )
 
 
@@ -292,8 +354,8 @@
     ]
 
 
-def attention_kernel(query, own, far, seen, valid, side, *rest):
-    out_own, out_first, out_second, attended, log_total, near, peer = rest
+def attention_kernel(query, own, far, seen, valid, *rest):
+    *side_outs, attended, log_total, near, peer, out_weight = rest
     keys, values = keys_values(own[...], far[...])
     mask = seen[...] > 0.0
     real = valid[...]
@@ -309,25 +371,24 @@
         attended[:, columns] = dot((exponent / denominator).astype(BF16), values).astype(BF16)
         logs = jnp.where(lanes == h, top + jnp.log(denominator), logs)
     log_total[...] = logs
-    first, second = attended[:, :CORE_ROWS], attended[:, CORE_ROWS:]
-    straight = side[0, 0] == 0
-    left = jnp.where(straight, first, second)
-    right = jnp.where(straight, second, first)
-    for k, x in enumerate(
-        (dot(attended[...], out_own[...]), dot(left, out_first[...]) + dot(right, out_second[...]))
-    ):
-        columns = slice(k * HALF, (k + 1) * HALF)
-        near[:, columns] = x[:QUARTER]
-        peer[:, columns] = x[QUARTER:].astype(BF16)
-
-
-def attention_forward(parts, geometry, meanwhile):
+    if len(side_outs) == 1:
+        output_weight(side_outs[0], out_weight)
+    else:
+        out_own, out_first, out_second = side_outs
+        straight = lax.axis_index("dp") % 2 == 0
+        first, second = out_first[...], out_second[...]
+        out_weight[:, :HALF] = out_own[...]
+        out_weight[:CORE_ROWS, HALF:] = jnp.where(straight, first, second)
+        out_weight[CORE_ROWS:, HALF:] = jnp.where(straight, second, first)
+    branch = dot(attended[...], out_weight[...])
+    near[...] = branch[:QUARTER]
+    peer[...] = branch[QUARTER:].astype(BF16)
+
+
+def attention_forward(query, pair, geometry, meanwhile):
     _, _, seen, valid = geometry
-    query, pair = rotate_parts(parts, geometry)
     far = over_col(pair)
-    pair, far, (side, *out_parts) = meanwhile(pair, far)
-    side = jnp.broadcast_to(jnp.asarray(side, jnp.int32), (1, 1))
-    smem = pl.BlockSpec(memory_space=pltpu.SMEM)
+    pair, far, out_parts = meanwhile(pair, far)
     attended, log_total, near, peer = local_call(
         attention_kernel,
         [
@@ -336,21 +397,22 @@
             (BLOCK, F32),
             (BLOCK, BF16),
         ],
-        [query, pair, far, seen, valid, side, *out_parts],
+        [query, pair, far, seen, valid, *out_parts],
         "attention_forward",
-        {5: smem},
+        {5: OUT_SPEC} if len(out_parts) == 1 else None,
+        OUT_SCRATCH,
     )
     return ((query, pair, far, log_total, attended), (near, over_row(peer)))
 
 
-def attention_back_kernel(cosine, sine, seen, upstream, peer, out_own, out_other, *rest):
-    query, own, far, log_total, out_grad, query_grad, pair_own, pair_far = rest
+def attention_back_kernel(cosine, sine, seen, upstream, peer, gathered, *rest):
+    query, own, far, log_total, out_grad, query_grad, pair_own, pair_far, out_weight = rest
     out_grad[:QUARTER, :] = upstream[...]
     out_grad[QUARTER:, :] = peer[...]
+    output_weight(gathered, out_weight)
     keys, values = keys_values(own[...], far[...])
     mask = seen[...] > 0.0
-    attended_grad = dot_across(out_grad[:, :HALF], out_own[...])
-    attended_grad = (attended_grad + dot_across(out_grad[:, HALF:], out_other[...])).astype(BF16)
+    attended_grad = dot_across(out_grad[...], out_weight[...]).astype(BF16)
     key_grad = jnp.zeros((TOK_DP, HEAD), F32)
     value_grad = jnp.zeros((TOK_DP, HEAD), F32)
     for h in range(Q_HEADS):
@@ -373,14 +435,16 @@
     pair_far[:, HEAD:] = value_grad[PAIR_ROWS:].astype(BF16)
 
 
-def input_grad_kernel(cosine, sine, query_grad, own, far, inputs, weight, *rest):
-    qkv_grad, near, peer, grad_gain = rest
+def input_grad_kernel(cosine, sine, query_grad, own, far, inputs, *rest):
+    *weights, qkv_grad, near, peer, grad_gain = rest
     pair = own[...] + far[...].astype(F32)
     qkv_grad[:, : Q_HEADS * HEAD] = query_grad[...]
     key_grad = turn(pair[:, :HEAD], cosine[...], -sine[...])
     qkv_grad[:, Q_HEADS * HEAD : QKV - HEAD] = key_grad.astype(BF16)
     qkv_grad[:, QKV - HEAD :] = pair[:, HEAD:].astype(BF16)
-    partial = dot_across(qkv_grad[...], weight[...])
+    partial = sum(
+        dot_across(qkv_grad[:, k * 256 : (k + 1) * 256], w[...]) for k, w in enumerate(weights)
+    )
     near[...] = partial[:QUARTER]
     peer[...] = partial[QUARTER:].astype(BF16)
     grad_gain[...] = jnp.sum(inputs[...].astype(F32) * partial, axis=0, keepdims=True)
@@ -412,10 +476,9 @@
     )(*operands)
 
 
-def attention_backward(upstream, cache, gain, weights, geometry, order, meanwhile, finish):
+def attention_backward(upstream, cache, gain, weights, geometry, meanwhile, between, finish):
     cosine, sine, seen, _ = geometry
     stream, inv_rms, inputs, query, pair, far, log_total, attended = cache
-    gathered, out_weight = weights
     out_grads = meanwhile(gather_two(upstream.astype(BF16)))
     width = Q_HEADS * HEAD
     out_grad, query_grad, pair_own, pair_far = local_call(
@@ -426,19 +489,21 @@
             ((PAIR_ROWS, 2 * HEAD), F32),
             ((PAIR_ROWS, 2 * HEAD), BF16),
         ],
-        [cosine, sine, seen, *out_grads, *out_weight, query, pair, far, log_total],
+        [cosine, sine, seen, *out_grads, weights, query, pair, far, log_total],
         "attention_backward",
+        {5: OUT_SPEC},
+        OUT_SCRATCH,
     )
     qkv_grad, near, peer, grad_gain = local_call(
         input_grad_kernel,
         [((PAIR_ROWS, QKV), BF16), (BLOCK, F32), (BLOCK, BF16), ((1, D), F32)],
-        [cosine, sine, query_grad, pair_own, over_col(pair_far), inputs, gathered],
+        [cosine, sine, query_grad, pair_own, over_col(between(pair_far)), inputs] + [weights] * 4,
         "attention_input_grad",
-        {6: pl.BlockSpec((D, QKV), lambda j: (0, 0))},
+        {6 + k: x for k, x in enumerate(QKV_SPECS)},
     )
     parts = (near, over_row(peer))
-    packed = attention_grads(inputs, attended, qkv_grad, out_grad, order)
-    parts = finish(parts, packed, grad_gain[0] / gain)
+    operands = (inputs, attended, qkv_grad, out_grad)
+    parts = finish(parts, operands, grad_gain[0] / gain)
     return norm_back(upstream, total(parts), stream, inv_rms, gain)
 
 
@@ -462,8 +527,9 @@
     return (mine, jnp.sum(jnp.where(mine, share, 0.0), axis=1, keepdims=True))
 
 
-def forward_kernel(x0, x1, x2, x3, chosen, router, wg, wu, wd, *rest):
-    inputs, gate, up, hidden, share, own, row, col, both, total_ref = rest
+def forward_kernel(x0, x1, x2, x3, chosen, router, wg, wu, *rest):
+    *down, inputs, gate, up, hidden, share = rest[: 6 if len(rest) > 5 else 5]
+    sends = rest[6:]
     step = pl.program_id(0)
 
     @pl.when(step == 0)
@@ -484,7 +550,10 @@
     for k in range(PARTS):
         part = slice(k * 128, (k + 1) * 128)
         hidden[:, part] = (share_of(share[...], step, k)[1] * low[:, part]).astype(BF16)
-    result = dot(hidden[...], wd[...])
+    if not down:
+        return
+    *sends, total_ref = sends
+    result = dot(hidden[...], down[0][...])
 
     @pl.when(step == 0)
     def _():
@@ -496,7 +565,7 @@
 
     @pl.when(step == STEPS - 1)
     def _():
-        send_blocks(total_ref[...], own, row, col, both)
+        send_blocks(total_ref[...], *sends)
 
 
 def weight_specs():
@@ -515,31 +584,47 @@
     return (own, over_row(row), over_col(col), over_both(both))
 
 
-def expert_forward(stream, gain, router, weights, chosen, meanwhile):
+def expert_forward(stream, gain, router, weights, chosen, meanwhile, last):
     inv_rms, normed = normalize(stream, gain)
     gathered = meanwhile(gather_four(normed))
     weights = weights[0]
+    count = 2 if last else 3
+    sends = [] if last else [jax.ShapeDtypeStruct(BLOCK, F32)]
+    sends = sends + [jax.ShapeDtypeStruct(BLOCK, BF16)] * (3 * len(sends))
     out = pl.pallas_call(
         forward_kernel,
         grid=(STEPS,),
-        in_specs=[whole(BLOCK)] * 4 + [whole(LANES), whole((128, D))] + weight_specs(),
-        out_specs=[whole(ALL), SLAB, SLAB, SLAB, whole(LANES)] + [whole(BLOCK)] * 4,
+        in_specs=[whole(BLOCK)] * 4 + [whole(LANES), whole((128, D))] + weight_specs()[:count],
+        out_specs=[whole(ALL), SLAB, SLAB, SLAB, whole(LANES)] + [whole(BLOCK)] * len(sends),
         out_shape=[
             jax.ShapeDtypeStruct(ALL, BF16),
             jax.ShapeDtypeStruct(ALL, F32),
             jax.ShapeDtypeStruct(ALL, F32),
             jax.ShapeDtypeStruct(ALL, BF16),
             jax.ShapeDtypeStruct(LANES, F32),
-            jax.ShapeDtypeStruct(BLOCK, F32),
         ]
-        + [jax.ShapeDtypeStruct(BLOCK, BF16)] * 3,
-        scratch_shapes=[pltpu.VMEM(ALL, F32)],
+        + sends,
+        scratch_shapes=[] if last else [pltpu.VMEM(ALL, F32)],
         compiler_params=pltpu.CompilerParams(vmem_limit_bytes=VMEM_LIMIT),
         cost_estimate=COST,
         name="experts_forward",
-    )(*gathered, chosen, router, weights, weights, weights)
-    inputs, gate, up, hidden, share, own, row, col, both = out
-    return ((stream, inv_rms, inputs, gate, up, share, hidden), (own, row, col, both))
+    )(*gathered, chosen, router, *[weights] * count)
+    inputs, gate, up, hidden, share, *sends = out
+    return ((stream, inv_rms, inputs, gate, up, share, hidden), sends)
+
+
+def last_down_kernel(hidden, weight, own, row, col, both):
+    send_blocks(dot(hidden[...], weight[...]), own, row, col, both)
+
+
+def last_down(hidden, weights):
+    return local_call(
+        last_down_kernel,
+        [(BLOCK, F32)] + [(BLOCK, BF16)] * 3,
+        [hidden, weights],
+        "last_down",
+        {1: pl.BlockSpec((D, D), lambda j: (0, 2))},
+    )
 
 
 def backward_kernel(y0, y1, y2, y3, gate, up, share, router, wg, wu, wd, *rest):
@@ -657,7 +742,9 @@
     parts = settle(send_four((own, row, col, both)))
     operands = (inputs, hidden, gate_grad, up_grad, out_grad, orders)
     packed = weight_grads(*operands, 0, [])
+    own, *parts = parts
     packed, *parts = tied(packed, *parts)
+    parts = (own, *parts)
     arrived = over_dp(packed, lambda i: i ^ 1)
     normed_grad = total(parts)
     router_grad = dot_down(logits_grad, inputs)
@@ -680,15 +767,17 @@
     straight = block % 16 * 2 + side
     target = (along_x + block // 4) % 4 * 8 + (along_z + block) % 4 * 2 + side
     source = jnp.arange(HALF, dtype=jnp.int32)
-    by_core, units, by_steps = [
+    target_z = (along_x + block) % 4 * 8 + (along_z + block // 4) % 4 * 2 + side
+    by_core, units, x_first, z_first = [
         (x[:, None] == source[None, :]).astype(BF16)
         for x in (
             straight * 24 + inner,
             inner // 12 * FF + straight * 12 + inner % 12,
             target * 24 + inner,
+            target_z * 24 + inner,
         )
     ]
-    return ([by_core, units], by_steps)
+    return ([by_core, units], [x_first, z_first])
 
 
 def shift_x(x, k):
@@ -719,11 +808,11 @@
     )
 
 
-def sum_everywhere(values):
-    values = values + over_row(values)
-    for step in (1, 8, 16, 2, 4):
-        values = values + over_dp(values, lambda i, step=step: i ^ step)
-    return values
+def sum_in_order(values, shift, place):
+    got = jnp.stack([values] + [shift(values, k) for k in range(1, 4)])
+    return sum(
+        lax.dynamic_index_in_dim(got, (place - j) % 4, 0, keepdims=False) for j in range(4)
+    )
 
 
 def place(expert_own, expert_other, attention, column):
@@ -791,26 +880,21 @@
         ],
         axis=0,
     )
-    small, index = tied(small, data_index)
     small_far = over_col(small)
-    own, other, qkv_own, out_own, out_send, *attention_own = take_pieces(0, index, weights, True)
+    own, other, qkv_own, out_own, out_send = take_pieces(0, data_index, weights, True)
+    small_far, other = tied(small_far, other)
     squares = small[-1, : 2 * QUARTER] + small_far[-1, : 2 * QUARTER]
     inv_rms = lax.rsqrt(squares / D + EPSILON)[:, None]
     normed = (tokens.astype(F32) * inv_rms * small[0]).astype(BF16)
     normed_pair = (normed, over_row(normed))
-    piece = expert_piece(own, over_col(other), data_index)
-    piece, out_send, *normed_pair = tied(piece, out_send, *normed_pair)
-    expert_parts = [gather_all(piece)]
-    near, away = [
-        jnp.concatenate([half_of(x, side, 0) for x in normed_pair], axis=0)
-        for side in (column, 1 - column)
-    ]
-    partial = dot(jnp.concatenate([near, away], axis=0), qkv_own)
-    qkv_far = over_col(partial[2 * QUARTER :].astype(BF16))
+    piece = whole_piece(own, over_col(other), data_index)
+    piece, peer_rows = tied(piece, normed_pair[1])
+    gathered_parts = [gather_all(piece)]
+    qkv, qkv_far, near = first_product(normed, peer_rows, qkv_own)
+    qkv_far = over_col(qkv_far)
+    data_index = later(data_index, near)
+    seq_lengths, expert_ids = [later(x, near) for x in (seq_lengths, expert_ids)]
     out_sent = over_col(out_send)
-    qkv = partial[: 2 * QUARTER]
-    qkv, data_index, seq_lengths, expert_ids = tied(qkv, data_index, seq_lengths, expert_ids)
-    loaded = take_pieces(1, data_index, weights, False)
     small = jnp.concatenate([small[:-1], small_far[:-1]], axis=1)
     gains = small[: 2 * LAYERS].reshape(LAYERS, 2, D)
     routers = small[2 * LAYERS :].reshape(LAYERS, EXPERTS, D).astype(BF16)
@@ -853,83 +937,64 @@
     )
 
     by_core, by_steps = exchange_orders(data_index)
-    attention_other = [None] * LAYERS
+    far = over_col(half_of(tokens, 1 - column, 0))
+    upstream = None
 
     def first_out(pair, pair_far):
-        nonlocal out_sent, by_core, by_steps, routers, chosen, far, loaded
-        values = tied(
-            pair, pair_far, out_sent, tokens, attention_own[1], by_steps, routers, chosen,
-            *by_core, *loaded
-        )
-        pair, pair_far, out_sent, rest, attention_own[1], by_steps, routers, chosen = values[:8]
-        by_core, loaded = values[8:10], list(values[10:])
-        attention_other[1] = over_col(attention_own[1])
-        far = to_quarter(rest, column)[:, HALF:]
-        return (pair, pair_far, (core, out_own, out_sent, over_dp(out_sent, lambda i: i ^ 1)))
-
-    far = None
-    cache, parts = attention_forward([qkv, qkv_far], geometry, first_out)
+        nonlocal far
+        pair_far, far = tied(pair_far, far)
+        return (pair, pair_far, (out_own, out_sent, over_dp(out_sent, lambda i: i ^ 1)))
+
+    cache, parts = attention_forward(*first_heads(qkv, qkv_far, geometry), geometry, first_out)
     stream = jnp.concatenate([half_of(tokens, column, 0), far], axis=1).astype(F32)
     quarter_rms = half_of(inv_rms, column, 0)
     far_normed = (far.astype(F32) * quarter_rms * gains[0, 0, HALF:]).astype(BF16)
     attention_caches = [(stream, quarter_rms, None) + cache]
     stream = stream + total(parts)
-    second_attention = attention_piece(attention_own[1], attention_other[1], data_index)
+
+    loaded = []
 
     def load_second(gathered):
-        nonlocal second_attention, upstream
-        upstream = to_quarter(cotangent, column)
-        second_attention, expert_parts[0], loaded[1], upstream, *gathered = tied(
-            second_attention, expert_parts[0], loaded[1], upstream, *gathered
-        )
+        loaded.extend(take_pieces(1, data_index, weights, False))
         loaded.append(over_col(loaded[1]))
         return gathered
 
-    upstream = None
     expert_cache, sends = expert_forward(
-        stream, gains[0, 1], routers[0], expert_parts, chosen[0], load_second
-    )
+        stream, gains[0, 1], routers[0], gathered_parts, chosen[0], load_second, False
+    )
+    second_piece = whole_piece(loaded[0], loaded[2], data_index)
+    share = expert_cache[5]
+    second_piece, share = tied(second_piece, share)
+    gathered_parts.append(gather_all(second_piece))
     stream = stream + total(send_four(sends))
-    caches = [expert_cache]
-    second_weights = attention_whole(gather_all(second_attention))
-    second_piece = expert_piece(loaded[0], loaded[2], data_index)
+    caches = [expert_cache[:5] + (share,) + expert_cache[6:]]
 
     inv_rms, normed = normalize(stream, gains[1, 0])
-    inputs = jnp.concatenate(gather_two(normed), axis=0)
-    qkv, second_piece = tied(dot(inputs, second_weights[0][:, :QKV]), second_piece)
-    expert_parts.append(gather_all(second_piece))
+    query, pair, inputs = make_heads(*gather_two(normed), gathered_parts[0], geometry)
     first_inputs = []
 
     def start_back(pair, pair_far):
-        pair, pair_far, attention_own[0], source = tied(
-            pair, pair_far, attention_own[0], far_normed
-        )
-        attention_other[0] = over_col(attention_own[0])
+        nonlocal upstream
+        pair_far, source, block = tied(pair_far, far_normed, cotangent)
+        upstream = to_quarter(block, column)
         first_inputs.append(source)
         first_inputs.append(over_row(source))
-        out_own, out_other = second_weights[1]
-        return (pair, pair_far, (0, out_own, out_other[:CORE_ROWS], out_other[CORE_ROWS:]))
-
-    cache, parts = attention_forward([qkv], geometry, start_back)
+        return (pair, pair_far, (gathered_parts[0],))
+
+    cache, parts = attention_forward(query, pair, geometry, start_back)
     attention_caches.append((stream, inv_rms, inputs) + cache)
     inputs = jnp.concatenate([near, jnp.concatenate(first_inputs, axis=0)], axis=1)
     attention_caches[0] = attention_caches[0][:2] + (inputs,) + attention_caches[0][3:]
     stream = stream + total(parts)
-    first_attention = attention_piece(attention_own[0], attention_other[0], data_index)
-
-    def load_last(gathered):
-        nonlocal first_attention, upstream
-        first_attention, expert_parts[1], upstream, *gathered = tied(
-            first_attention, expert_parts[1], upstream, *gathered
-        )
-        return gathered
-
-    expert_cache, sends = expert_forward(
-        stream, gains[1, 1], routers[1], expert_parts[1:], chosen[1], load_last
+
+    expert_cache, _ = expert_forward(
+        stream, gains[1, 1], routers[1], gathered_parts[1:], chosen[1], lambda x: x, True
     )
     caches.append(expert_cache)
-    first_whole = gather_all(first_attention)
+    last_hidden = expert_cache[-1]
     gathered = gather_four(upstream)
+    expert_parts = gathered_parts
+    second_weights, first_weights = gathered_parts
 
     upstream, finish_second, expert_gain, router_grad = expert_backward(
         upstream.astype(F32),
@@ -944,17 +1009,13 @@
     smalls = [None, expert_gain[None], router_grad]
     waiting = None
 
-    def start_first(out_grads):
-        nonlocal first_whole, expert_sum
-        expert_sum, first_whole, *out_grads = finish_second(first_whole, *out_grads)
+    expert_sum = None
+
+    def keep(parts, operands, attention_gain):
+        nonlocal waiting, expert_sum
+        expert_sum, *parts = finish_second(*parts)
         expert_sum = sum_over_cores(expert_sum)
-        return out_grads
-
-    expert_sum = None
-
-    def keep(parts, packed, attention_gain):
-        nonlocal waiting
-        waiting = packed
+        waiting = operands
         smalls[0] = attention_gain[None]
         return parts
 
@@ -964,21 +1025,11 @@
         gains[1, 0],
         second_weights,
         geometry,
-        by_steps,
-        start_first,
+        lambda x: x,
+        lambda x: x,
         keep,
     )
     gathered = gather_four(upstream.astype(BF16))
-    second_sum = sum_pairs(waiting)
-    second_sum, *gathered = tied(*second_sum, *gathered)
-    second_sum = sum_round([second_sum], (shift_x,))
-
-    def settle(parts):
-        nonlocal second_sum
-        second_sum, *parts = tied(*second_sum, *parts)
-        second_sum = sum_round([second_sum], (shift_z,))[0]
-        return parts
-
     upstream, finish_first, expert_gain, router_grad = expert_backward(
         upstream,
         caches[0],
@@ -987,23 +1038,28 @@
         expert_parts[0],
         by_core,
         gathered,
-        settle,
-    )
-    first_weights = attention_whole(first_whole)
+        lambda x: x,
+    )
     first_sum = None
     last = None
 
-    def start_sum(out_grads):
-        nonlocal sends, first_sum, expert_sum
-        values = finish_first(expert_sum, *sends, *out_grads)
-        first_sum, expert_sum, sends, out_grads = values[0], values[1], values[2:6], values[6:]
+    def finish_sum(out_grads):
+        nonlocal first_sum
+        first_sum, *out_grads = finish_first(*out_grads)
+        return out_grads
+
+    def start_sum(far_pair):
+        nonlocal first_sum, expert_sum
+        first_sum, expert_sum, far_pair = tied(first_sum, expert_sum, far_pair)
         first_sum = sum_over_cores(first_sum)
-        return out_grads
-
-    def keep_last(parts, packed, attention_gain):
-        nonlocal last, second_sum
-        *last, second_sum, own, peer = tied(*packed, second_sum, *parts)
-        last = sum_pairs(last)
+        return far_pair
+
+    def keep_last(parts, operands, attention_gain):
+        nonlocal last, waiting
+        packed = attention_grads(*operands, by_steps[0])
+        *packed, own, peer = tied(*packed, *parts)
+        values = tied(*packed, *waiting)
+        last = [sum_pairs(x)[0] for x in (values[:2], attention_grads(*values[2:], by_steps[1]))]
         smalls[:0] = [attention_gain[None], expert_gain[None], router_grad]
         return (own, peer)
 
@@ -1013,15 +1069,21 @@
         gains[0, 0],
         first_weights,
         geometry,
-        by_steps,
+        finish_sum,
         start_sum,
         keep_last,
     )
+    small = jnp.concatenate(smalls, axis=0)
+    last = sum_round(last, (shift_x, shift_z))
+    *last, last_hidden, small, expert_sum = tied(*last, last_hidden, small, expert_sum)
+    small = small[:, :HALF] + over_col(small[:, HALF:])
+    small = small + over_row(small)
+    small = small + over_dp(small, lambda i: i ^ 1)
+    along_x, along_z = data_index // 8, data_index // 2 % 4
+    small = sum_in_order(sum_in_order(small, shift_x, along_x), shift_z, along_z)
+    small = small.reshape(LAYERS, 2 + EXPERTS, HALF)
+    sends = last_down(last_hidden, gathered_parts[1])
     block_output = from_quarter((stream + total(send_four(sends))).astype(BF16), column)
-    small = jnp.concatenate(smalls, axis=0)
-    small = small[:, :HALF] + over_col(small[:, HALF:])
-    small = sum_everywhere(small).reshape(LAYERS, 2 + EXPERTS, HALF)
-    small, expert_sum, last = tied(small, expert_sum, *last)
 
     def columns(values):
         return [
@@ -1035,13 +1097,11 @@
             for k in range(2)
         ]
 
-    last = sum_round([last], (shift_x,))
     second, _ = place(*columns(expert_sum), [], column)
-    last, *second = tied(*last, *second)
-    last = sum_round([last], (shift_z,))[0]
+    last = sum_round(last, (shift_z, shift_x))
     half = QKV + HALF
     first, ((qkv_second, out_second), (qkv_first, out_first)) = place(
-        *columns(first_sum), [(x[:, :half], x[:, half:]) for x in (second_sum, last)], column
+        *columns(first_sum), [(x[:, :half], x[:, half:]) for x in last[::-1]], column
     )
     grad_tokens = from_quarter(upstream.astype(BF16), column)
 

time: 695 us -> 647 us (0.931)
  local copies, waits for them, and re-layouts: 81.4 us -> 49.5 us
  waiting for transfers between devices: 277 us -> 253 us
  starting transfers between devices: 95.2 us -> 108 us
  other arithmetic: 47.1 us -> 39.9 us
    all_gather x4 -> x2, waiting for transfers between devices: 16.8 us -> 0.01 us  [gather_all(): return lax.all_gather(piece, 'dp', axis=0, tiled=True)]
    pallas_call x8 -> x12, Pallas kernels: 32.4 us -> 43.8 us  [local_call(): pl.pallas_call(kernel, grid=(1,), in_specs=[specs.get(k) or whole(x.shape...]
    unnamed x363 -> x321, local copies, waits for them, and re-layouts: 48 us -> 37.9 us
    slice x15 -> x2, local copies, waits for them, and re-layouts: 9.55 us -> 0.52 us  [the longest x1 0.51 us: later(): return index + (value[0, 0].astype(F32) * 0.0).astype(jnp.int32)]
    ppermute x22 -> x24, starting transfers between devices: 23.3 us -> 28.4 us  [over_dp(): return lax.ppermute(x, 'dp', [(i, target(i)) for i in range(N_DP)])]
    ppermute x26 -> x24, waiting for transfers between devices: 96.1 us -> 91 us  [over_col(): return lax.ppermute(x, 'col', SWAP)]
    ppermute x26 -> x24, starting transfers between devices: 49.4 us -> 52.4 us  [over_col(): return lax.ppermute(x, 'col', SWAP)]
    ppermute x22 -> x24, waiting for transfers between devices: 75.2 us -> 72.5 us  [over_dp(): return lax.ppermute(x, 'dp', [(i, target(i)) for i in range(N_DP)])]
  transfers between devices with their start and end apart: 80 -> 78, of which waited for: 44 -> 44; matrix products, arithmetic and copies ran while one was open for 11% -> 7% of each run, Pallas kernels for 23% -> 21%
where the time goes in v4:
time: 647 us; the launch traced here: 635 us
  waiting for transfers between devices  253 us (39%)
  Pallas kernels  166 us (26%)
  starting transfers between devices  108 us (17%)
  local copies, waits for them, and re-layouts  49.5 us (8%)
  other arithmetic  39.9 us (6%)
  between operations  17.2 us (3%)
    ppermute x24, waiting for transfers between devices, over_col(): return lax.ppermute(x, 'col', SWAP)  91 us
    ppermute x24, waiting for transfers between devices, over_dp(): return lax.ppermute(x, 'dp', [(i, target(i)) for i in range(N_DP)])  72.5 us
    ppermute x18, waiting for transfers between devices, over_row(): return lax.ppermute(x, 'row', SWAP)  60.8 us
    ppermute x24, starting transfers between devices, over_col(): return lax.ppermute(x, 'col', SWAP)  52.4 us
    pallas_call x4, Pallas kernels, weight_grads(): pl.pallas_call(grads_kernel, grid=(6,), in_specs=[left(lambda j: jnp.mini...  48.5 us
    pallas_call x12, Pallas kernels, local_call(): pl.pallas_call(kernel, grid=(1,), in_specs=[specs.get(k) or whole(x.shape...  43.8 us
    unnamed x321, local copies, waits for them, and re-layouts  37.9 us
    pallas_call x2, Pallas kernels, expert_backward(): pl.pallas_call(backward_kernel, grid=(STEPS,), in_specs=[whole(BLOCK)] *...  32.9 us
  transfers between devices with their start and end apart: 78, of which 44 were waited for; matrix products, arithmetic and copies ran while one was open for 7% of the time, Pallas kernels for 21%

profile of v4, /device:TPU:6, one launch (start us, length us, event | category | flops | bytes accessed | tf_op | source)
XLA Modules:
  0.0 634.7 jit_solution(4786847854185025154)
XLA Ops:
  20.9 13.7 %collective-permute-done.1.other = bf16[48,5248]{1,0:T(8,128)(2,1)S(1)} collective-permute-done((bf16[48,5248]{1,0:T(8,128)(2,1)S(1)}, bf16[48,5248]{1,0:T(8,128)(2,1)S(1)}, u32[]{:S(2)}, u32[]{:S(2)}) %collective-permute-start.1) | collective-permute-done | bytes 503840 | tf_op jit(solution)/shard_map/ppermute | solution.py:66
  64.0 9.1 %collective-permute-done.3.far = bf16[256,1024]{1,0:T(8,128)(2,1)S(1)} collective-permute-done((bf16[256,1024]{1,0:T(8,128)(2,1)}, bf16[256,1024]{1,0:T(8,128)(2,1)S(1)}, u32[]{:S(2)}, u32[]{:S(2)}) %collective-permute-start.3) | collective-permute-done | bytes 524320 | tf_op jit(solution)/shard_map/ppermute | solution.py:66
  82.6 6.3 attention_forward.2
  107.9 5.5 collective-permute-done.26.other
  114.3 6.1 collective-permute-done.9.x1
  120.4 5.7 collective-permute-done.10.x2
  127.9 14.1 %experts_forward.2 = (bf16[512,1536]{1,0:T(8,128)(2,1)S(1)}, f32[512,1536]{1,0:T(8,128)}, f32[512,1536]{1,0:T(8,128)}, bf16[512,1536]{1,0:T(8,128)(2,1)}, f32[51...) custom-call(bf16[128,1536]{1,0:T(8,128)(2,1)S(1)} %multiply_convert_, ...), custom_call_target="tpu_custom_call" | custom-call | flops 7247757312 | bytes 25165824 | tf_op jit(solution)/shard_map/experts_forward/pallas_call | solution.py:594
  150.3 12.8 %collective-permute-done.14 = bf16[128,1536]{1,0:T(8,128)(2,1)S(1)} collective-permute-done((bf16[128,1536]{1,0:T(8,128)(2,1)}, bf16[128,1536]{1,0:T(8,128)(2,1)S(1)}, u32[]{:S(2)}, u32[]{:S(2)}) %collective-permute-start.14) | collective-permute-done | bytes 393248 | tf_op jit(solution)/shard_map/ppermute | solution.py:70
  167.0 7.5 %collective-permute-done.15.peer = bf16[128,1536]{1,0:T(8,128)(2,1)S(1)} collective-permute-done((bf16[128,1536]{1,0:T(8,128)(2,1)S(1)}, bf16[128,1536]{1,0:T(8,128)(2,1)S(1)}, u32[]{:S(2)}, u32[]{:S(2)}) %collective-permute-start.15) | collective-permute-done | bytes 393248 | tf_op jit(solution)/shard_map/ppermute | solution.py:62
  184.9 6.9 %attention_forward.3 = (bf16[256,768]{1,0:T(8,128)(2,1)S(1)}, f32[256,128]{1,0:T(8,128)S(1)}, f32[128,1536]{1,0:T(8,128)S(1)}, bf16[128,1536]{1,0:T(8,128)(2,1)S(1)}) custom-call(bf16[256,768]{1,0:T(8,128)(2,1)S(1)} %get-tuple-element.153.query.rest_0_, bf16[256,256]{1,0:T(8,128)(2,1)S(1)} %get-tuple-element.154.own.rest_1_, ...), custom_call_target="tpu_custom_call" | custom-call | flops 4294967296 | bytes 8388608 | tf_op jit(solution)/shard_map/attention_forward/pallas_call | solution.py:318
  198.3 6.6 %collective-permute-done.17 = bf16[128,1536]{1,0:T(8,128)(2,1)} collective-permute-done((bf16[128,1536]{1,0:T(8,128)(2,1)S(1)}, bf16[128,1536]{1,0:T(8,128)(2,1)}, u32[]{:S(2)}, u32[]{:S(2)}) %collective-permute-start.17) | collective-permute-done | bytes 393248 | tf_op jit(solution)/shard_map/ppermute | solution.py:62
  219.6 8.3 %collective-permute-done.24.x2 = bf16[128,1536]{1,0:T(8,128)(2,1)S(1)} collective-permute-done((bf16[128,1536]{1,0:T(8,128)(2,1)S(1)}, bf16[128,1536]{1,0:T(8,128)(2,1)S(1)}, u32[]{:S(2)}, u32[]{:S(2)}) %collective-permute-start.24) | collective-permute-done | bytes 393248 | tf_op jit(solution)/shard_map/ppermute | solution.py:66
  228.6 8.1 %collective-permute-done.25.x3 = bf16[128,1536]{1,0:T(8,128)(2,1)S(1)} collective-permute-done((bf16[128,1536]{1,0:T(8,128)(2,1)S(1)}, bf16[128,1536]{1,0:T(8,128)(2,1)S(1)}, u32[]{:S(2)}, u32[]{:S(2)}) %collective-permute-start.25) | collective-permute-done | bytes 393248 | tf_op jit(solution)/shard_map/ppermute | solution.py:70
  243.4 10.3 %experts_forward.3 = (bf16[512,1536]{1,0:T(8,128)(2,1)S(1)}, f32[512,1536]{1,0:T(8,128)}, f32[512,1536]{1,0:T(8,128)}, bf16[512,1536]{1,0:T(8,128)(2,1)S(1)}, f32[512,128]{1,0:T(8,128)S(1)}) custom-call(bf16[128,1536]{1,0:T(8,128)(2,1)S(1)} %copy-done.11, bf16[128,1536]{1,0:T(8,128)(2,1)S(1)} %copy-done.34, bf16[128,1536]{1,0:T(8,128)(2,1)S(1)} %copy-done.36, ...), custom_call_target="tpu_custom_call" | custom-call | flops 7247757312 | bytes 25165824 | tf_op jit(solution)/shard_map/experts_forward/pallas_call | solution.py:594
  253.8 16.9 %experts_backward.2 = (bf16[512,1536]{1,0:T(8,128)(2,1)S(1)}, bf16[512,1536]{1,0:T(8,128)(2,1)}, bf16[512,1536]{1,0:T(8,128)(2,1)}, bf16[512,256]{1,0:T(8,128)(2...) custom-call(bf16[128,1536]{1,0:T(8,128)(2,1)} %get-tuple-element.390, ...), custom_call_target="tpu_custom_call" | custom-call | flops 7247757312 | bytes 25165824 | tf_op jit(solution)/shard_map/experts_backward/pallas_call | solution.py:726
  276.6 10.5 %expert_weight_grads.4 = bf16[384,9216]{1,0:T(8,128)(2,1)} custom-call(bf16[512,1536]{1,0:T(8,128)(2,1)S(1)} %get-tuple-element.171.inputs, bf16[512,1536]{1,0:T(8,128)(2,1)S(1)} %get-tuple-element.239.hidden, bf16[512,1536]{1,0:T(8,128)(2,1)} %get-tuple-element.173.gate_grad, bf16[512,1536]{1,0:T(8,128)(2,1)} %get-tuple-element.174.up_grad, ...), custom_call_target="tpu_custom_call" | custom-call | flops 4831838208 | bytes 25165824 | tf_op jit(solution)/shard_map/expert_weight_grads/pallas_call | solution.py:703
  291.8 11.5 %collective-permute-done.31.peer = bf16[128,1536]{1,0:T(8,128)(2,1)S(1)} collective-permute-done((bf16[128,1536]{1,0:T(8,128)(2,1)S(1)}, bf16[128,1536]{1,0:T(8,128)(2,1)S(1)}, u32[]{:S(2)}, u32[]{:S(2)}) %collective-permute-start.31) | collective-permute-done | bytes 393248 | tf_op jit(solution)/shard_map/ppermute | solution.py:62
  303.3 6.2 attention_backward.2
  322.0 13.6 %expert_weight_grads.5 = f32[384,9216]{1,0:T(8,128)} custom-call(bf16[512,1536]{1,0:T(8,128)(2,1)S(1)} %get-tuple-element.171.inputs, bf16[512,1536]{1,0:T(8,128)(2,1)S(1)} %get-tuple-element.239.hidden, bf16[512,1536]{1,0:T(8,128)(2,1)} %get-tuple-element.173.gate_grad, bf16[512,1536]{1,0:T(8,128)(2,1)} %get-tuple-element.174.up_grad, ...), custom_call_target="tpu_custom_call" | custom-call | flops 4831838208 | bytes 25165824 | tf_op jit(solution)/shard_map/expert_weight_grads/pallas_call | solution.py:703
  345.4 7.0 %collective-permute-done.34.y1 = bf16[128,1536]{1,0:T(8,128)(2,1)S(1)} collective-permute-done((bf16[128,1536]{1,0:T(8,128)(2,1)S(1)}, bf16[128,1536]{1,0:T(8,128)(2,1)S(1)}, u32[]{:S(2)}, u32[]{:S(2)}) %collective-permute-start.34) | collective-permute-done | bytes 393248 | tf_op jit(solution)/shard_map/ppermute | solution.py:62
  352.4 7.3 %collective-permute-done.35.y2 = bf16[128,1536]{1,0:T(8,128)(2,1)S(1)} collective-permute-done((bf16[128,1536]{1,0:T(8,128)(2,1)S(1)}, bf16[128,1536]{1,0:T(8,128)(2,1)S(1)}, u32[]{:S(2)}, u32[]{:S(2)}) %collective-permute-start.35) | collective-permute-done | bytes 393248 | tf_op jit(solution)/shard_map/ppermute | solution.py:66
  362.6 16.0 %experts_backward.3 = (bf16[512,1536]{1,0:T(8,128)(2,1)S(1)}, bf16[512,1536]{1,0:T(8,128)(2,1)}, bf16[512,1536]{1,0:T(8,128)(2,1)}, bf16[512,256]{1,0:T(8,128)(2...) custom-call(bf16[128,1536]{1,0:T(8,128)(2,1)S(1)} %get-tuple-element, ...), custom_call_target="tpu_custom_call" | custom-call | flops 7247757312 | bytes 25165824 | tf_op jit(solution)/shard_map/experts_backward/pallas_call | solution.py:726
  384.5 10.7 %expert_weight_grads.6 = bf16[384,9216]{1,0:T(8,128)(2,1)} custom-call(bf16[512,1536]{1,0:T(8,128)(2,1)S(1)} %copy-done.2, bf16[512,1536]{1,0:T(8,128)(2,1)S(1)} %copy-done.20, bf16[512,1536]{1,0:T(8,128)(2,1)} %get-tuple-element.195.gate_grad, bf16[512,1536]{1,0:T(8,128)(2,1)} %get-tuple-element.196.up_grad, bf16[512,1536]{1,0:T(8,128)(2,1)} %copy-done.22, ...), custom_call_target="tpu_custom_call" | custom-call | flops 4831838208 | bytes 25165824 | tf_op jit(solution)/shard_map/expert_weight_grads/pallas_call | solution.py:703
  402.0 9.6 %collective-permute-done.40.rest_0_ = bf16[384,9216]{1,0:T(8,128)(2,1)} collective-permute-done((bf16[384,9216]{1,0:T(8,128)(2,1)}, bf16[384,9216]{1,0:T(8,128)(2,1)}, u32[]{:S(2)}, u32[]{:S(2)}) %collective-permute-start.40) | collective-permute-done | bytes 7077920 | tf_op jit(solution)/shard_map/ppermute | solution.py:74
  411.6 13.6 %expert_weight_grads.7 = f32[384,9216]{1,0:T(8,128)} custom-call(bf16[512,1536]{1,0:T(8,128)(2,1)S(1)} %copy-done.2, bf16[512,1536]{1,0:T(8,128)(2,1)S(1)} %copy-done.20, bf16[512,1536]{1,0:T(8,128)(2,1)} %get-tuple-element.195.gate_grad, bf16[512,1536]{1,0:T(8,128)(2,1)} %get-tuple-element.196.up_grad, bf16[512,1536]{1,0:T(8,128)(2,1)} %copy-done.22, ...), custom_call_target="tpu_custom_call" | custom-call | flops 4831838208 | bytes 25165824 | tf_op jit(solution)/shard_map/expert_weight_grads/pallas_call | solution.py:703
  430.0 6.3 attention_backward.3
  454.5 6.2 attention_weight_grads.2
  463.3 6.2 attention_weight_grads.3
  472.3 7.6 %collective-permute-done.56 = bf16[128,768]{1,0:T(8,128)(2,1)S(1)} collective-permute-done((bf16[128,768]{1,0:T(8,128)(2,1)S(1)}, bf16[128,768]{1,0:T(8,128)(2,1)S(1)}, u32[]{:S(2)}, u32[]{:S(2)}) %collective-permute-start.56) | collective-permute-done | bytes 196640 | tf_op jit(solution)/shard_map/ppermute | solution.py:66
  496.8 17.9 %collective-permute-done.47 = bf16[96,3584]{1,0:T(8,128)(2,1)S(1)} collective-permute-done((bf16[96,3584]{1,0:T(8,128)(2,1)S(1)}, bf16[96,3584]{1,0:T(8,128)(2,1)S(1)}, u32[]{:S(2)}, u32[]{:S(2)}) %collective-permute-start.47) | collective-permute-done | bytes 688160 | tf_op jit(solution)/shard_map/ppermute | solution.py:74
  517.7 21.1 %collective-permute-done.46 = bf16[96,3584]{1,0:T(8,128)(2,1)S(1)} collective-permute-done((bf16[96,3584]{1,0:T(8,128)(2,1)S(1)}, bf16[96,3584]{1,0:T(8,128)(2,1)S(1)}, u32[]{:S(2)}, u32[]{:S(2)}) %collective-permute-start.46) | collective-permute-done | bytes 688160 | tf_op jit(solution)/shard_map/ppermute | solution.py:74
  615.4 6.8 %collective-permute-done.72 = bf16[24,8192]{1,0:T(8,128)(2,1)S(1)} collective-permute-done((bf16[24,8192]{1,0:T(8,128)(2,1)S(1)}, bf16[24,8192]{1,0:T(8,128)(2,1)S(1)}, u32[]{:S(2)}, u32[]{:S(2)}) %collective-permute-start.72) | collective-permute-done | bytes 393248 | tf_op jit(solution)/shard_map/ppermute | solution.py:66
  (639 shorter events, 301.4 us)
Async XLA Ops:
  7.2 119.7 %all-gather.3.cloned.1.call-start = ((), (), s32[]{:S(2)}) async-start(), calls=%async_computation.2 | async-start | bytes 20275200 | tf_op jit(solution)/shard_map/all_gather | solution.py:227
  19.2 20.7 %collective-permute-start.2 = (bf16[256,768]{1,0:T(8,128)(2,1)S(1)}, bf16[256,768]{1,0:T(8,128)(2,1)S(1)}, u32[]{:S(2)}, u32[]{:S(2)}) collective-permute-start(bf16[256,768]{1,0:T(8,128)(2,1)S(1)} %fusion.7.own), channel_id=1, source_target_pairs={{0,2},{2,0},{1,3},{3,1},{4,6},{6,4},{5,7},{7,5},{8,10},{10,8},{9,1... | collective-permute-start | bytes 1179656 | tf_op jit(solution)/shard_map/ppermute | solution.py:62
  40.0 197.5 %all-gather.5.cloned.1.call-start = ((), (), s32[]{:S(2)}) async-start(), calls=%async_computation.3 | async-start | bytes 20275200 | tf_op jit(solution)/shard_map/all_gather | solution.py:227
  41.9 35.8 %collective-permute-start.5 = (bf16[128,768]{1,0:T(8,128)(2,1)}, bf16[128,768]{1,0:T(8,128)(2,1)S(1)}, u32[]{:S(2)}, u32[]{:S(2)}) collective-permute-start(bf16[128,768]{1,0:T(8,128)(2,1)} %get-tuple-element.398), channel_id=1, source_target_pairs={{0,1},{1,0},{2,3},{3,2},{4,5},{5,4},{6,7},{7,6},{8,9},{9,8},{10,11... | collective-permute-start | bytes 589832 | tf_op jit(solution)/shard_map/ppermute | solution.py:66
  44.8 19.2 %collective-permute-start.6 = (bf16[384,768]{1,0:T(8,128)(2,1)S(1)}, bf16[384,768]{1,0:T(8,128)(2,1)}, u32[]{:S(2)}, u32[]{:S(2)}) collective-permute-start(bf16[384,768]{1,0:T(8,128)(2,1)S(1)} %get-tuple-element.145), channel_id=1, source_target_pairs={{0,1},{1,0},{2,3},{3,2},{4,5},{5,4},{6,7},{7,6},{8,9},{9,8},{10,11... | collective-permute-start | bytes 1769480 | tf_op jit(solution)/shard_map/ppermute | solution.py:66
  54.1 19.1 %collective-permute-start.3 = (bf16[256,1024]{1,0:T(8,128)(2,1)}, bf16[256,1024]{1,0:T(8,128)(2,1)S(1)}, u32[]{:S(2)}, u32[]{:S(2)}) collective-permute-start(bf16[256,1024]{1,0:T(8,128)(2,1)} %copy-done.65), channel_id=1, source_target_pairs={{0,1},{1,0},{2,3},{3,2},{4,5},{5,4},{6,7},{7,6},{8,9},{9,8},{10,11... | collective-permute-start | bytes 1572872 | tf_op jit(solution)/shard_map/ppermute | solution.py:66
  92.0 21.4 %collective-permute-start.26 = (bf16[48,5248]{1,0:T(8,128)(2,1)S(1)}, bf16[48,5248]{1,0:T(8,128)(2,1)S(1)}, u32[]{:S(2)}, u32[]{:S(2)}) collective-permute-start(bf16[48,5248]{1,0:T(8,128)(2,1)S(1)} %get-tuple-element.164), channel_id=1, source_target_pairs={{0,1},{1,0},{2,3},{3,2},{4,5},{5,4},{6,7},{7,6},{8,9},{9,8},{10,11... | collective-permute-start | bytes 1511432 | tf_op jit(solution)/shard_map/ppermute | solution.py:66
  102.1 18.3 %collective-permute-start.9 = (bf16[128,1536]{1,0:T(8,128)(2,1)S(1)}, bf16[128,1536]{1,0:T(8,128)(2,1)S(1)}, u32[]{:S(2)}, u32[]{:S(2)}) collective-permute-start(bf16[128,1536]{1,0:T(8,128)(2,1)S(1)} %multiply_convert_fusion.2.x0), channel_id=1, source_target_pairs={{0,2},{2,0},{1,3},{3,1},{4,6},{6,4},{5,7},{7,5},{8,10},{10,8},{9,1... | collective-permute-start | bytes 1179656 | tf_op jit(solution)/shard_map/ppermute | solution.py:62
  103.0 23.1 %collective-permute-start.10 = (bf16[128,1536]{1,0:T(8,128)(2,1)}, bf16[128,1536]{1,0:T(8,128)(2,1)S(1)}, u32[]{:S(2)}, u32[]{:S(2)}) collective-permute-start(bf16[128,1536]{1,0:T(8,128)(2,1)} %pad_maximum_fusion.1), channel_id=1, source_target_pairs={{0,1},{1,0},{2,3},{3,2},{4,5},{5,4},{6,7},{7,6},{8,9},{9,8},{10,11... | collective-permute-start | bytes 1179656 | tf_op jit(solution)/shard_map/ppermute | solution.py:66
  106.4 19.7 %collective-permute-start.11 = (bf16[128,1536]{1,0:T(8,128)(2,1)}, bf16[128,1536]{1,0:T(8,128)(2,1)S(1)}, u32[]{:S(2)}, u32[]{:S(2)}) collective-permute-start(bf16[128,1536]{1,0:T(8,128)(2,1)} %pad_maximum_fusion.1), channel_id=1, source_target_pairs={{0,3},{1,2},{2,1},{3,0},{4,7},{5,6},{6,5},{7,4},{8,11},{9,10},{10,... | collective-permute-start | bytes 1179656 | tf_op jit(solution)/shard_map/ppermute | solution.py:70
  146.1 291.4 %reduce-scatter.7.cloned.1.call-start = ((), (), s32[]{:S(2)}) async-start(), calls=%async_computation.4 | async-start | bytes 15040512
  206.9 21.0 %collective-permute-start.24 = (bf16[128,1536]{1,0:T(8,128)(2,1)S(1)}, bf16[128,1536]{1,0:T(8,128)(2,1)S(1)}, u32[]{:S(2)}, u32[]{:S(2)}) collective-permute-start(bf16[128,1536]{1,0:T(8,128)(2,1)S(1)} %pad_maximum_fusion.4), channel_id=1, source_target_pairs={{0,1},{1,0},{2,3},{3,2},{4,5},{5,4},{6,7},{7,6},{8,9},{9,8},{10,11... | collective-permute-start | bytes 1179656 | tf_op jit(solution)/shard_map/ppermute | solution.py:66
  209.6 27.1 %collective-permute-start.25 = (bf16[128,1536]{1,0:T(8,128)(2,1)S(1)}, bf16[128,1536]{1,0:T(8,128)(2,1)S(1)}, u32[]{:S(2)}, u32[]{:S(2)}) collective-permute-start(bf16[128,1536]{1,0:T(8,128)(2,1)S(1)} %pad_maximum_fusion.4), channel_id=1, source_target_pairs={{0,3},{1,2},{2,1},{3,0},{4,7},{5,6},{6,5},{7,4},{8,11},{9,10},{10,... | collective-permute-start | bytes 1179656 | tf_op jit(solution)/shard_map/ppermute | solution.py:70
  213.1 40.7 %collective-permute-start.21 = (bf16[128,1536]{1,0:T(8,128)(2,1)}, bf16[128,1536]{1,0:T(8,128)(2,1)}, u32[]{:S(2)}, u32[]{:S(2)}) collective-permute-start(bf16[128,1536]{1,0:T(8,128)(2,1)} %get-tuple-element.389), channel_id=1, source_target_pairs={{0,1},{1,0},{2,3},{3,2},{4,5},{5,4},{6,7},{7,6},{8,9},{9,8},{10,11... | collective-permute-start | bytes 1179656 | tf_op jit(solution)/shard_map/ppermute | solution.py:66
  213.4 40.4 %collective-permute-start.22 = (bf16[128,1536]{1,0:T(8,128)(2,1)}, bf16[128,1536]{1,0:T(8,128)(2,1)}, u32[]{:S(2)}, u32[]{:S(2)}) collective-permute-start(bf16[128,1536]{1,0:T(8,128)(2,1)} %get-tuple-element.389), channel_id=1, source_target_pairs={{0,3},{1,2},{2,1},{3,0},{4,7},{5,6},{6,5},{7,4},{8,11},{9,10},{10,... | collective-permute-start | bytes 1179656 | tf_op jit(solution)/shard_map/ppermute | solution.py:70
  219.2 34.5 %collective-permute-start.20 = (bf16[128,1536]{1,0:T(8,128)(2,1)}, bf16[128,1536]{1,0:T(8,128)(2,1)}, u32[]{:S(2)}, u32[]{:S(2)}) collective-permute-start(bf16[128,1536]{1,0:T(8,128)(2,1)} %get-tuple-element.390.y0), channel_id=1, source_target_pairs={{0,2},{2,0},{1,3},{3,1},{4,6},{6,4},{5,7},{7,5},{8,10},{10,8},{9,1... | collective-permute-start | bytes 1179656 | tf_op jit(solution)/shard_map/ppermute | solution.py:62
  288.2 33.8 %collective-permute-start.30 = (bf16[384,9216]{1,0:T(8,128)(2,1)}, bf16[384,9216]{1,0:T(8,128)(2,1)}, u32[]{:S(2)}, u32[]{:S(2)}) collective-permute-start(bf16[384,9216]{1,0:T(8,128)(2,1)} %expert_weight_grads.4), channel_id=1, source_target_pairs={{0,4},{4,0},{8,12},{12,8},{16,20},{20,16},{24,28},{28,24},{32,36},... | collective-permute-start | bytes 21233672 | tf_op jit(solution)/shard_map/ppermute | solution.py:74
  335.7 275.8 %reduce-scatter.9.cloned.1.call-start = ((), (), s32[]{:S(2)}) async-start(), calls=%async_computation.5 | async-start | bytes 15040512
  341.9 17.7 %collective-permute-start.35 = (bf16[128,1536]{1,0:T(8,128)(2,1)S(1)}, bf16[128,1536]{1,0:T(8,128)(2,1)S(1)}, u32[]{:S(2)}, u32[]{:S(2)}) collective-permute-start(bf16[128,1536]{1,0:T(8,128)(2,1)S(1)} %pad_maximum_fusion.5), channel_id=1, source_target_pairs={{0,1},{1,0},{2,3},{3,2},{4,5},{5,4},{6,7},{7,6},{8,9},{9,8},{10,11... | collective-permute-start | bytes 1179656 | tf_op jit(solution)/shard_map/ppermute | solution.py:66
  343.8 18.8 %collective-permute-start.36 = (bf16[128,1536]{1,0:T(8,128)(2,1)S(1)}, bf16[128,1536]{1,0:T(8,128)(2,1)S(1)}, u32[]{:S(2)}, u32[]{:S(2)}) collective-permute-start(bf16[128,1536]{1,0:T(8,128)(2,1)S(1)} %pad_maximum_fusion.5), channel_id=1, source_target_pairs={{0,3},{1,2},{2,1},{3,0},{4,7},{5,6},{6,5},{7,4},{8,11},{9,10},{10,... | collective-permute-start | bytes 1179656 | tf_op jit(solution)/shard_map/ppermute | solution.py:70
  401.6 23.7 %collective-permute-start.41 = (bf16[128,1536]{1,0:T(8,128)(2,1)S(1)}, bf16[128,1536]{1,0:T(8,128)(2,1)}, u32[]{:S(2)}, u32[]{:S(2)}) collective-permute-start(bf16[128,1536]{1,0:T(8,128)(2,1)S(1)} %get-tuple-element.206.upstream), channel_id=1, source_target_pairs={{0,2},{2,0},{1,3},{3,1},{4,6},{6,4},{5,7},{7,5},{8,10},{10,8},{9,1... | collective-permute-start | bytes 1179656 | tf_op jit(solution)/shard_map/ppermute | solution.py:62
  462.5 18.2 %collective-permute-start.44 = (bf16[384,3584]{1,0:T(8,128)(2,1)}, bf16[384,3584]{1,0:T(8,128)(2,1)}, u32[]{:S(2)}, u32[]{:S(2)}) collective-permute-start(bf16[384,3584]{1,0:T(8,128)(2,1)} %get-tuple-element.227), channel_id=1, source_target_pairs={{0,4},{4,0},{8,12},{12,8},{16,20},{20,16},{24,28},{28,24},{32,36},... | collective-permute-start | bytes 8257544 | tf_op jit(solution)/shard_map/ppermute | solution.py:74
  469.5 19.9 %collective-permute-start.48 = (bf16[384,3584]{1,0:T(8,128)(2,1)}, bf16[384,3584]{1,0:T(8,128)(2,1)}, u32[]{:S(2)}, u32[]{:S(2)}) collective-permute-start(bf16[384,3584]{1,0:T(8,128)(2,1)} %get-tuple-element.233), channel_id=1, source_target_pairs={{0,4},{4,0},{8,12},{12,8},{16,20},{20,16},{24,28},{28,24},{32,36},... | collective-permute-start | bytes 8257544 | tf_op jit(solution)/shard_map/ppermute | solution.py:74
  484.5 30.2 %collective-permute-start.47 = (bf16[96,3584]{1,0:T(8,128)(2,1)S(1)}, bf16[96,3584]{1,0:T(8,128)(2,1)S(1)}, u32[]{:S(2)}, u32[]{:S(2)}) collective-permute-start(bf16[96,3584]{1,0:T(8,128)(2,1)S(1)} %get-tuple-element.323), channel_id=1, source_target_pairs={{0,96},{4,100},{8,104},{12,108},{16,112},{20,116},{24,120},{28,124... | collective-permute-start | bytes 2064392 | tf_op jit(solution)/shard_map/ppermute | solution.py:74
  486.7 52.1 %collective-permute-start.46 = (bf16[96,3584]{1,0:T(8,128)(2,1)S(1)}, bf16[96,3584]{1,0:T(8,128)(2,1)S(1)}, u32[]{:S(2)}, u32[]{:S(2)}) collective-permute-start(bf16[96,3584]{1,0:T(8,128)(2,1)S(1)} %get-tuple-element.324), channel_id=1, source_target_pairs={{0,64},{4,68},{8,72},{12,76},{16,80},{20,84},{24,88},{28,92},{32,9... | collective-permute-start | bytes 2064392 | tf_op jit(solution)/shard_map/ppermute | solution.py:74
  488.1 50.6 %collective-permute-start.45 = (bf16[96,3584]{1,0:T(8,128)(2,1)S(1)}, bf16[96,3584]{1,0:T(8,128)(2,1)S(1)}, u32[]{:S(2)}, u32[]{:S(2)}) collective-permute-start(bf16[96,3584]{1,0:T(8,128)(2,1)S(1)} %get-tuple-element.322), channel_id=1, source_target_pairs={{0,32},{4,36},{8,40},{12,44},{16,48},{20,52},{24,56},{28,60},{32,6... | collective-permute-start | bytes 2064392 | tf_op jit(solution)/shard_map/ppermute | solution.py:74
  492.0 47.1 %collective-permute-start.51 = (bf16[96,3584]{1,0:T(8,128)(2,1)S(1)}, bf16[96,3584]{1,0:T(8,128)(2,1)S(1)}, u32[]{:S(2)}, u32[]{:S(2)}) collective-permute-start(bf16[96,3584]{1,0:T(8,128)(2,1)S(1)} %get-tuple-element.320), channel_id=1, source_target_pairs={{0,24},{4,28},{8,0},{12,4},{16,8},{20,12},{24,16},{28,20},{32,56},... | collective-permute-start | bytes 2064392 | tf_op jit(solution)/shard_map/ppermute | solution.py:74
  496.1 43.1 %collective-permute-start.50 = (bf16[96,3584]{1,0:T(8,128)(2,1)S(1)}, bf16[96,3584]{1,0:T(8,128)(2,1)S(1)}, u32[]{:S(2)}, u32[]{:S(2)}) collective-permute-start(bf16[96,3584]{1,0:T(8,128)(2,1)S(1)} %get-tuple-element.321), channel_id=1, source_target_pairs={{0,16},{4,20},{8,24},{12,28},{16,0},{20,4},{24,8},{28,12},{32,48},... | collective-permute-start | bytes 2064392 | tf_op jit(solution)/shard_map/ppermute | solution.py:74
  514.8 26.3 %collective-permute-start.49 = (bf16[96,3584]{1,0:T(8,128)(2,1)S(1)}, bf16[96,3584]{1,0:T(8,128)(2,1)S(1)}, u32[]{:S(2)}, u32[]{:S(2)}) collective-permute-start(bf16[96,3584]{1,0:T(8,128)(2,1)S(1)} %get-tuple-element.319), channel_id=1, source_target_pairs={{0,8},{4,12},{8,16},{12,20},{16,24},{20,28},{24,0},{28,4},{32,40},... | collective-permute-start | bytes 2064392 | tf_op jit(solution)/shard_map/ppermute | solution.py:74
  546.5 55.4 %collective-permute-start.54 = (bf16[128,1536]{1,0:T(8,128)(2,1)S(1)}, bf16[128,1536]{1,0:T(8,128)(2,1)}, u32[]{:S(2)}, u32[]{:S(2)}) collective-permute-start(bf16[128,1536]{1,0:T(8,128)(2,1)S(1)} %get-tuple-element.243), channel_id=1, source_target_pairs={{0,3},{1,2},{2,1},{3,0},{4,7},{5,6},{6,5},{7,4},{8,11},{9,10},{10,... | collective-permute-start | bytes 1179656 | tf_op jit(solution)/shard_map/ppermute | solution.py:70
  551.8 18.2 %collective-permute-start.70 = (bf16[24,3584]{1,0:T(8,128)(2,1)S(1)}, bf16[24,3584]{1,0:T(8,128)(2,1)S(1)}, u32[]{:S(2)}, u32[]{:S(2)}) collective-permute-start(bf16[24,3584]{1,0:T(8,128)(2,1)S(1)} %get-tuple-element.330), channel_id=1, source_target_pairs={{0,64},{4,68},{8,72},{12,76},{16,80},{20,84},{24,88},{28,92},{32,9... | collective-permute-start | bytes 516104 | tf_op jit(solution)/shard_map/ppermute | solution.py:74
  560.9 41.0 %collective-permute-start.53 = (bf16[128,1536]{1,0:T(8,128)(2,1)S(1)}, bf16[128,1536]{1,0:T(8,128)(2,1)}, u32[]{:S(2)}, u32[]{:S(2)}) collective-permute-start(bf16[128,1536]{1,0:T(8,128)(2,1)S(1)} %get-tuple-element.242), channel_id=1, source_target_pairs={{0,1},{1,0},{2,3},{3,2},{4,5},{5,4},{6,7},{7,6},{8,9},{9,8},{10,11... | collective-permute-start | bytes 1179656 | tf_op jit(solution)/shard_map/ppermute | solution.py:66
  (182 other events, 1575.9 us)
Sparse Core Ops, SparseCore 0:
  40.1 81.4 all-gather.2
  146.2 79.8 all-gather.4
  335.8 101.6 reduce-scatter.6
  441.2 140.1 reduce-scatter.8

commit v5 on v4

--- a/solution.py
+++ b/solution.py
@@ -99,8 +99,12 @@
     return lax.optimization_barrier(values)
 
 
+def none_of(value):
+    return value[0, 0].astype(F32) * 0.0
+
+
 def later(index, value):
-    return index + (value[0, 0].astype(F32) * 0.0).astype(jnp.int32)
+    return index + none_of(value).astype(jnp.int32)
 
 
 def pack(parts):
@@ -1055,14 +1059,19 @@
         return far_pair
 
     def keep_last(parts, operands, attention_gain):
-        nonlocal last, waiting
+        nonlocal last, small
+        small = jnp.concatenate([attention_gain[None], expert_gain[None], router_grad] + smalls)
+        small = small[:, :HALF] + over_col(small[:, HALF:])
         packed = attention_grads(*operands, by_steps[0])
-        *packed, own, peer = tied(*packed, *parts)
-        values = tied(*packed, *waiting)
-        last = [sum_pairs(x)[0] for x in (values[:2], attention_grads(*values[2:], by_steps[1]))]
-        smalls[:0] = [attention_gain[None], expert_gain[None], router_grad]
-        return (own, peer)
-
+        small = small + none_of(packed[0])
+        after_first = by_steps[1] + none_of(packed[0]).astype(BF16)
+        second_packed = attention_grads(*waiting, after_first)
+        small = small + over_row(small) + none_of(second_packed[0])
+        last = [sum_pairs(x)[0] for x in (packed, second_packed)]
+        small = small + over_dp(small, lambda i: i ^ 1)
+        return parts
+
+    small = None
     upstream = attention_backward(
         upstream,
         attention_caches[0],
@@ -1073,18 +1082,13 @@
         start_sum,
         keep_last,
     )
-    small = jnp.concatenate(smalls, axis=0)
+    expert_sum = expert_sum + none_of(last[1])
+    last_hidden = last_hidden + none_of(last[1]).astype(BF16)
     last = sum_round(last, (shift_x, shift_z))
-    *last, last_hidden, small, expert_sum = tied(*last, last_hidden, small, expert_sum)
-    small = small[:, :HALF] + over_col(small[:, HALF:])
-    small = small + over_row(small)
-    small = small + over_dp(small, lambda i: i ^ 1)
+    small = small + none_of(last[0]) + none_of(last[1])
     along_x, along_z = data_index // 8, data_index // 2 % 4
     small = sum_in_order(sum_in_order(small, shift_x, along_x), shift_z, along_z)
     small = small.reshape(LAYERS, 2 + EXPERTS, HALF)
-    sends = last_down(last_hidden, gathered_parts[1])
-    block_output = from_quarter((stream + total(send_four(sends))).astype(BF16), column)
-
     def columns(values):
         return [
             jnp.concatenate(
@@ -1098,7 +1102,11 @@
         ]
 
     second, _ = place(*columns(expert_sum), [], column)
+    sends = send_four(last_down(last_hidden, gathered_parts[1]))
+    *last, second[0], far_send = tied(*last, second[0], sends[3])
     last = sum_round(last, (shift_z, shift_x))
+    stream = stream + total((*sends[:3], far_send))
+    block_output = from_quarter(stream.astype(BF16), column)
     half = QKV + HALF
     first, ((qkv_second, out_second), (qkv_first, out_first)) = place(
         *columns(first_sum), [(x[:, :half], x[:, half:]) for x in last[::-1]], column

time: 647 us -> 625 us (0.966)
  waiting for transfers between devices: 253 us -> 214 us
  local copies, waits for them, and re-layouts: 49.5 us -> 58.5 us
    ppermute x24, waiting for transfers between devices: 72.5 us -> 48 us  [over_dp(): return lax.ppermute(x, 'dp', [(i, target(i)) for i in range(N_DP)])]
    ppermute x24, starting transfers between devices: 52.4 us -> 61.8 us  [over_col(): return lax.ppermute(x, 'col', SWAP)]
    ppermute x18, waiting for transfers between devices: 60.8 us -> 52.1 us  [over_row(): return lax.ppermute(x, 'row', SWAP)]
    unnamed x321 -> x354, local copies, waits for them, and re-layouts: 37.9 us -> 41 us
  transfers between devices with their start and end apart: 78 -> 78, of which waited for: 44 -> 39; matrix products, arithmetic and copies ran while one was open for 7% -> 9% of each run, Pallas kernels for 21% -> 22%
where the time goes in v5:
time: 625 us; the launch traced here: 614 us
  waiting for transfers between devices  214 us (34%)
  Pallas kernels  166 us (27%)
  starting transfers between devices  110 us (18%)
  local copies, waits for them, and re-layouts  58.5 us (9%)
  other arithmetic  42.7 us (7%)
  between operations  20.3 us (3%)
    ppermute x24, waiting for transfers between devices, over_col(): return lax.ppermute(x, 'col', SWAP)  87.7 us
    ppermute x24, starting transfers between devices, over_col(): return lax.ppermute(x, 'col', SWAP)  61.8 us
    ppermute x18, waiting for transfers between devices, over_row(): return lax.ppermute(x, 'row', SWAP)  52.1 us
    pallas_call x4, Pallas kernels, weight_grads(): pl.pallas_call(grads_kernel, grid=(6,), in_specs=[left(lambda j: jnp.mini...  48.4 us
    ppermute x24, waiting for transfers between devices, over_dp(): return lax.ppermute(x, 'dp', [(i, target(i)) for i in range(N_DP)])  48 us
    pallas_call x12, Pallas kernels, local_call(): pl.pallas_call(kernel, grid=(1,), in_specs=[specs.get(k) or whole(x.shape...  44.5 us
    unnamed x354, local copies, waits for them, and re-layouts  41 us
    pallas_call x2, Pallas kernels, expert_backward(): pl.pallas_call(backward_kernel, grid=(STEPS,), in_specs=[whole(BLOCK)] *...  32.5 us
  transfers between devices with their start and end apart: 78, of which 39 were waited for; matrix products, arithmetic and copies ran while one was open for 9% of the time, Pallas kernels for 22%

profile of v5, /device:TPU:6, one launch (start us, length us, event | category | flops | bytes accessed | tf_op | source)
XLA Modules:
  0.0 614.4 jit_solution(16760784200616336130)
XLA Ops:
  20.9 13.7 %collective-permute-done.1.other = bf16[48,5248]{1,0:T(8,128)(2,1)S(1)} collective-permute-done((bf16[48,5248]{1,0:T(8,128)(2,1)S(1)}, bf16[48,5248]{1,0:T(8,128)(2,1)S(1)}, u32[]{:S(2)}, u32[]{:S(2)}) %collective-permute-start.1) | collective-permute-done | bytes 503840 | tf_op jit(solution)/shard_map/ppermute | solution.py:66
  64.1 9.1 %collective-permute-done.3.far = bf16[256,1024]{1,0:T(8,128)(2,1)S(1)} collective-permute-done((bf16[256,1024]{1,0:T(8,128)(2,1)}, bf16[256,1024]{1,0:T(8,128)(2,1)S(1)}, u32[]{:S(2)}, u32[]{:S(2)}) %collective-permute-start.3) | collective-permute-done | bytes 524320 | tf_op jit(solution)/shard_map/ppermute | solution.py:66
  81.4 6.3 %attention_forward.2 = (bf16[256,768]{1,0:T(8,128)(2,1)S(1)}, f32[256,128]{1,0:T(8,128)S(1)}, f32[128,1536]{1,0:T(8,128)S(1)}, bf16[128,1536]{1,0:T(8,128)(2,1)S(1)}) custom-call(bf16[256,768]{1,0:T(8,128)(2,1)S(1)} %get-tuple-element.131.query.rest_0_, bf16[256,256]{1,0:T(8,128)(2,1)S(1)} %get-tuple-element.129.own.rest_1_, ...), custom_call_target="tpu_custom_call" | custom-call | flops 4294967296 | bytes 8388608 | tf_op jit(solution)/shard_map/attention_forward/pallas_call | solution.py:322
  113.0 6.1 collective-permute-done.9.x1
  119.2 5.7 collective-permute-done.10.x2
  126.6 14.0 %experts_forward.2 = (bf16[512,1536]{1,0:T(8,128)(2,1)S(1)}, f32[512,1536]{1,0:T(8,128)}, f32[512,1536]{1,0:T(8,128)}, bf16[512,1536]{1,0:T(8,128)(2,1)}, f32[51...) custom-call(bf16[128,1536]{1,0:T(8,128)(2,1)S(1)} %multiply_convert_, ...), custom_call_target="tpu_custom_call" | custom-call | flops 7247757312 | bytes 25165824 | tf_op jit(solution)/shard_map/experts_forward/pallas_call | solution.py:598
  149.0 13.3 %collective-permute-done.14 = bf16[128,1536]{1,0:T(8,128)(2,1)S(1)} collective-permute-done((bf16[128,1536]{1,0:T(8,128)(2,1)}, bf16[128,1536]{1,0:T(8,128)(2,1)S(1)}, u32[]{:S(2)}, u32[]{:S(2)}) %collective-permute-start.14) | collective-permute-done | bytes 393248 | tf_op jit(solution)/shard_map/ppermute | solution.py:70
  166.8 6.8 %collective-permute-done.15.peer = bf16[128,1536]{1,0:T(8,128)(2,1)S(1)} collective-permute-done((bf16[128,1536]{1,0:T(8,128)(2,1)S(1)}, bf16[128,1536]{1,0:T(8,128)(2,1)S(1)}, u32[]{:S(2)}, u32[]{:S(2)}) %collective-permute-start.15) | collective-permute-done | bytes 393248 | tf_op jit(solution)/shard_map/ppermute | solution.py:62
  184.0 6.8 %attention_forward.3 = (bf16[256,768]{1,0:T(8,128)(2,1)S(1)}, f32[256,128]{1,0:T(8,128)S(1)}, f32[128,1536]{1,0:T(8,128)S(1)}, bf16[128,1536]{1,0:T(8,128)(2,1)S(1)}) custom-call(bf16[256,768]{1,0:T(8,128)(2,1)S(1)} %get-tuple-element.142.query.rest_0_, bf16[256,256]{1,0:T(8,128)(2,1)S(1)} %get-tuple-element.143.own.rest_1_, ...), custom_call_target="tpu_custom_call" | custom-call | flops 4294967296 | bytes 8388608 | tf_op jit(solution)/shard_map/attention_forward/pallas_call | solution.py:322
  204.4 5.7 collective-permute-start.19
  217.2 11.4 %collective-permute-done.19.x2 = bf16[128,1536]{1,0:T(8,128)(2,1)S(1)} collective-permute-done((bf16[128,1536]{1,0:T(8,128)(2,1)S(1)}, bf16[128,1536]{1,0:T(8,128)(2,1)S(1)}, u32[]{:S(2)}, u32[]{:S(2)}) %collective-permute-start.19) | collective-permute-done | bytes 393248 | tf_op jit(solution)/shard_map/ppermute | solution.py:66
  229.3 7.6 %collective-permute-done.20.x3 = bf16[128,1536]{1,0:T(8,128)(2,1)S(1)} collective-permute-done((bf16[128,1536]{1,0:T(8,128)(2,1)S(1)}, bf16[128,1536]{1,0:T(8,128)(2,1)S(1)}, u32[]{:S(2)}, u32[]{:S(2)}) %collective-permute-start.20) | collective-permute-done | bytes 393248 | tf_op jit(solution)/shard_map/ppermute | solution.py:70
  243.7 10.2 %experts_forward.3 = (bf16[512,1536]{1,0:T(8,128)(2,1)S(1)}, f32[512,1536]{1,0:T(8,128)}, f32[512,1536]{1,0:T(8,128)}, bf16[512,1536]{1,0:T(8,128)(2,1)S(1)}, f32[512,128]{1,0:T(8,128)S(1)}) custom-call(bf16[128,1536]{1,0:T(8,128)(2,1)S(1)} %copy-done.12, bf16[128,1536]{1,0:T(8,128)(2,1)S(1)} %copy-done.38, bf16[128,1536]{1,0:T(8,128)(2,1)S(1)} %copy-done.40, ...), custom_call_target="tpu_custom_call" | custom-call | flops 7247757312 | bytes 25165824 | tf_op jit(solution)/shard_map/experts_forward/pallas_call | solution.py:598
  253.9 16.9 %experts_backward.2 = (bf16[512,1536]{1,0:T(8,128)(2,1)S(1)}, bf16[512,1536]{1,0:T(8,128)(2,1)}, bf16[512,1536]{1,0:T(8,128)(2,1)}, bf16[512,256]{1,0:T(8,128)(2...) custom-call(bf16[128,1536]{1,0:T(8,128)(2,1)} %get-tuple-element.370, ...), custom_call_target="tpu_custom_call" | custom-call | flops 7247757312 | bytes 25165824 | tf_op jit(solution)/shard_map/experts_backward/pallas_call | solution.py:730
  276.7 10.5 %expert_weight_grads.4 = bf16[384,9216]{1,0:T(8,128)(2,1)} custom-call(bf16[512,1536]{1,0:T(8,128)(2,1)S(1)} %get-tuple-element.159.inputs, bf16[512,1536]{1,0:T(8,128)(2,1)S(1)} %get-tuple-element.151.hidden, bf16[512,1536]{1,0:T(8,128)(2,1)} %get-tuple-element.160.gate_grad, bf16[512,1536]{1,0:T(8,128)(2,1)} %get-tuple-element.161.up_grad, ...), custom_call_target="tpu_custom_call" | custom-call | flops 4831838208 | bytes 25165824 | tf_op jit(solution)/shard_map/expert_weight_grads/pallas_call | solution.py:707
  289.8 11.5 %collective-permute-done.29.peer = bf16[128,1536]{1,0:T(8,128)(2,1)S(1)} collective-permute-done((bf16[128,1536]{1,0:T(8,128)(2,1)S(1)}, bf16[128,1536]{1,0:T(8,128)(2,1)S(1)}, u32[]{:S(2)}, u32[]{:S(2)}) %collective-permute-start.29) | collective-permute-done | bytes 393248 | tf_op jit(solution)/shard_map/ppermute | solution.py:62
  301.3 6.2 %attention_backward.2 = (bf16[256,1536]{1,0:T(8,128)(2,1)S(1)}, bf16[256,768]{1,0:T(8,128)(2,1)S(1)}, f32[256,256]{1,0:T(8,128)S(1)}, bf16[256,256]{1,0:T(8,128)(2,1)S(1)}) custom-call(f32[256,128]{1,0:T(8,128)S(1)} %pad_maximum_fusion.12.cosine, f32[256,128]{1,0:T(8,128)S(1)} %pad_maximum_fusion.13.sine, f32[256,512]{1,0:T(8,128)S(1)} %and_convert_fusion.seen, ...), custom_call_target="tpu_custom_call" | custom-call | flops 4294967296 | bytes 8388608 | tf_op jit(solution)/shard_map/attention_backward/pallas_call | solution.py:322
  320.0 13.6 %expert_weight_grads.5 = f32[384,9216]{1,0:T(8,128)} custom-call(bf16[512,1536]{1,0:T(8,128)(2,1)S(1)} %get-tuple-element.159.inputs, bf16[512,1536]{1,0:T(8,128)(2,1)S(1)} %get-tuple-element.151.hidden, bf16[512,1536]{1,0:T(8,128)(2,1)} %get-tuple-element.160.gate_grad, bf16[512,1536]{1,0:T(8,128)(2,1)} %get-tuple-element.161.up_grad, ...), custom_call_target="tpu_custom_call" | custom-call | flops 4831838208 | bytes 25165824 | tf_op jit(solution)/shard_map/expert_weight_grads/pallas_call | solution.py:707
  344.2 7.0 %collective-permute-done.34.y1 = bf16[128,1536]{1,0:T(8,128)(2,1)S(1)} collective-permute-done((bf16[128,1536]{1,0:T(8,128)(2,1)S(1)}, bf16[128,1536]{1,0:T(8,128)(2,1)S(1)}, u32[]{:S(2)}, u32[]{:S(2)}) %collective-permute-start.34) | collective-permute-done | bytes 393248 | tf_op jit(solution)/shard_map/ppermute | solution.py:62
  351.2 8.3 %collective-permute-done.35.y2 = bf16[128,1536]{1,0:T(8,128)(2,1)S(1)} collective-permute-done((bf16[128,1536]{1,0:T(8,128)(2,1)S(1)}, bf16[128,1536]{1,0:T(8,128)(2,1)S(1)}, u32[]{:S(2)}, u32[]{:S(2)}) %collective-permute-start.35) | collective-permute-done | bytes 393248 | tf_op jit(solution)/shard_map/ppermute | solution.py:66
  362.4 15.6 %experts_backward.3 = (bf16[512,1536]{1,0:T(8,128)(2,1)S(1)}, bf16[512,1536]{1,0:T(8,128)(2,1)}, bf16[512,1536]{1,0:T(8,128)(2,1)}, bf16[512,256]{1,0:T(8,128)(2...) custom-call(bf16[128,1536]{1,0:T(8,128)(2,1)S(1)} %get-tuple-element, ...), custom_call_target="tpu_custom_call" | custom-call | flops 7247757312 | bytes 25165824 | tf_op jit(solution)/shard_map/experts_backward/pallas_call | solution.py:730
  383.9 10.6 %expert_weight_grads.6 = bf16[384,9216]{1,0:T(8,128)(2,1)} custom-call(bf16[512,1536]{1,0:T(8,128)(2,1)S(1)} %copy-done.2, bf16[512,1536]{1,0:T(8,128)(2,1)S(1)} %copy-done.20, bf16[512,1536]{1,0:T(8,128)(2,1)} %get-tuple-element.187.gate_grad, bf16[512,1536]{1,0:T(8,128)(2,1)} %get-tuple-element.188.up_grad, bf16[512,1536]{1,0:T(8,128)(2,1)} %copy-done.22, ...), custom_call_target="tpu_custom_call" | custom-call | flops 4831838208 | bytes 25165824 | tf_op jit(solution)/shard_map/expert_weight_grads/pallas_call | solution.py:707
  401.3 6.2 %collective-permute-done.31 = bf16[128,768]{1,0:T(8,128)(2,1)S(1)} collective-permute-done((bf16[128,768]{1,0:T(8,128)(2,1)}, bf16[128,768]{1,0:T(8,128)(2,1)S(1)}, u32[]{:S(2)}, u32[]{:S(2)}) %collective-permute-start.31) | collective-permute-done | bytes 196640 | tf_op jit(solution)/shard_map/ppermute | solution.py:62
  415.1 13.6 %expert_weight_grads.7 = f32[384,9216]{1,0:T(8,128)} custom-call(bf16[512,1536]{1,0:T(8,128)(2,1)S(1)} %copy-done.3, bf16[512,1536]{1,0:T(8,128)(2,1)S(1)} %copy-done.21, bf16[512,1536]{1,0:T(8,128)(2,1)} %get-tuple-element.187.gate_grad, bf16[512,1536]{1,0:T(8,128)(2,1)} %get-tuple-element.188.up_grad, bf16[512,1536]{1,0:T(8,128)(2,1)} %copy-done.22, ...), custom_call_target="tpu_custom_call" | custom-call | flops 4831838208 | bytes 25165824 | tf_op jit(solution)/shard_map/expert_weight_grads/pallas_call | solution.py:707
  432.4 6.3 %attention_backward.3 = (bf16[256,1536]{1,0:T(8,128)(2,1)S(1)}, bf16[256,768]{1,0:T(8,128)(2,1)S(1)}, f32[256,256]{1,0:T(8,128)S(1)}, bf16[256,256]{1,0:T(8,128)(2,1)S(1)}) custom-call(f32[256,128]{1,0:T(8,128)S(1)} %pad_maximum_fusion.12.cosine, f32[256,128]{1,0:T(8,128)S(1)} %pad_maximum_fusion.13.sine, f32[256,512]{1,0:T(8,128)S(1)} %and_convert_fusion.seen, ...), custom_call_target="tpu_custom_call" | custom-call | flops 4294967296 | bytes 8388608 | tf_op jit(solution)/shard_map/attention_backward/pallas_call | solution.py:322
  452.5 6.2 %attention_weight_grads.2 = (bf16[384,3584]{1,0:T(8,128)(2,1)}, bf16[384,3584]{1,0:T(8,128)(2,1)}) custom-call(bf16[256,1536]{1,0:T(8,128)(2,1)S(1)} %copy-done.13, bf16[256,768]{1,0:T(8,128)(2,1)S(1)} %copy-done.78, bf16[256,1024]{1,0:T(8,128)(2,1)S(1)} %get-tuple-element.207.qkv_grad, bf16[256,1536]{1,0:T(8,128)(2,1)S(1)} %get-tuple-element.208.out_grad, ...), custom_call_target="tpu_custom_call" | custom-call | flops 1811939328 | bytes 10485760 | tf_op jit(solution)/shard_map/attention_weight_grads/pallas_call | solution.py:472
  466.7 6.2 %attention_weight_grads.3 = (bf16[384,3584]{1,0:T(8,128)(2,1)}, bf16[384,3584]{1,0:T(8,128)(2,1)}) custom-call(bf16[256,1536]{1,0:T(8,128)(2,1)S(1)} %copy-done.30, bf16[256,768]{1,0:T(8,128)(2,1)S(1)} %copy-done.71, bf16[256,1024]{1,0:T(8,128)(2,1)S(1)} %copy-done.68, bf16[256,1536]{1,0:T(8,128)(2,1)S(1)} %copy-done.66, bf16[768,768]{1,0:T(8,128)(2,1)S(1)} %fusion.5.order), custom_call_target="tpu_custom_call" | custom-call | flops 1811939328 | bytes 10485760 | tf_op jit(solution)/shard_map/attention_weight_grads/pallas_call | solution.py:472
  481.2 5.6 collective-permute-done.57
  510.3 10.1 %collective-permute-done.49 = bf16[96,3584]{1,0:T(8,128)(2,1)S(1)} collective-permute-done((bf16[96,3584]{1,0:T(8,128)(2,1)}, bf16[96,3584]{1,0:T(8,128)(2,1)S(1)}, u32[]{:S(2)}, u32[]{:S(2)}) %collective-permute-start.49) | collective-permute-done | bytes 688160 | tf_op jit(solution)/shard_map/ppermute | solution.py:74
  521.6 15.7 %collective-permute-done.48 = bf16[96,3584]{1,0:T(8,128)(2,1)} collective-permute-done((bf16[96,3584]{1,0:T(8,128)(2,1)}, bf16[96,3584]{1,0:T(8,128)(2,1)}, u32[]{:S(2)}, u32[]{:S(2)}) %collective-permute-start.48) | collective-permute-done | bytes 688160 | tf_op jit(solution)/shard_map/ppermute | solution.py:74
  543.7 11.4 %collective-permute-done.50 = bf16[96,3584]{1,0:T(8,128)(2,1)S(1)} collective-permute-done((bf16[96,3584]{1,0:T(8,128)(2,1)S(1)}, bf16[96,3584]{1,0:T(8,128)(2,1)S(1)}, u32[]{:S(2)}, u32[]{:S(2)}) %collective-permute-start.50) | collective-permute-done | bytes 688160 | tf_op jit(solution)/shard_map/ppermute | solution.py:74
  595.7 6.3 %collective-permute-done.73 = bf16[24,8192]{1,0:T(8,128)(2,1)S(1)} collective-permute-done((bf16[24,8192]{1,0:T(8,128)(2,1)S(1)}, bf16[24,8192]{1,0:T(8,128)(2,1)S(1)}, u32[]{:S(2)}, u32[]{:S(2)}) %collective-permute-start.73) | collective-permute-done | bytes 393248 | tf_op jit(solution)/shard_map/ppermute | solution.py:66
  (677 shorter events, 289.5 us)
Async XLA Ops:
  7.2 118.4 %all-gather.3.cloned.1.call-start = ((), (), s32[]{:S(2)}) async-start(), calls=%async_computation.2 | async-start | bytes 20275200 | tf_op jit(solution)/shard_map/all_gather | solution.py:231
  19.3 20.8 %collective-permute-start.2 = (bf16[256,768]{1,0:T(8,128)(2,1)S(1)}, bf16[256,768]{1,0:T(8,128)(2,1)}, u32[]{:S(2)}, u32[]{:S(2)}) collective-permute-start(bf16[256,768]{1,0:T(8,128)(2,1)S(1)} %fusion.8.own), channel_id=1, source_target_pairs={{0,2},{2,0},{1,3},{3,1},{4,6},{6,4},{5,7},{7,5},{8,10},{10,8},{9,1... | collective-permute-start | bytes 1179656 | tf_op jit(solution)/shard_map/ppermute | solution.py:62
  40.1 197.6 %all-gather.5.cloned.1.call-start = ((), (), s32[]{:S(2)}) async-start(), calls=%async_computation.3 | async-start | bytes 20275200 | tf_op jit(solution)/shard_map/all_gather | solution.py:231
  41.9 34.5 %collective-permute-start.5 = (bf16[128,768]{1,0:T(8,128)(2,1)}, bf16[128,768]{1,0:T(8,128)(2,1)S(1)}, u32[]{:S(2)}, u32[]{:S(2)}) collective-permute-start(bf16[128,768]{1,0:T(8,128)(2,1)} %get-tuple-element.378), channel_id=1, source_target_pairs={{0,1},{1,0},{2,3},{3,2},{4,5},{5,4},{6,7},{7,6},{8,9},{9,8},{10,11... | collective-permute-start | bytes 589832 | tf_op jit(solution)/shard_map/ppermute | solution.py:66
  44.8 19.2 %collective-permute-start.6 = (bf16[384,768]{1,0:T(8,128)(2,1)S(1)}, bf16[384,768]{1,0:T(8,128)(2,1)}, u32[]{:S(2)}, u32[]{:S(2)}) collective-permute-start(bf16[384,768]{1,0:T(8,128)(2,1)S(1)} %get-tuple-element.134), channel_id=1, source_target_pairs={{0,1},{1,0},{2,3},{3,2},{4,5},{5,4},{6,7},{7,6},{8,9},{9,8},{10,11... | collective-permute-start | bytes 1769480 | tf_op jit(solution)/shard_map/ppermute | solution.py:66
  54.1 19.1 %collective-permute-start.3 = (bf16[256,1024]{1,0:T(8,128)(2,1)}, bf16[256,1024]{1,0:T(8,128)(2,1)S(1)}, u32[]{:S(2)}, u32[]{:S(2)}) collective-permute-start(bf16[256,1024]{1,0:T(8,128)(2,1)} %copy-done.69), channel_id=1, source_target_pairs={{0,1},{1,0},{2,3},{3,2},{4,5},{5,4},{6,7},{7,6},{8,9},{9,8},{10,11... | collective-permute-start | bytes 1572872 | tf_op jit(solution)/shard_map/ppermute | solution.py:66
  90.6 21.6 %collective-permute-start.21 = (bf16[48,5248]{1,0:T(8,128)(2,1)S(1)}, bf16[48,5248]{1,0:T(8,128)(2,1)S(1)}, u32[]{:S(2)}, u32[]{:S(2)}) collective-permute-start(bf16[48,5248]{1,0:T(8,128)(2,1)S(1)} %get-tuple-element.148), channel_id=1, source_target_pairs={{0,1},{1,0},{2,3},{3,2},{4,5},{5,4},{6,7},{7,6},{8,9},{9,8},{10,11... | collective-permute-start | bytes 1511432 | tf_op jit(solution)/shard_map/ppermute | solution.py:66
  101.0 18.2 %collective-permute-start.9 = (bf16[128,1536]{1,0:T(8,128)(2,1)S(1)}, bf16[128,1536]{1,0:T(8,128)(2,1)S(1)}, u32[]{:S(2)}, u32[]{:S(2)}) collective-permute-start(bf16[128,1536]{1,0:T(8,128)(2,1)S(1)} %multiply_convert_fusion.2.x0), channel_id=1, source_target_pairs={{0,2},{2,0},{1,3},{3,1},{4,6},{6,4},{5,7},{7,5},{8,10},{10,8},{9,1... | collective-permute-start | bytes 1179656 | tf_op jit(solution)/shard_map/ppermute | solution.py:62
  101.9 23.0 %collective-permute-start.10 = (bf16[128,1536]{1,0:T(8,128)(2,1)}, bf16[128,1536]{1,0:T(8,128)(2,1)S(1)}, u32[]{:S(2)}, u32[]{:S(2)}) collective-permute-start(bf16[128,1536]{1,0:T(8,128)(2,1)} %pad_maximum_fusion.2), channel_id=1, source_target_pairs={{0,1},{1,0},{2,3},{3,2},{4,5},{5,4},{6,7},{7,6},{8,9},{9,8},{10,11... | collective-permute-start | bytes 1179656 | tf_op jit(solution)/shard_map/ppermute | solution.py:66
  105.3 19.6 %collective-permute-start.11 = (bf16[128,1536]{1,0:T(8,128)(2,1)}, bf16[128,1536]{1,0:T(8,128)(2,1)S(1)}, u32[]{:S(2)}, u32[]{:S(2)}) collective-permute-start(bf16[128,1536]{1,0:T(8,128)(2,1)} %pad_maximum_fusion.2), channel_id=1, source_target_pairs={{0,3},{1,2},{2,1},{3,0},{4,7},{5,6},{6,5},{7,4},{8,11},{9,10},{10,... | collective-permute-start | bytes 1179656 | tf_op jit(solution)/shard_map/ppermute | solution.py:70
  144.7 294.0 %reduce-scatter.7.cloned.1.call-start = ((), (), s32[]{:S(2)}) async-start(), calls=%async_computation.4 | async-start | bytes 15040512
  204.4 24.2 %collective-permute-start.19 = (bf16[128,1536]{1,0:T(8,128)(2,1)S(1)}, bf16[128,1536]{1,0:T(8,128)(2,1)S(1)}, u32[]{:S(2)}, u32[]{:S(2)}) collective-permute-start(bf16[128,1536]{1,0:T(8,128)(2,1)S(1)} %pad_maximum_fusion.3), channel_id=1, source_target_pairs={{0,1},{1,0},{2,3},{3,2},{4,5},{5,4},{6,7},{7,6},{8,9},{9,8},{10,11... | collective-permute-start | bytes 1179656 | tf_op jit(solution)/shard_map/ppermute | solution.py:66
  210.1 26.9 %collective-permute-start.20 = (bf16[128,1536]{1,0:T(8,128)(2,1)S(1)}, bf16[128,1536]{1,0:T(8,128)(2,1)S(1)}, u32[]{:S(2)}, u32[]{:S(2)}) collective-permute-start(bf16[128,1536]{1,0:T(8,128)(2,1)S(1)} %pad_maximum_fusion.3), channel_id=1, source_target_pairs={{0,3},{1,2},{2,1},{3,0},{4,7},{5,6},{6,5},{7,4},{8,11},{9,10},{10,... | collective-permute-start | bytes 1179656 | tf_op jit(solution)/shard_map/ppermute | solution.py:70
  212.6 41.3 %collective-permute-start.24 = (bf16[128,1536]{1,0:T(8,128)(2,1)}, bf16[128,1536]{1,0:T(8,128)(2,1)}, u32[]{:S(2)}, u32[]{:S(2)}) collective-permute-start(bf16[128,1536]{1,0:T(8,128)(2,1)} %get-tuple-element.369), channel_id=1, source_target_pairs={{0,1},{1,0},{2,3},{3,2},{4,5},{5,4},{6,7},{7,6},{8,9},{9,8},{10,11... | collective-permute-start | bytes 1179656 | tf_op jit(solution)/shard_map/ppermute | solution.py:66
  213.7 40.2 %collective-permute-start.25 = (bf16[128,1536]{1,0:T(8,128)(2,1)}, bf16[128,1536]{1,0:T(8,128)(2,1)}, u32[]{:S(2)}, u32[]{:S(2)}) collective-permute-start(bf16[128,1536]{1,0:T(8,128)(2,1)} %get-tuple-element.369), channel_id=1, source_target_pairs={{0,3},{1,2},{2,1},{3,0},{4,7},{5,6},{6,5},{7,4},{8,11},{9,10},{10,... | collective-permute-start | bytes 1179656 | tf_op jit(solution)/shard_map/ppermute | solution.py:70
  216.6 37.2 %collective-permute-start.23 = (bf16[128,1536]{1,0:T(8,128)(2,1)}, bf16[128,1536]{1,0:T(8,128)(2,1)}, u32[]{:S(2)}, u32[]{:S(2)}) collective-permute-start(bf16[128,1536]{1,0:T(8,128)(2,1)} %get-tuple-element.370.y0), channel_id=1, source_target_pairs={{0,2},{2,0},{1,3},{3,1},{4,6},{6,4},{5,7},{7,5},{8,10},{10,8},{9,1... | collective-permute-start | bytes 1179656 | tf_op jit(solution)/shard_map/ppermute | solution.py:62
  287.2 32.8 %collective-permute-start.32 = (bf16[384,9216]{1,0:T(8,128)(2,1)}, bf16[384,9216]{1,0:T(8,128)(2,1)}, u32[]{:S(2)}, u32[]{:S(2)}) collective-permute-start(bf16[384,9216]{1,0:T(8,128)(2,1)} %expert_weight_grads.4), channel_id=1, source_target_pairs={{0,4},{4,0},{8,12},{12,8},{16,20},{20,16},{24,28},{28,24},{32,36},... | collective-permute-start | bytes 21233672 | tf_op jit(solution)/shard_map/ppermute | solution.py:74
  333.7 257.6 %reduce-scatter.9.cloned.1.call-start = ((), (), s32[]{:S(2)}) async-start(), calls=%async_computation.5 | async-start | bytes 15040512
  340.8 18.7 %collective-permute-start.35 = (bf16[128,1536]{1,0:T(8,128)(2,1)S(1)}, bf16[128,1536]{1,0:T(8,128)(2,1)S(1)}, u32[]{:S(2)}, u32[]{:S(2)}) collective-permute-start(bf16[128,1536]{1,0:T(8,128)(2,1)S(1)} %pad_maximum_fusion.6), channel_id=1, source_target_pairs={{0,1},{1,0},{2,3},{3,2},{4,5},{5,4},{6,7},{7,6},{8,9},{9,8},{10,11... | collective-permute-start | bytes 1179656 | tf_op jit(solution)/shard_map/ppermute | solution.py:66
  343.6 18.9 %collective-permute-start.36 = (bf16[128,1536]{1,0:T(8,128)(2,1)S(1)}, bf16[128,1536]{1,0:T(8,128)(2,1)S(1)}, u32[]{:S(2)}, u32[]{:S(2)}) collective-permute-start(bf16[128,1536]{1,0:T(8,128)(2,1)S(1)} %pad_maximum_fusion.6), channel_id=1, source_target_pairs={{0,3},{1,2},{2,1},{3,0},{4,7},{5,6},{6,5},{7,4},{8,11},{9,10},{10,... | collective-permute-start | bytes 1179656 | tf_op jit(solution)/shard_map/ppermute | solution.py:70
  458.8 28.9 %collective-permute-start.46 = (bf16[384,3584]{1,0:T(8,128)(2,1)}, bf16[384,3584]{1,0:T(8,128)(2,1)}, u32[]{:S(2)}, u32[]{:S(2)}) collective-permute-start(bf16[384,3584]{1,0:T(8,128)(2,1)} %get-tuple-element.209), channel_id=1, source_target_pairs={{0,4},{4,0},{8,12},{12,8},{16,20},{20,16},{24,28},{28,24},{32,36},... | collective-permute-start | bytes 8257544 | tf_op jit(solution)/shard_map/ppermute | solution.py:74
  472.9 24.0 %collective-permute-start.43 = (bf16[384,3584]{1,0:T(8,128)(2,1)}, bf16[384,3584]{1,0:T(8,128)(2,1)S(1)}, u32[]{:S(2)}, u32[]{:S(2)}) collective-permute-start(bf16[384,3584]{1,0:T(8,128)(2,1)} %get-tuple-element.211), channel_id=1, source_target_pairs={{0,4},{4,0},{8,12},{12,8},{16,20},{20,16},{24,28},{28,24},{32,36},... | collective-permute-start | bytes 8257544 | tf_op jit(solution)/shard_map/ppermute | solution.py:74
  481.1 76.7 %collective-permute-start.60 = (f32[20,768]{1,0:T(8,128)S(1)}, f32[20,768]{1,0:T(8,128)S(1)}, u32[]{:S(2)}, u32[]{:S(2)}) collective-permute-start(f32[20,768]{1,0:T(8,128)S(1)} %add_add_fusion.3), channel_id=1, source_target_pairs={{0,4},{4,0},{8,12},{12,8},{16,20},{20,16},{24,28},{28,24},{32,36},... | collective-permute-start | bytes 184328 | tf_op jit(solution)/shard_map/ppermute | solution.py:74
  492.7 27.7 %collective-permute-start.49 = (bf16[96,3584]{1,0:T(8,128)(2,1)}, bf16[96,3584]{1,0:T(8,128)(2,1)S(1)}, u32[]{:S(2)}, u32[]{:S(2)}) collective-permute-start(bf16[96,3584]{1,0:T(8,128)(2,1)} %get-tuple-element.301), channel_id=1, source_target_pairs={{0,96},{4,100},{8,104},{12,108},{16,112},{20,116},{24,120},{28,124... | collective-permute-start | bytes 2064392 | tf_op jit(solution)/shard_map/ppermute | solution.py:74
  493.5 43.8 %collective-permute-start.48 = (bf16[96,3584]{1,0:T(8,128)(2,1)}, bf16[96,3584]{1,0:T(8,128)(2,1)}, u32[]{:S(2)}, u32[]{:S(2)}) collective-permute-start(bf16[96,3584]{1,0:T(8,128)(2,1)} %get-tuple-element.302), channel_id=1, source_target_pairs={{0,64},{4,68},{8,72},{12,76},{16,80},{20,84},{24,88},{28,92},{32,9... | collective-permute-start | bytes 2064392 | tf_op jit(solution)/shard_map/ppermute | solution.py:74
  494.7 43.0 %collective-permute-start.47 = (bf16[96,3584]{1,0:T(8,128)(2,1)}, bf16[96,3584]{1,0:T(8,128)(2,1)}, u32[]{:S(2)}, u32[]{:S(2)}) collective-permute-start(bf16[96,3584]{1,0:T(8,128)(2,1)} %get-tuple-element.300), channel_id=1, source_target_pairs={{0,32},{4,36},{8,40},{12,44},{16,48},{20,52},{24,56},{28,60},{32,6... | collective-permute-start | bytes 2064392 | tf_op jit(solution)/shard_map/ppermute | solution.py:74
  507.9 34.4 %collective-permute-start.52 = (bf16[96,3584]{1,0:T(8,128)(2,1)S(1)}, bf16[96,3584]{1,0:T(8,128)(2,1)S(1)}, u32[]{:S(2)}, u32[]{:S(2)}) collective-permute-start(bf16[96,3584]{1,0:T(8,128)(2,1)S(1)} %get-tuple-element.298), channel_id=1, source_target_pairs={{0,24},{4,28},{8,0},{12,4},{16,8},{20,12},{24,16},{28,20},{32,56},... | collective-permute-start | bytes 2064392 | tf_op jit(solution)/shard_map/ppermute | solution.py:74
  520.4 22.7 %collective-permute-start.51 = (bf16[96,3584]{1,0:T(8,128)(2,1)S(1)}, bf16[96,3584]{1,0:T(8,128)(2,1)S(1)}, u32[]{:S(2)}, u32[]{:S(2)}) collective-permute-start(bf16[96,3584]{1,0:T(8,128)(2,1)S(1)} %get-tuple-element.299), channel_id=1, source_target_pairs={{0,16},{4,20},{8,24},{12,28},{16,0},{20,4},{24,8},{28,12},{32,48},... | collective-permute-start | bytes 2064392 | tf_op jit(solution)/shard_map/ppermute | solution.py:74
  537.6 22.6 %collective-permute-start.54 = (bf16[128,1536]{1,0:T(8,128)(2,1)S(1)}, bf16[128,1536]{1,0:T(8,128)(2,1)S(1)}, u32[]{:S(2)}, u32[]{:S(2)}) collective-permute-start(bf16[128,1536]{1,0:T(8,128)(2,1)S(1)} %get-tuple-element.217), channel_id=1, source_target_pairs={{0,3},{1,2},{2,1},{3,0},{4,7},{5,6},{6,5},{7,4},{8,11},{9,10},{10,... | collective-permute-start | bytes 1179656 | tf_op jit(solution)/shard_map/ppermute | solution.py:70
  542.2 20.2 %collective-permute-start.45 = (bf16[128,1536]{1,0:T(8,128)(2,1)S(1)}, bf16[128,1536]{1,0:T(8,128)(2,1)S(1)}, u32[]{:S(2)}, u32[]{:S(2)}) collective-permute-start(bf16[128,1536]{1,0:T(8,128)(2,1)S(1)} %get-tuple-element.214), channel_id=1, source_target_pairs={{0,1},{1,0},{2,3},{3,2},{4,5},{5,4},{6,7},{7,6},{8,9},{9,8},{10,11... | collective-permute-start | bytes 1179656 | tf_op jit(solution)/shard_map/ppermute | solution.py:66
  543.1 19.3 %collective-permute-start.44 = (bf16[128,1536]{1,0:T(8,128)(2,1)S(1)}, bf16[128,1536]{1,0:T(8,128)(2,1)S(1)}, u32[]{:S(2)}, u32[]{:S(2)}) collective-permute-start(bf16[128,1536]{1,0:T(8,128)(2,1)S(1)} %get-tuple-element.213), channel_id=1, source_target_pairs={{0,2},{2,0},{1,3},{3,1},{4,6},{6,4},{5,7},{7,5},{8,10},{10,8},{9,1... | collective-permute-start | bytes 1179656 | tf_op jit(solution)/shard_map/ppermute | solution.py:62
  562.7 27.7 %collective-permute-start.55 = (bf16[128,768]{1,0:T(8,128)(2,1)S(1)}, bf16[128,768]{1,0:T(8,128)(2,1)S(1)}, u32[]{:S(2)}, u32[]{:S(2)}) collective-permute-start(bf16[128,768]{1,0:T(8,128)(2,1)S(1)} %get-tuple-element.366), channel_id=1, source_target_pairs={{0,1},{1,0},{2,3},{3,2},{4,5},{5,4},{6,7},{7,6},{8,9},{9,8},{10,11... | collective-permute-start | bytes 589832 | tf_op jit(solution)/shard_map/ppermute | solution.py:66
  (196 other events, 1603.8 us)
Sparse Core Ops, SparseCore 0:
  40.2 81.5 all-gather.2
  144.9 79.9 all-gather.4
  333.8 98.0 reduce-scatter.6
  439.5 138.5 reduce-scatter.8

commit v6 on v5

--- a/solution.py
+++ b/solution.py
@@ -520,9 +520,18 @@
         target[:, HALF:] = block[:, :HALF]
 
 
-def join_blocks(blocks, target):
-    for k, block in enumerate(blocks):
-        target[k * QUARTER : (k + 1) * QUARTER, :] = block[...]
+def fetch(pairs, sems):
+    copies = [pltpu.make_async_copy(x, y, sems.at[k]) for k, (x, y) in enumerate(pairs)]
+    for copy in copies:
+        copy.start()
+    for copy in copies:
+        copy.wait()
+
+
+def row_blocks(blocks, target):
+    return [
+        (block, target.at[pl.ds(k * QUARTER, QUARTER), :]) for k, block in enumerate(blocks)
+    ]
 
 
 def share_of(share, step, k):
@@ -531,14 +540,16 @@
     return (mine, jnp.sum(jnp.where(mine, share, 0.0), axis=1, keepdims=True))
 
 
-def forward_kernel(x0, x1, x2, x3, chosen, router, wg, wu, *rest):
+def forward_kernel(x0, x1, x2, x3, mask_ref, router_ref, wg, wu, *rest):
+    *rest, chosen, router, sems = rest
     *down, inputs, gate, up, hidden, share = rest[: 6 if len(rest) > 5 else 5]
     sends = rest[6:]
     step = pl.program_id(0)
 
     @pl.when(step == 0)
     def _():
-        join_blocks((x0, x1, x2, x3), inputs)
+        blocks = row_blocks((x0, x1, x2, x3), inputs)
+        fetch(blocks + [(mask_ref, chosen), (router_ref, router)], sems)
         logits = dot_across(inputs[...], router[...])
         picked = chosen[...] > 0.0
         top = jnp.max(jnp.where(picked, logits, MASKED_SCORE), axis=1, keepdims=True)
@@ -572,6 +583,9 @@
         send_blocks(total_ref[...], *sends)
 
 
+FAR = pl.BlockSpec(memory_space=pltpu.HBM)
+
+
 def weight_specs():
     return [
         pl.BlockSpec((D, WIDE), lambda j: (0, j)),
@@ -598,7 +612,7 @@
     out = pl.pallas_call(
         forward_kernel,
         grid=(STEPS,),
-        in_specs=[whole(BLOCK)] * 4 + [whole(LANES), whole((128, D))] + weight_specs()[:count],
+        in_specs=[FAR] * 6 + weight_specs()[:count],
         out_specs=[whole(ALL), SLAB, SLAB, SLAB, whole(LANES)] + [whole(BLOCK)] * len(sends),
         out_shape=[
             jax.ShapeDtypeStruct(ALL, BF16),
@@ -608,7 +622,8 @@
             jax.ShapeDtypeStruct(LANES, F32),
         ]
         + sends,
-        scratch_shapes=[] if last else [pltpu.VMEM(ALL, F32)],
+        scratch_shapes=([] if last else [pltpu.VMEM(ALL, F32)])
+        + [pltpu.VMEM(LANES, F32), pltpu.VMEM((128, D), BF16), pltpu.SemaphoreType.DMA((6,))],
         compiler_params=pltpu.CompilerParams(vmem_limit_bytes=VMEM_LIMIT),
         cost_estimate=COST,
         name="experts_forward",
@@ -632,12 +647,12 @@
 
 
 def backward_kernel(y0, y1, y2, y3, gate, up, share, router, wg, wu, wd, *rest):
-    grads, gate_grad, up_grad, logits_grad, own, row, col, both, total_ref, share_grad = rest
+    grads, gate_grad, up_grad, logits_grad, own, row, col, both, total_ref, share_grad, sems = rest
     step = pl.program_id(0)
 
     @pl.when(step == 0)
     def _():
-        join_blocks((y0, y1, y2, y3), grads)
+        fetch(row_blocks((y0, y1, y2, y3), grads), sems)
         share_grad[...] = jnp.zeros_like(share_grad)
 
     hidden_grad = dot_across(grads[...], wd[...])
@@ -730,14 +745,18 @@
     out = pl.pallas_call(
         backward_kernel,
         grid=(STEPS,),
-        in_specs=[whole(BLOCK)] * 4
+        in_specs=[FAR] * 4
         + [SLAB, SLAB, whole(LANES), whole((128, D))]
         + weight_specs(),
         out_specs=[whole(ALL), SLAB, SLAB, whole((TOK_DP, 256))] + [whole(BLOCK)] * 4,
         out_shape=[jax.ShapeDtypeStruct(ALL, BF16)] * 3
         + [jax.ShapeDtypeStruct((TOK_DP, 256), BF16), jax.ShapeDtypeStruct(BLOCK, F32)]
         + [jax.ShapeDtypeStruct(BLOCK, BF16)] * 3,
-        scratch_shapes=[pltpu.VMEM(ALL, F32), pltpu.VMEM(LANES, F32)],
+        scratch_shapes=[
+            pltpu.VMEM(ALL, F32),
+            pltpu.VMEM(LANES, F32),
+            pltpu.SemaphoreType.DMA((4,)),
+        ],
         compiler_params=pltpu.CompilerParams(vmem_limit_bytes=VMEM_LIMIT),
         cost_estimate=COST,
         name="experts_backward",

time: 625 us -> 630 us (level)
  no operation moved by 1% of the time
where the time goes in v6:
time: 630 us; the launch traced here: 619 us
  waiting for transfers between devices  214 us (34%)
  Pallas kernels  171 us (27%)
  starting transfers between devices  110 us (17%)
  local copies, waits for them, and re-layouts  58.4 us (9%)
  other arithmetic  42.7 us (7%)
  between operations  20.3 us (3%)
    ppermute x24, waiting for transfers between devices, over_col(): return lax.ppermute(x, 'col', SWAP)  87.4 us
    ppermute x24, starting transfers between devices, over_col(): return lax.ppermute(x, 'col', SWAP)  61.6 us
    ppermute x18, waiting for transfers between devices, over_row(): return lax.ppermute(x, 'row', SWAP)  52.2 us
    pallas_call x4, Pallas kernels, weight_grads(): pl.pallas_call(grads_kernel, grid=(6,), in_specs=[left(lambda j: jnp.mini...  48.4 us
    ppermute x24, waiting for transfers between devices, over_dp(): return lax.ppermute(x, 'dp', [(i, target(i)) for i in range(N_DP)])  47.5 us
    pallas_call x12, Pallas kernels, local_call(): pl.pallas_call(kernel, grid=(1,), in_specs=[specs.get(k) or whole(x.shape...  44.5 us
    unnamed x354, local copies, waits for them, and re-layouts  40.9 us
    pallas_call x2, Pallas kernels, expert_backward(): pl.pallas_call(backward_kernel, grid=(STEPS,), in_specs=[FAR] * 4 + [SLAB...  35.4 us
  transfers between devices with their start and end apart: 78, of which 39 were waited for; matrix products, arithmetic and copies ran while one was open for 9% of the time, Pallas kernels for 22%

profile of v6, /device:TPU:6, one launch (start us, length us, event | category | flops | bytes accessed | tf_op | source)
XLA Modules:
  0.0 619.4 jit_solution(11714276324768099418)
XLA Ops:
  20.9 13.7 %collective-permute-done.1.other = bf16[48,5248]{1,0:T(8,128)(2,1)S(1)} collective-permute-done((bf16[48,5248]{1,0:T(8,128)(2,1)S(1)}, bf16[48,5248]{1,0:T(8,128)(2,1)S(1)}, u32[]{:S(2)}, u32[]{:S(2)}) %collective-permute-start.1) | collective-permute-done | bytes 503840 | tf_op jit(solution)/shard_map/ppermute | solution.py:66
  64.1 9.1 %collective-permute-done.3.far = bf16[256,1024]{1,0:T(8,128)(2,1)S(1)} collective-permute-done((bf16[256,1024]{1,0:T(8,128)(2,1)}, bf16[256,1024]{1,0:T(8,128)(2,1)S(1)}, u32[]{:S(2)}, u32[]{:S(2)}) %collective-permute-start.3) | collective-permute-done | bytes 524320 | tf_op jit(solution)/shard_map/ppermute | solution.py:66
  81.4 6.3 %attention_forward.2 = (bf16[256,768]{1,0:T(8,128)(2,1)S(1)}, f32[256,128]{1,0:T(8,128)S(1)}, f32[128,1536]{1,0:T(8,128)S(1)}, bf16[128,1536]{1,0:T(8,128)(2,1)S(1)}) custom-call(bf16[256,768]{1,0:T(8,128)(2,1)S(1)} %get-tuple-element.131.query.rest_0_, bf16[256,256]{1,0:T(8,128)(2,1)S(1)} %get-tuple-element.129.own.rest_1_, ...), custom_call_target="tpu_custom_call" | custom-call | flops 4294967296 | bytes 8388608 | tf_op jit(solution)/shard_map/attention_forward/pallas_call | solution.py:322
  113.0 6.1 collective-permute-done.9.x1
  119.2 5.7 collective-permute-done.10.x2
  126.6 15.2 %experts_forward.2 = (bf16[512,1536]{1,0:T(8,128)(2,1)S(1)}, f32[512,1536]{1,0:T(8,128)}, f32[512,1536]{1,0:T(8,128)}, bf16[512,1536]{1,0:T(8,128)(2,1)}, f32[51...) custom-call(bf16[128,1536]{1,0:T(8,128)(2,1)S(1)} %multiply_convert_, ...), custom_call_target="tpu_custom_call" | custom-call | flops 7247757312 | bytes 25165824 | tf_op jit(solution)/shard_map/experts_forward/pallas_call | solution.py:612
  150.1 13.3 %collective-permute-done.14 = bf16[128,1536]{1,0:T(8,128)(2,1)S(1)} collective-permute-done((bf16[128,1536]{1,0:T(8,128)(2,1)}, bf16[128,1536]{1,0:T(8,128)(2,1)S(1)}, u32[]{:S(2)}, u32[]{:S(2)}) %collective-permute-start.14) | collective-permute-done | bytes 393248 | tf_op jit(solution)/shard_map/ppermute | solution.py:70
  168.0 6.8 %collective-permute-done.15.peer = bf16[128,1536]{1,0:T(8,128)(2,1)S(1)} collective-permute-done((bf16[128,1536]{1,0:T(8,128)(2,1)S(1)}, bf16[128,1536]{1,0:T(8,128)(2,1)S(1)}, u32[]{:S(2)}, u32[]{:S(2)}) %collective-permute-start.15) | collective-permute-done | bytes 393248 | tf_op jit(solution)/shard_map/ppermute | solution.py:62
  185.2 6.8 %attention_forward.3 = (bf16[256,768]{1,0:T(8,128)(2,1)S(1)}, f32[256,128]{1,0:T(8,128)S(1)}, f32[128,1536]{1,0:T(8,128)S(1)}, bf16[128,1536]{1,0:T(8,128)(2,1)S(1)}) custom-call(bf16[256,768]{1,0:T(8,128)(2,1)S(1)} %get-tuple-element.142.query.rest_0_, bf16[256,256]{1,0:T(8,128)(2,1)S(1)} %get-tuple-element.143.own.rest_1_, ...), custom_call_target="tpu_custom_call" | custom-call | flops 4294967296 | bytes 8388608 | tf_op jit(solution)/shard_map/attention_forward/pallas_call | solution.py:322
  205.6 5.7 collective-permute-start.19
  218.4 11.4 %collective-permute-done.19.x2 = bf16[128,1536]{1,0:T(8,128)(2,1)S(1)} collective-permute-done((bf16[128,1536]{1,0:T(8,128)(2,1)S(1)}, bf16[128,1536]{1,0:T(8,128)(2,1)S(1)}, u32[]{:S(2)}, u32[]{:S(2)}) %collective-permute-start.19) | collective-permute-done | bytes 393248 | tf_op jit(solution)/shard_map/ppermute | solution.py:66
  230.5 8.0 %collective-permute-done.20.x3 = bf16[128,1536]{1,0:T(8,128)(2,1)S(1)} collective-permute-done((bf16[128,1536]{1,0:T(8,128)(2,1)S(1)}, bf16[128,1536]{1,0:T(8,128)(2,1)S(1)}, u32[]{:S(2)}, u32[]{:S(2)}) %collective-permute-start.20) | collective-permute-done | bytes 393248 | tf_op jit(solution)/shard_map/ppermute | solution.py:70
  245.2 11.3 %experts_forward.3 = (bf16[512,1536]{1,0:T(8,128)(2,1)S(1)}, f32[512,1536]{1,0:T(8,128)}, f32[512,1536]{1,0:T(8,128)}, bf16[512,1536]{1,0:T(8,128)(2,1)S(1)}, f32[512,128]{1,0:T(8,128)S(1)}) custom-call(bf16[128,1536]{1,0:T(8,128)(2,1)S(1)} %copy-done.12, bf16[128,1536]{1,0:T(8,128)(2,1)S(1)} %copy-done.38, bf16[128,1536]{1,0:T(8,128)(2,1)S(1)} %copy-done.40, ...), custom_call_target="tpu_custom_call" | custom-call | flops 7247757312 | bytes 25165824 | tf_op jit(solution)/shard_map/experts_forward/pallas_call | solution.py:612
  256.6 18.9 %experts_backward.2 = (bf16[512,1536]{1,0:T(8,128)(2,1)S(1)}, bf16[512,1536]{1,0:T(8,128)(2,1)}, bf16[512,1536]{1,0:T(8,128)(2,1)}, bf16[512,256]{1,0:T(8,128)(2...) custom-call(bf16[128,1536]{1,0:T(8,128)(2,1)} %get-tuple-element.370, ...), custom_call_target="tpu_custom_call" | custom-call | flops 7247757312 | bytes 25165824 | tf_op jit(solution)/shard_map/experts_backward/pallas_call | solution.py:745
  281.4 10.5 %expert_weight_grads.4 = bf16[384,9216]{1,0:T(8,128)(2,1)} custom-call(bf16[512,1536]{1,0:T(8,128)(2,1)S(1)} %get-tuple-element.159.inputs, bf16[512,1536]{1,0:T(8,128)(2,1)S(1)} %get-tuple-element.151.hidden, bf16[512,1536]{1,0:T(8,128)(2,1)} %get-tuple-element.160.gate_grad, bf16[512,1536]{1,0:T(8,128)(2,1)} %get-tuple-element.161.up_grad, ...), custom_call_target="tpu_custom_call" | custom-call | flops 4831838208 | bytes 25165824 | tf_op jit(solution)/shard_map/expert_weight_grads/pallas_call | solution.py:722
  294.6 11.5 %collective-permute-done.29.peer = bf16[128,1536]{1,0:T(8,128)(2,1)S(1)} collective-permute-done((bf16[128,1536]{1,0:T(8,128)(2,1)S(1)}, bf16[128,1536]{1,0:T(8,128)(2,1)S(1)}, u32[]{:S(2)}, u32[]{:S(2)}) %collective-permute-start.29) | collective-permute-done | bytes 393248 | tf_op jit(solution)/shard_map/ppermute | solution.py:62
  306.1 6.2 %attention_backward.2 = (bf16[256,1536]{1,0:T(8,128)(2,1)S(1)}, bf16[256,768]{1,0:T(8,128)(2,1)S(1)}, f32[256,256]{1,0:T(8,128)S(1)}, bf16[256,256]{1,0:T(8,128)(2,1)S(1)}) custom-call(f32[256,128]{1,0:T(8,128)S(1)} %pad_maximum_fusion.12.cosine, f32[256,128]{1,0:T(8,128)S(1)} %pad_maximum_fusion.13.sine, f32[256,512]{1,0:T(8,128)S(1)} %and_convert_fusion.seen, ...), custom_call_target="tpu_custom_call" | custom-call | flops 4294967296 | bytes 8388608 | tf_op jit(solution)/shard_map/attention_backward/pallas_call | solution.py:322
  324.8 13.6 %expert_weight_grads.5 = f32[384,9216]{1,0:T(8,128)} custom-call(bf16[512,1536]{1,0:T(8,128)(2,1)S(1)} %get-tuple-element.159.inputs, bf16[512,1536]{1,0:T(8,128)(2,1)S(1)} %get-tuple-element.151.hidden, bf16[512,1536]{1,0:T(8,128)(2,1)} %get-tuple-element.160.gate_grad, bf16[512,1536]{1,0:T(8,128)(2,1)} %get-tuple-element.161.up_grad, ...), custom_call_target="tpu_custom_call" | custom-call | flops 4831838208 | bytes 25165824 | tf_op jit(solution)/shard_map/expert_weight_grads/pallas_call | solution.py:722
  349.0 7.0 %collective-permute-done.34.y1 = bf16[128,1536]{1,0:T(8,128)(2,1)S(1)} collective-permute-done((bf16[128,1536]{1,0:T(8,128)(2,1)S(1)}, bf16[128,1536]{1,0:T(8,128)(2,1)S(1)}, u32[]{:S(2)}, u32[]{:S(2)}) %collective-permute-start.34) | collective-permute-done | bytes 393248 | tf_op jit(solution)/shard_map/ppermute | solution.py:62
  356.0 8.2 %collective-permute-done.35.y2 = bf16[128,1536]{1,0:T(8,128)(2,1)S(1)} collective-permute-done((bf16[128,1536]{1,0:T(8,128)(2,1)S(1)}, bf16[128,1536]{1,0:T(8,128)(2,1)S(1)}, u32[]{:S(2)}, u32[]{:S(2)}) %collective-permute-start.35) | collective-permute-done | bytes 393248 | tf_op jit(solution)/shard_map/ppermute | solution.py:66
  367.2 16.5 %experts_backward.3 = (bf16[512,1536]{1,0:T(8,128)(2,1)S(1)}, bf16[512,1536]{1,0:T(8,128)(2,1)}, bf16[512,1536]{1,0:T(8,128)(2,1)}, bf16[512,256]{1,0:T(8,128)(2...) custom-call(bf16[128,1536]{1,0:T(8,128)(2,1)S(1)} %get-tuple-element, ...), custom_call_target="tpu_custom_call" | custom-call | flops 7247757312 | bytes 25165824 | tf_op jit(solution)/shard_map/experts_backward/pallas_call | solution.py:745
  389.5 10.6 %expert_weight_grads.6 = bf16[384,9216]{1,0:T(8,128)(2,1)} custom-call(bf16[512,1536]{1,0:T(8,128)(2,1)S(1)} %copy-done.2, bf16[512,1536]{1,0:T(8,128)(2,1)S(1)} %copy-done.20, bf16[512,1536]{1,0:T(8,128)(2,1)} %get-tuple-element.187.gate_grad, bf16[512,1536]{1,0:T(8,128)(2,1)} %get-tuple-element.188.up_grad, bf16[512,1536]{1,0:T(8,128)(2,1)} %copy-done.22, ...), custom_call_target="tpu_custom_call" | custom-call | flops 4831838208 | bytes 25165824 | tf_op jit(solution)/shard_map/expert_weight_grads/pallas_call | solution.py:722
  407.0 6.2 %collective-permute-done.31 = bf16[128,768]{1,0:T(8,128)(2,1)S(1)} collective-permute-done((bf16[128,768]{1,0:T(8,128)(2,1)}, bf16[128,768]{1,0:T(8,128)(2,1)S(1)}, u32[]{:S(2)}, u32[]{:S(2)}) %collective-permute-start.31) | collective-permute-done | bytes 196640 | tf_op jit(solution)/shard_map/ppermute | solution.py:62
  420.6 13.6 %expert_weight_grads.7 = f32[384,9216]{1,0:T(8,128)} custom-call(bf16[512,1536]{1,0:T(8,128)(2,1)S(1)} %copy-done.3, bf16[512,1536]{1,0:T(8,128)(2,1)S(1)} %copy-done.21, bf16[512,1536]{1,0:T(8,128)(2,1)} %get-tuple-element.187.gate_grad, bf16[512,1536]{1,0:T(8,128)(2,1)} %get-tuple-element.188.up_grad, bf16[512,1536]{1,0:T(8,128)(2,1)} %copy-done.22, ...), custom_call_target="tpu_custom_call" | custom-call | flops 4831838208 | bytes 25165824 | tf_op jit(solution)/shard_map/expert_weight_grads/pallas_call | solution.py:722
  437.9 6.3 %attention_backward.3 = (bf16[256,1536]{1,0:T(8,128)(2,1)S(1)}, bf16[256,768]{1,0:T(8,128)(2,1)S(1)}, f32[256,256]{1,0:T(8,128)S(1)}, bf16[256,256]{1,0:T(8,128)(2,1)S(1)}) custom-call(f32[256,128]{1,0:T(8,128)S(1)} %pad_maximum_fusion.12.cosine, f32[256,128]{1,0:T(8,128)S(1)} %pad_maximum_fusion.13.sine, f32[256,512]{1,0:T(8,128)S(1)} %and_convert_fusion.seen, ...), custom_call_target="tpu_custom_call" | custom-call | flops 4294967296 | bytes 8388608 | tf_op jit(solution)/shard_map/attention_backward/pallas_call | solution.py:322
  458.1 6.2 %attention_weight_grads.2 = (bf16[384,3584]{1,0:T(8,128)(2,1)}, bf16[384,3584]{1,0:T(8,128)(2,1)}) custom-call(bf16[256,1536]{1,0:T(8,128)(2,1)S(1)} %copy-done.13, bf16[256,768]{1,0:T(8,128)(2,1)S(1)} %copy-done.78, bf16[256,1024]{1,0:T(8,128)(2,1)S(1)} %get-tuple-element.207.qkv_grad, bf16[256,1536]{1,0:T(8,128)(2,1)S(1)} %get-tuple-element.208.out_grad, ...), custom_call_target="tpu_custom_call" | custom-call | flops 1811939328 | bytes 10485760 | tf_op jit(solution)/shard_map/attention_weight_grads/pallas_call | solution.py:472
  472.2 6.2 %attention_weight_grads.3 = (bf16[384,3584]{1,0:T(8,128)(2,1)}, bf16[384,3584]{1,0:T(8,128)(2,1)}) custom-call(bf16[256,1536]{1,0:T(8,128)(2,1)S(1)} %copy-done.30, bf16[256,768]{1,0:T(8,128)(2,1)S(1)} %copy-done.71, bf16[256,1024]{1,0:T(8,128)(2,1)S(1)} %copy-done.68, bf16[256,1536]{1,0:T(8,128)(2,1)S(1)} %copy-done.66, bf16[768,768]{1,0:T(8,128)(2,1)S(1)} %fusion.5.order), custom_call_target="tpu_custom_call" | custom-call | flops 1811939328 | bytes 10485760 | tf_op jit(solution)/shard_map/attention_weight_grads/pallas_call | solution.py:472
  486.8 5.7 collective-permute-done.57
  515.9 10.4 %collective-permute-done.49 = bf16[96,3584]{1,0:T(8,128)(2,1)S(1)} collective-permute-done((bf16[96,3584]{1,0:T(8,128)(2,1)}, bf16[96,3584]{1,0:T(8,128)(2,1)S(1)}, u32[]{:S(2)}, u32[]{:S(2)}) %collective-permute-start.49) | collective-permute-done | bytes 688160 | tf_op jit(solution)/shard_map/ppermute | solution.py:74
  527.4 15.6 %collective-permute-done.48 = bf16[96,3584]{1,0:T(8,128)(2,1)} collective-permute-done((bf16[96,3584]{1,0:T(8,128)(2,1)}, bf16[96,3584]{1,0:T(8,128)(2,1)}, u32[]{:S(2)}, u32[]{:S(2)}) %collective-permute-start.48) | collective-permute-done | bytes 688160 | tf_op jit(solution)/shard_map/ppermute | solution.py:74
  549.5 11.3 %collective-permute-done.50 = bf16[96,3584]{1,0:T(8,128)(2,1)S(1)} collective-permute-done((bf16[96,3584]{1,0:T(8,128)(2,1)S(1)}, bf16[96,3584]{1,0:T(8,128)(2,1)S(1)}, u32[]{:S(2)}, u32[]{:S(2)}) %collective-permute-start.50) | collective-permute-done | bytes 688160 | tf_op jit(solution)/shard_map/ppermute | solution.py:74
  600.6 6.3 %collective-permute-done.73 = bf16[24,8192]{1,0:T(8,128)(2,1)S(1)} collective-permute-done((bf16[24,8192]{1,0:T(8,128)(2,1)S(1)}, bf16[24,8192]{1,0:T(8,128)(2,1)S(1)}, u32[]{:S(2)}, u32[]{:S(2)}) %collective-permute-start.73) | collective-permute-done | bytes 393248 | tf_op jit(solution)/shard_map/ppermute | solution.py:66
  (677 shorter events, 288.7 us)
Async XLA Ops:
  7.2 118.4 %all-gather.3.cloned.1.call-start = ((), (), s32[]{:S(2)}) async-start(), calls=%async_computation.2 | async-start | bytes 20275200 | tf_op jit(solution)/shard_map/all_gather | solution.py:231
  19.3 20.8 %collective-permute-start.2 = (bf16[256,768]{1,0:T(8,128)(2,1)S(1)}, bf16[256,768]{1,0:T(8,128)(2,1)}, u32[]{:S(2)}, u32[]{:S(2)}) collective-permute-start(bf16[256,768]{1,0:T(8,128)(2,1)S(1)} %fusion.8.own), channel_id=1, source_target_pairs={{0,2},{2,0},{1,3},{3,1},{4,6},{6,4},{5,7},{7,5},{8,10},{10,8},{9,1... | collective-permute-start | bytes 1179656 | tf_op jit(solution)/shard_map/ppermute | solution.py:62
  40.1 199.2 %all-gather.5.cloned.1.call-start = ((), (), s32[]{:S(2)}) async-start(), calls=%async_computation.3 | async-start | bytes 20275200 | tf_op jit(solution)/shard_map/all_gather | solution.py:231
  41.9 34.5 %collective-permute-start.5 = (bf16[128,768]{1,0:T(8,128)(2,1)}, bf16[128,768]{1,0:T(8,128)(2,1)S(1)}, u32[]{:S(2)}, u32[]{:S(2)}) collective-permute-start(bf16[128,768]{1,0:T(8,128)(2,1)} %get-tuple-element.378), channel_id=1, source_target_pairs={{0,1},{1,0},{2,3},{3,2},{4,5},{5,4},{6,7},{7,6},{8,9},{9,8},{10,11... | collective-permute-start | bytes 589832 | tf_op jit(solution)/shard_map/ppermute | solution.py:66
  44.8 19.2 %collective-permute-start.6 = (bf16[384,768]{1,0:T(8,128)(2,1)S(1)}, bf16[384,768]{1,0:T(8,128)(2,1)}, u32[]{:S(2)}, u32[]{:S(2)}) collective-permute-start(bf16[384,768]{1,0:T(8,128)(2,1)S(1)} %get-tuple-element.134), channel_id=1, source_target_pairs={{0,1},{1,0},{2,3},{3,2},{4,5},{5,4},{6,7},{7,6},{8,9},{9,8},{10,11... | collective-permute-start | bytes 1769480 | tf_op jit(solution)/shard_map/ppermute | solution.py:66
  54.1 19.1 %collective-permute-start.3 = (bf16[256,1024]{1,0:T(8,128)(2,1)}, bf16[256,1024]{1,0:T(8,128)(2,1)S(1)}, u32[]{:S(2)}, u32[]{:S(2)}) collective-permute-start(bf16[256,1024]{1,0:T(8,128)(2,1)} %copy-done.69), channel_id=1, source_target_pairs={{0,1},{1,0},{2,3},{3,2},{4,5},{5,4},{6,7},{7,6},{8,9},{9,8},{10,11... | collective-permute-start | bytes 1572872 | tf_op jit(solution)/shard_map/ppermute | solution.py:66
  90.6 21.6 %collective-permute-start.21 = (bf16[48,5248]{1,0:T(8,128)(2,1)S(1)}, bf16[48,5248]{1,0:T(8,128)(2,1)S(1)}, u32[]{:S(2)}, u32[]{:S(2)}) collective-permute-start(bf16[48,5248]{1,0:T(8,128)(2,1)S(1)} %get-tuple-element.148), channel_id=1, source_target_pairs={{0,1},{1,0},{2,3},{3,2},{4,5},{5,4},{6,7},{7,6},{8,9},{9,8},{10,11... | collective-permute-start | bytes 1511432 | tf_op jit(solution)/shard_map/ppermute | solution.py:66
  101.0 18.2 %collective-permute-start.9 = (bf16[128,1536]{1,0:T(8,128)(2,1)S(1)}, bf16[128,1536]{1,0:T(8,128)(2,1)S(1)}, u32[]{:S(2)}, u32[]{:S(2)}) collective-permute-start(bf16[128,1536]{1,0:T(8,128)(2,1)S(1)} %multiply_convert_fusion.2.x0), channel_id=1, source_target_pairs={{0,2},{2,0},{1,3},{3,1},{4,6},{6,4},{5,7},{7,5},{8,10},{10,8},{9,1... | collective-permute-start | bytes 1179656 | tf_op jit(solution)/shard_map/ppermute | solution.py:62
  101.9 23.0 %collective-permute-start.10 = (bf16[128,1536]{1,0:T(8,128)(2,1)}, bf16[128,1536]{1,0:T(8,128)(2,1)S(1)}, u32[]{:S(2)}, u32[]{:S(2)}) collective-permute-start(bf16[128,1536]{1,0:T(8,128)(2,1)} %pad_maximum_fusion.2), channel_id=1, source_target_pairs={{0,1},{1,0},{2,3},{3,2},{4,5},{5,4},{6,7},{7,6},{8,9},{9,8},{10,11... | collective-permute-start | bytes 1179656 | tf_op jit(solution)/shard_map/ppermute | solution.py:66
  105.3 19.6 %collective-permute-start.11 = (bf16[128,1536]{1,0:T(8,128)(2,1)}, bf16[128,1536]{1,0:T(8,128)(2,1)S(1)}, u32[]{:S(2)}, u32[]{:S(2)}) collective-permute-start(bf16[128,1536]{1,0:T(8,128)(2,1)} %pad_maximum_fusion.2), channel_id=1, source_target_pairs={{0,3},{1,2},{2,1},{3,0},{4,7},{5,6},{6,5},{7,4},{8,11},{9,10},{10,... | collective-permute-start | bytes 1179656 | tf_op jit(solution)/shard_map/ppermute | solution.py:70
  145.9 298.3 %reduce-scatter.7.cloned.1.call-start = ((), (), s32[]{:S(2)}) async-start(), calls=%async_computation.4 | async-start | bytes 15040512
  205.6 24.2 %collective-permute-start.19 = (bf16[128,1536]{1,0:T(8,128)(2,1)S(1)}, bf16[128,1536]{1,0:T(8,128)(2,1)S(1)}, u32[]{:S(2)}, u32[]{:S(2)}) collective-permute-start(bf16[128,1536]{1,0:T(8,128)(2,1)S(1)} %pad_maximum_fusion.3), channel_id=1, source_target_pairs={{0,1},{1,0},{2,3},{3,2},{4,5},{5,4},{6,7},{7,6},{8,9},{9,8},{10,11... | collective-permute-start | bytes 1179656 | tf_op jit(solution)/shard_map/ppermute | solution.py:66
  211.3 27.2 %collective-permute-start.20 = (bf16[128,1536]{1,0:T(8,128)(2,1)S(1)}, bf16[128,1536]{1,0:T(8,128)(2,1)S(1)}, u32[]{:S(2)}, u32[]{:S(2)}) collective-permute-start(bf16[128,1536]{1,0:T(8,128)(2,1)S(1)} %pad_maximum_fusion.3), channel_id=1, source_target_pairs={{0,3},{1,2},{2,1},{3,0},{4,7},{5,6},{6,5},{7,4},{8,11},{9,10},{10,... | collective-permute-start | bytes 1179656 | tf_op jit(solution)/shard_map/ppermute | solution.py:70
  213.8 42.8 %collective-permute-start.24 = (bf16[128,1536]{1,0:T(8,128)(2,1)}, bf16[128,1536]{1,0:T(8,128)(2,1)}, u32[]{:S(2)}, u32[]{:S(2)}) collective-permute-start(bf16[128,1536]{1,0:T(8,128)(2,1)} %get-tuple-element.369), channel_id=1, source_target_pairs={{0,1},{1,0},{2,3},{3,2},{4,5},{5,4},{6,7},{7,6},{8,9},{9,8},{10,11... | collective-permute-start | bytes 1179656 | tf_op jit(solution)/shard_map/ppermute | solution.py:66
  214.9 41.7 %collective-permute-start.25 = (bf16[128,1536]{1,0:T(8,128)(2,1)}, bf16[128,1536]{1,0:T(8,128)(2,1)}, u32[]{:S(2)}, u32[]{:S(2)}) collective-permute-start(bf16[128,1536]{1,0:T(8,128)(2,1)} %get-tuple-element.369), channel_id=1, source_target_pairs={{0,3},{1,2},{2,1},{3,0},{4,7},{5,6},{6,5},{7,4},{8,11},{9,10},{10,... | collective-permute-start | bytes 1179656 | tf_op jit(solution)/shard_map/ppermute | solution.py:70
  217.8 38.8 %collective-permute-start.23 = (bf16[128,1536]{1,0:T(8,128)(2,1)}, bf16[128,1536]{1,0:T(8,128)(2,1)}, u32[]{:S(2)}, u32[]{:S(2)}) collective-permute-start(bf16[128,1536]{1,0:T(8,128)(2,1)} %get-tuple-element.370.y0), channel_id=1, source_target_pairs={{0,2},{2,0},{1,3},{3,1},{4,6},{6,4},{5,7},{7,5},{8,10},{10,8},{9,1... | collective-permute-start | bytes 1179656 | tf_op jit(solution)/shard_map/ppermute | solution.py:62
  292.0 32.8 %collective-permute-start.32 = (bf16[384,9216]{1,0:T(8,128)(2,1)}, bf16[384,9216]{1,0:T(8,128)(2,1)}, u32[]{:S(2)}, u32[]{:S(2)}) collective-permute-start(bf16[384,9216]{1,0:T(8,128)(2,1)} %expert_weight_grads.4), channel_id=1, source_target_pairs={{0,4},{4,0},{8,12},{12,8},{16,20},{20,16},{24,28},{28,24},{32,36},... | collective-permute-start | bytes 21233672 | tf_op jit(solution)/shard_map/ppermute | solution.py:74
  338.5 257.8 %reduce-scatter.9.cloned.1.call-start = ((), (), s32[]{:S(2)}) async-start(), calls=%async_computation.5 | async-start | bytes 15040512
  345.6 18.7 %collective-permute-start.35 = (bf16[128,1536]{1,0:T(8,128)(2,1)S(1)}, bf16[128,1536]{1,0:T(8,128)(2,1)S(1)}, u32[]{:S(2)}, u32[]{:S(2)}) collective-permute-start(bf16[128,1536]{1,0:T(8,128)(2,1)S(1)} %pad_maximum_fusion.6), channel_id=1, source_target_pairs={{0,1},{1,0},{2,3},{3,2},{4,5},{5,4},{6,7},{7,6},{8,9},{9,8},{10,11... | collective-permute-start | bytes 1179656 | tf_op jit(solution)/shard_map/ppermute | solution.py:66
  348.3 18.8 %collective-permute-start.36 = (bf16[128,1536]{1,0:T(8,128)(2,1)S(1)}, bf16[128,1536]{1,0:T(8,128)(2,1)S(1)}, u32[]{:S(2)}, u32[]{:S(2)}) collective-permute-start(bf16[128,1536]{1,0:T(8,128)(2,1)S(1)} %pad_maximum_fusion.6), channel_id=1, source_target_pairs={{0,3},{1,2},{2,1},{3,0},{4,7},{5,6},{6,5},{7,4},{8,11},{9,10},{10,... | collective-permute-start | bytes 1179656 | tf_op jit(solution)/shard_map/ppermute | solution.py:70
  464.3 29.0 %collective-permute-start.46 = (bf16[384,3584]{1,0:T(8,128)(2,1)}, bf16[384,3584]{1,0:T(8,128)(2,1)}, u32[]{:S(2)}, u32[]{:S(2)}) collective-permute-start(bf16[384,3584]{1,0:T(8,128)(2,1)} %get-tuple-element.209), channel_id=1, source_target_pairs={{0,4},{4,0},{8,12},{12,8},{16,20},{20,16},{24,28},{28,24},{32,36},... | collective-permute-start | bytes 8257544 | tf_op jit(solution)/shard_map/ppermute | solution.py:74
  478.4 24.0 %collective-permute-start.43 = (bf16[384,3584]{1,0:T(8,128)(2,1)}, bf16[384,3584]{1,0:T(8,128)(2,1)S(1)}, u32[]{:S(2)}, u32[]{:S(2)}) collective-permute-start(bf16[384,3584]{1,0:T(8,128)(2,1)} %get-tuple-element.211), channel_id=1, source_target_pairs={{0,4},{4,0},{8,12},{12,8},{16,20},{20,16},{24,28},{28,24},{32,36},... | collective-permute-start | bytes 8257544 | tf_op jit(solution)/shard_map/ppermute | solution.py:74
  486.7 76.9 %collective-permute-start.60 = (f32[20,768]{1,0:T(8,128)S(1)}, f32[20,768]{1,0:T(8,128)S(1)}, u32[]{:S(2)}, u32[]{:S(2)}) collective-permute-start(f32[20,768]{1,0:T(8,128)S(1)} %add_add_fusion.3), channel_id=1, source_target_pairs={{0,4},{4,0},{8,12},{12,8},{16,20},{20,16},{24,28},{28,24},{32,36},... | collective-permute-start | bytes 184328 | tf_op jit(solution)/shard_map/ppermute | solution.py:74
  498.2 28.1 %collective-permute-start.49 = (bf16[96,3584]{1,0:T(8,128)(2,1)}, bf16[96,3584]{1,0:T(8,128)(2,1)S(1)}, u32[]{:S(2)}, u32[]{:S(2)}) collective-permute-start(bf16[96,3584]{1,0:T(8,128)(2,1)} %get-tuple-element.301), channel_id=1, source_target_pairs={{0,96},{4,100},{8,104},{12,108},{16,112},{20,116},{24,120},{28,124... | collective-permute-start | bytes 2064392 | tf_op jit(solution)/shard_map/ppermute | solution.py:74
  499.1 43.9 %collective-permute-start.48 = (bf16[96,3584]{1,0:T(8,128)(2,1)}, bf16[96,3584]{1,0:T(8,128)(2,1)}, u32[]{:S(2)}, u32[]{:S(2)}) collective-permute-start(bf16[96,3584]{1,0:T(8,128)(2,1)} %get-tuple-element.302), channel_id=1, source_target_pairs={{0,64},{4,68},{8,72},{12,76},{16,80},{20,84},{24,88},{28,92},{32,9... | collective-permute-start | bytes 2064392 | tf_op jit(solution)/shard_map/ppermute | solution.py:74
  500.4 42.9 %collective-permute-start.47 = (bf16[96,3584]{1,0:T(8,128)(2,1)}, bf16[96,3584]{1,0:T(8,128)(2,1)}, u32[]{:S(2)}, u32[]{:S(2)}) collective-permute-start(bf16[96,3584]{1,0:T(8,128)(2,1)} %get-tuple-element.300), channel_id=1, source_target_pairs={{0,32},{4,36},{8,40},{12,44},{16,48},{20,52},{24,56},{28,60},{32,6... | collective-permute-start | bytes 2064392 | tf_op jit(solution)/shard_map/ppermute | solution.py:74
  513.4 34.6 %collective-permute-start.52 = (bf16[96,3584]{1,0:T(8,128)(2,1)S(1)}, bf16[96,3584]{1,0:T(8,128)(2,1)S(1)}, u32[]{:S(2)}, u32[]{:S(2)}) collective-permute-start(bf16[96,3584]{1,0:T(8,128)(2,1)S(1)} %get-tuple-element.298), channel_id=1, source_target_pairs={{0,24},{4,28},{8,0},{12,4},{16,8},{20,12},{24,16},{28,20},{32,56},... | collective-permute-start | bytes 2064392 | tf_op jit(solution)/shard_map/ppermute | solution.py:74
  526.3 22.8 %collective-permute-start.51 = (bf16[96,3584]{1,0:T(8,128)(2,1)S(1)}, bf16[96,3584]{1,0:T(8,128)(2,1)S(1)}, u32[]{:S(2)}, u32[]{:S(2)}) collective-permute-start(bf16[96,3584]{1,0:T(8,128)(2,1)S(1)} %get-tuple-element.299), channel_id=1, source_target_pairs={{0,16},{4,20},{8,24},{12,28},{16,0},{20,4},{24,8},{28,12},{32,48},... | collective-permute-start | bytes 2064392 | tf_op jit(solution)/shard_map/ppermute | solution.py:74
  543.4 22.8 %collective-permute-start.54 = (bf16[128,1536]{1,0:T(8,128)(2,1)S(1)}, bf16[128,1536]{1,0:T(8,128)(2,1)S(1)}, u32[]{:S(2)}, u32[]{:S(2)}) collective-permute-start(bf16[128,1536]{1,0:T(8,128)(2,1)S(1)} %get-tuple-element.217), channel_id=1, source_target_pairs={{0,3},{1,2},{2,1},{3,0},{4,7},{5,6},{6,5},{7,4},{8,11},{9,10},{10,... | collective-permute-start | bytes 1179656 | tf_op jit(solution)/shard_map/ppermute | solution.py:70
  548.0 20.3 %collective-permute-start.45 = (bf16[128,1536]{1,0:T(8,128)(2,1)S(1)}, bf16[128,1536]{1,0:T(8,128)(2,1)S(1)}, u32[]{:S(2)}, u32[]{:S(2)}) collective-permute-start(bf16[128,1536]{1,0:T(8,128)(2,1)S(1)} %get-tuple-element.214), channel_id=1, source_target_pairs={{0,1},{1,0},{2,3},{3,2},{4,5},{5,4},{6,7},{7,6},{8,9},{9,8},{10,11... | collective-permute-start | bytes 1179656 | tf_op jit(solution)/shard_map/ppermute | solution.py:66
  549.1 19.2 %collective-permute-start.44 = (bf16[128,1536]{1,0:T(8,128)(2,1)S(1)}, bf16[128,1536]{1,0:T(8,128)(2,1)S(1)}, u32[]{:S(2)}, u32[]{:S(2)}) collective-permute-start(bf16[128,1536]{1,0:T(8,128)(2,1)S(1)} %get-tuple-element.213), channel_id=1, source_target_pairs={{0,2},{2,0},{1,3},{3,1},{4,6},{6,4},{5,7},{7,5},{8,10},{10,8},{9,1... | collective-permute-start | bytes 1179656 | tf_op jit(solution)/shard_map/ppermute | solution.py:62
  568.6 26.8 %collective-permute-start.55 = (bf16[128,768]{1,0:T(8,128)(2,1)S(1)}, bf16[128,768]{1,0:T(8,128)(2,1)S(1)}, u32[]{:S(2)}, u32[]{:S(2)}) collective-permute-start(bf16[128,768]{1,0:T(8,128)(2,1)S(1)} %get-tuple-element.366), channel_id=1, source_target_pairs={{0,1},{1,0},{2,3},{3,2},{4,5},{5,4},{6,7},{7,6},{8,9},{9,8},{10,11... | collective-permute-start | bytes 589832 | tf_op jit(solution)/shard_map/ppermute | solution.py:66
  (196 other events, 1609.3 us)
Sparse Core Ops, SparseCore 0:
  40.2 81.5 all-gather.2
  146.0 79.9 all-gather.4
  338.6 98.5 reduce-scatter.6
  445.0 136.9 reduce-scatter.8
